TPU v7x, 128 devices: a whole 4x4x4 slice. The times are simulated.
128 devices in a mesh: shot: 8 (over y_lo, x), space: 16 (over y_hi, z, core).
Axes of the slice: x: 4, y: 4 (y_hi: 2, y_lo: 2; y = y_hi * 2 + y_lo), z: 4, core: 2. Of those that a mesh axis runs over, the one named last changes fastest.
Arguments:
- prior_field: bfloat16 [8, 128, 128, 256], P('shot', 'space'), may hold values from -3 to 3
- current_field: bfloat16 [8, 128, 128, 256], P('shot', 'space'), may hold values from -3 to 3
- model_store: bfloat16 [64, 128, 64, 64], P('shot', 'space'), may hold values from 1.5 to 4.5
- tile_home: int32 [64], replicated, may hold values from 0 to 63, as said below
- aperture: int32 [8, 8], replicated, may hold values from 0 to 63, as said below
- source_cell: int32 [8, 3], P('shot'), may hold values from 0 to 254, as said below
- source_frac: int32 [8, 3], P('shot'), may hold values from 0 to 7
- wavelet: float32 [8, 8], P('shot'), may hold values from -8 to 8
- receiver_cell: int32 [8, 16, 64, 3], P('shot', 'space'), may hold values from 0 to 254, as said below
- receiver_frac: int32 [8, 16, 64, 3], P('shot', 'space'), may hold values from 0 to 7
- receiver_count: int32 [8, 16], P('shot', 'space'), may hold values from 1 to 64, 512 in all within a row
- trace_owner: int32 [8, 16, 64, 1], P('shot', 'space'), may hold values from 0 to 7; in each aligned block of 64 rows (0 to 63, 64 to 127, ..., all dimensions but the last counted through in order) at most 16 rows name the same one
Outputs:
- final_field: float32 [8, 128, 128, 256], P('shot', 'space')
- gathers: float32 [8, 16, 8, 128], P('shot', 'space')
Inputs may be any that keep to these rules, and one draw needn't show every extreme that they name: `tile_home`: a permutation; lateral tile g = y * 8 + z sits at row y and column z of the survey grid. The tiles of one aperture are distinct; at most 2 of them have the same tile_home // 8, and some aperture has 2 such tiles. `source_cell`: plane below 127, row below 127, column below 255. `receiver_cell`: plane below 7, row below 127, column below 255. `trace_owner`: among the receivers of one device at most 16 name one shot index.
All inputs are finite; a program needn't handle non-finite values. No bound on the sum of `receiver_count` on one device may be relied on, other than what follows from the above.
Results may differ from a plain program's by a relative error of at most 0.0008.
Values may be sent and summed in bfloat16 or wider, within the bound.
No kernel may reach another device: no remote copies, remote signals or barrier semaphores. Data moves between devices by JAX's collectives and lax.ppermute only.
A program may use at most 64 MiB of HBM per device.

v0:
```python
import jax
import jax.numpy as jnp
import numpy as np
from jax import lax
from jax.experimental import pallas as pl
from jax.experimental.pallas import tpu as pltpu
from jax.sharding import PartitionSpec as P

STEPS = 8
CAPR = 16
PL = 8
ROWS = 128
COLS = 256
EDGE = 64
SLOTS = 64
SCALE = 5040.0
TAPS = (8064.0, -1008.0, 128.0, -9.0)
CENTRE_COLS = -43008.0
CENTRE_ROWS = -42.0
COURANT = 0.09

VMEM = pl.BlockSpec(memory_space=pltpu.VMEM)
SMEM = pl.BlockSpec(memory_space=pltpu.SMEM)
f32 = jnp.float32
bf16 = jnp.bfloat16


def band_matrix(size, centre):
    gap = np.abs(np.arange(size)[:, None] - np.arange(size)[None, :])
    out = np.where(gap == 0, centre, 0.0)
    for k in range(1, 5):
        out = np.where(gap == k, TAPS[k - 1], out)
    return out


def constants():
    cols = band_matrix(COLS, CENTRE_COLS)
    rows = band_matrix(ROWS, CENTRE_ROWS)
    return (
        jnp.asarray(np.concatenate([cols, cols], 0), bf16),
        jnp.asarray(np.concatenate([rows, rows], 1), bf16),
    )


def call(body, outs, ins, scratch=(), limit=None, cost=None):
    return pl.pallas_call(
        body,
        out_shape=[jax.ShapeDtypeStruct(s, d) for s, d in outs],
        in_specs=ins,
        out_specs=[VMEM] * len(outs),
        scratch_shapes=list(scratch),
        compiler_params=pltpu.CompilerParams(vmem_limit_bytes=limit),
        cost_estimate=pl.CostEstimate(flops=cost[0], bytes_accessed=cost[1], transcendentals=0) if cost else None,
    )


def pack_kernel(home, wanted, store, out):
    me = lax.axis_index("shot")

    def group(s, _):
        def slot(j, count):
            row = home[wanted[s, j]]
            mine = row // 8 == me
            for rank in range(2):

                @pl.when(mine & (count == rank))
                def _():
                    out[s, :, :, rank * EDGE : (rank + 1) * EDGE] = store[row % 8]

            return count + mine.astype(jnp.int32)

        lax.fori_loop(0, 8, slot, jnp.int32(0))
        return 0

    lax.fori_loop(0, 8, group, 0)


def assemble_kernel(home, wanted, arrived, own, send_in, send_x):
    me = lax.axis_index("shot")
    even = lax.rem(lax.axis_index("space"), 2) == 0
    owners = []
    ranks = []
    for j in range(8):
        owners.append(home[wanted[me, j]] // 8)
        rank = jnp.int32(0)
        for i in range(j):
            rank = rank + (owners[i] == owners[j]).astype(jnp.int32)
        ranks.append(rank)
    lane = lax.broadcasted_iota(jnp.int32, (EDGE, 2 * EDGE), 1)
    for a in range(2):
        for half in range(2):
            left, right = a * 4 + half * 2, a * 4 + half * 2 + 1
            swap_left = (ranks[left] == 1).astype(jnp.int32)
            swap_right = (ranks[right] == 0).astype(jnp.int32)

            def plane(p, _, left=left, right=right, a=a, half=half, swap_left=swap_left, swap_right=swap_right):
                x = arrived[owners[left], p].astype(f32)
                y = arrived[owners[right], p].astype(f32)
                x = jnp.where(swap_left == 1, pltpu.roll(x, EDGE, 1), x)
                y = jnp.where(swap_right == 1, pltpu.roll(y, EDGE, 1), y)
                both = jnp.where(lane < EDGE, x, y).astype(bf16)
                own[p, a * EDGE : (a + 1) * EDGE, half * 2 * EDGE : (half + 1) * 2 * EDGE] = both
                return 0

            lax.fori_loop(0, PL, plane, 0)
    first_in = jnp.where(even, 4, 0)
    first_x = jnp.where(even, 0, 4)
    send_in[...] = own[pl.ds(first_in, 4)]
    send_x[...] = own[pl.ds(first_x, 4)]


def lateral(weights, across, src, first, count, dst, dst_first=0):
    def body(i, _):
        u = src[first + i]
        hi = u.astype(bf16)
        lo = (u - hi.astype(f32)).astype(bf16)
        lhs = jnp.concatenate([hi, lo, across[...]], 1)
        rhs = jnp.concatenate([weights[...], hi, lo], 0)
        dst[dst_first + i] = jnp.dot(lhs, rhs, preferred_element_type=f32)
        return 0

    lax.fori_loop(0, count, body, 0)


CH_R = 16
CH_C = 128


def tiles(body):
    def step(t, _):
        r = pl.multiple_of(lax.div(t, COLS // CH_C) * CH_R, CH_R)
        c = pl.multiple_of(lax.rem(t, COLS // CH_C) * CH_C, CH_C)
        body(pl.ds(r, CH_R), pl.ds(c, CH_C))
        return 0

    lax.fori_loop(0, (ROWS // CH_R) * (COLS // CH_C), step, 0)


def depth(us, e):
    acc = None
    for k in range(1, 5):
        term = TAPS[k - 1] * (us[e + k] + us[e - k])
        acc = term if acc is None else acc + term
    return acc


def hat(frac):
    share = frac.astype(f32) * 0.125
    return 1.0 - share, share


def add_source(dst, first_plane, count, cell, frac, pulse):
    lane = lax.broadcasted_iota(jnp.int32, (1, COLS), 1)
    wd, wr, wc = hat(frac[0, 0]), hat(frac[0, 1]), hat(frac[0, 2])
    column = jnp.where(lane == cell[0, 2], wc[0], 0.0) + jnp.where(lane == cell[0, 2] + 1, wc[1], 0.0)
    for dp in range(2):
        at = cell[0, 0] + dp - first_plane

        @pl.when((at >= 0) & (at < count))
        def _():
            for dr in range(2):
                row = pl.ds(cell[0, 1] + dr, 1)
                dst[at, row, :] = dst[at, row, :] + pulse * (wd[dp] * wr[dr] * column)


def sample(src, plane_off, n, cells, fracs, count, spread, place, owner, rows, out):
    def one(r, _):
        wd, wr = hat(fracs[0, 0, r, 0]), hat(fracs[0, 0, r, 1])
        p, y = cells[0, 0, r, 0] + plane_off, cells[0, 0, r, 1]
        acc = None
        for dp in range(2):
            for dr in range(2):
                term = (wd[dp] * wr[dr]) * src[p + dp, pl.ds(y + dr, 1), :]
                acc = term if acc is None else acc + term
        rows[pl.ds(r, 1), :] = acc
        return 0

    lax.fori_loop(0, count[0, 0], one, 0)
    slot = lax.broadcasted_iota(jnp.int32, (SLOTS, 1), 0)
    values = jnp.where(slot < count[0, 0], jnp.sum(rows[...] * spread[...], axis=1, keepdims=True), 0.0)
    placed = values * place[...]
    for q in range(8):
        out[q, n : n + 1, :] = jnp.sum(jnp.where(owner[0, 0] == q, placed, 0.0), axis=0, keepdims=True)


def receiver_kernel(cells, fracs, count, owner, spread, place):
    lane = lax.broadcasted_iota(jnp.int32, (SLOTS, COLS), 1)
    share = fracs[0, 0, :, 2:3].astype(f32) * 0.125
    at = cells[0, 0, :, 2:3]
    spread[...] = jnp.where(lane == at, 1.0 - share, 0.0) + jnp.where(lane == at + 1, share, 0.0)
    me = lax.axis_index("shot")
    slot = lax.broadcasted_iota(jnp.int32, (SLOTS, 1), 0)
    live = slot < count[0, 0]
    group = lax.broadcasted_iota(jnp.int32, (SLOTS, 128), 1)
    chosen = jnp.where((owner[0, 0] == group) & live, 1.0, 0.0)
    earlier = jnp.where(
        lax.broadcasted_iota(jnp.int32, (SLOTS, SLOTS), 1) < lax.broadcasted_iota(jnp.int32, (SLOTS, SLOTS), 0), 1.0, 0.0
    )
    before = jnp.dot(earlier.astype(bf16), chosen.astype(bf16), preferred_element_type=f32)
    rank = jnp.sum(before * chosen, axis=1, keepdims=True).astype(jnp.int32)
    place[...] = jnp.where((group == rank + me * CAPR) & live, 1.0, 0.0)


def open_kernel(weights, across, own, got_in, got_x, total, ext):
    even = lax.rem(lax.axis_index("space"), 2) == 0
    at_in = jnp.where(even, 16, 0)
    at_x = jnp.where(even, 0, 16)
    for p in range(PL):
        ext[8 + p] = own[0, p].astype(f32)
        ext[at_in + p] = got_in[0, p].astype(f32)
        ext[at_x + p] = got_x[0, p].astype(f32)
    lateral(weights, across, ext, 4, 16, total)

    def tile(r, c):
        us = [ext[p, r, c] for p in range(24)]
        for i in range(16):
            total[i, r, c] = total[i, r, c] + depth(us, i + 4)

    tiles(tile)


def finish(weights, across, ext_own, previous, coef, u_in, lat, u_out):
    lateral(weights, across, u_in, 4, PL, lat)

    def tile(r, c):
        us = [u_in[p, r, c] for p in range(16)]
        for i in range(PL):
            u_out[i, r, c] = 2.0 * us[i + 4] - previous(i, r, c) + coef[i + 4, r, c] * (lat[i, r, c] + depth(us, i + 4))

    tiles(tile)


def pack_send(u, send_in, send_x):
    even = lax.rem(lax.axis_index("space"), 2) == 0
    for p in range(PL):
        hi = u[p].astype(bf16)
        send_in[p] = hi
        send_x[p] = hi
    near_in = jnp.where(even, PL - 1, 0)
    near_x = jnp.where(even, 0, PL - 1)
    for ref, near in ((send_in, near_in), (send_x, near_x)):
        edge = u[near]
        ref[PL] = (edge - edge.astype(bf16).astype(f32)).astype(bf16)


def first_kernel(
    weights, across, cell, frac, pulses, cells, fracs, count, owner, spread, place,
    total, cur, pri, pri_in, pri_x, v, v_in, v_x,
    next_ext, last, coef, send_in, send_x, gath, lat, rows,
):
    band = lax.axis_index("space")
    even = lax.rem(band, 2) == 0

    def factor(x):
        scaled = x.astype(f32) * COURANT
        return scaled * scaled * (1.0 / SCALE)

    c_in = jnp.where(even, 12, 0)
    c_x = jnp.where(even, 0, 12)
    half_in = jnp.where(even, 0, 4)
    half_x = jnp.where(even, 4, 0)
    for p in range(PL):
        coef[4 + p] = factor(v[p])
        next_ext[4 + p] = 2.0 * cur[0, p].astype(f32) - pri[0, p].astype(f32) + coef[4 + p] * total[4 + p]
    for p in range(4):
        coef[c_in + p] = factor(v_in[p])
        coef[c_x + p] = factor(v_x[p])
    return even, c_in, c_x, half_in, half_x


def round_kernel(
    first_step, weights, across, cell, frac, pulses, cells, fracs, count, owner, spread, place,
    u, got_in, got_x, prev, coef, gath_in,
    next_ext, last, send_in, send_x, gath, ext, lat, rows,
):
    band = lax.axis_index("space")
    even = lax.rem(band, 2) == 0
    at_in = jnp.where(even, 16, 0)
    at_x = jnp.where(even, 0, 16)
    near_in = jnp.where(even, 16, 7)
    near_x = jnp.where(even, 7, 16)
    gath[...] = gath_in[...]
    for p in range(PL):
        ext[8 + p] = u[p]
        ext[at_in + p] = got_in[p].astype(f32)
        ext[at_x + p] = got_x[p].astype(f32)
    ext[near_in] = ext[near_in] + got_in[PL].astype(f32)
    ext[near_x] = ext[near_x] + got_x[PL].astype(f32)
    lateral(weights, across, ext, 4, 16, lat)

    def tile(r, c):
        us = [ext[p, r, c] for p in range(24)]
        for i in range(16):
            next_ext[i, r, c] = 2.0 * us[i + 4] - prev[i, r, c] + coef[i, r, c] * (lat[i, r, c] + depth(us, i + 4))

    tiles(tile)
    add_source(next_ext, band * PL - 4, 16, cell, frac, pulses[0, first_step])
    second_half(first_step, band, weights, across, cell, frac, pulses, cells, fracs, count, owner, spread, place,
                next_ext, lambda i, r, c: u[i, r, c], coef, lat, last, send_in, send_x, gath, rows)


def second_half(first_step, band, weights, across, cell, frac, pulses, cells, fracs, count, owner, spread, place,
                next_ext, previous, coef, lat, last, send_in, send_x, gath, rows):
    finish(weights, across, None, previous, coef, next_ext, lat, last)
    add_source(last, band * PL, PL, cell, frac, pulses[0, first_step + 1])
    if send_in is not None:
        pack_send(last, send_in, send_x)
    sample(next_ext, 4, first_step, cells, fracs, count, spread, place, owner, rows, gath)
    sample(last, 0, first_step + 1, cells, fracs, count, spread, place, owner, rows, gath)


def first_round_kernel(
    weights, across, cell, frac, pulses, cells, fracs, count, owner, spread, place,
    total, cur, cur_in, cur_x, pri, pri_in, pri_x, v, v_in, v_x,
    next_ext, last, coef, send_in, send_x, gath, lat, rows,
):
    band = lax.axis_index("space")
    even = lax.rem(band, 2) == 0

    def factor(x):
        scaled = x.astype(f32) * COURANT
        return scaled * scaled * (1.0 / SCALE)

    def step(at, now, before, vel):
        c = factor(vel)
        coef[at] = c
        next_ext[at] = 2.0 * now.astype(f32) - before.astype(f32) + c * total[at]

    at_in = jnp.where(even, 12, 0)
    at_x = jnp.where(even, 0, 12)
    half_in = jnp.where(even, 0, 4)
    half_x = jnp.where(even, 4, 0)
    for p in range(PL):
        step(4 + p, cur[0, p], pri[0, p], v[p])
    for p in range(4):
        step(at_in + p, cur_in[0, half_in + p], pri_in[0, half_in + p], v_in[p])
        step(at_x + p, cur_x[0, half_x + p], pri_x[0, half_x + p], v_x[p])
    add_source(next_ext, band * PL - 4, 16, cell, frac, pulses[0, 0])
    second_half(0, band, weights, across, cell, frac, pulses, cells, fracs, count, owner, spread, place,
                next_ext, lambda i, r, c: cur[0, i, r, c].astype(f32), coef, lat, last, send_in, send_x, gath, rows)


def last_round_kernel(first_step, *refs):
    refs = list(refs)
    ins, (last, gath, next_ext, ext, lat, rows) = refs[:-6], refs[-6:]
    round_kernel(first_step, *ins, next_ext, last, None, None, gath, ext, lat, rows)


MIB = 1 << 20


def on_device(
    prior_field, current_field, model_store, tile_home, aperture, source_cell, source_frac,
    wavelet, receiver_cell, receiver_frac, receiver_count, trace_owner,
):
    size = lax.axis_size("space")
    pair_in = [(i, i ^ 1) for i in range(size)]
    pair_x = [(i, i + 1) for i in range(1, size - 1, 2)] + [(i + 1, i) for i in range(1, size - 1, 2)]

    def swap(x):
        return lax.ppermute(x, "space", pair_in), lax.ppermute(x, "space", pair_x)

    weights, across = constants()
    out = call(pack_kernel, [((8, PL, EDGE, 2 * EDGE), bf16)], [SMEM, SMEM, VMEM], limit=8 * MIB)(
        tile_home, aperture, model_store
    )[0]
    arrived = lax.all_to_all(out, "shot", split_axis=0, concat_axis=0, tiled=True)
    cur_in, cur_x = swap(current_field)
    pri_in, pri_x = swap(prior_field)
    spread, place = call(
        receiver_kernel, [((SLOTS, COLS), f32), ((SLOTS, 128), f32)], [VMEM, VMEM, SMEM, VMEM], limit=4 * MIB
    )(receiver_cell, receiver_frac, receiver_count, trace_owner)
    plane = (ROWS, COLS)
    total = call(
        open_kernel, [((16,) + plane, f32)], [VMEM] * 5, [pltpu.VMEM((24,) + plane, f32)], limit=16 * MIB
    )(weights, across, current_field, cur_in, cur_x)[0]
    v, v_send_in, v_send_x = call(
        assemble_kernel, [((PL,) + plane, bf16), ((4,) + plane, bf16), ((4,) + plane, bf16)], [SMEM, SMEM, VMEM], limit=8 * MIB
    )(tile_home, aperture, arrived)
    v_in = lax.ppermute(v_send_in, "space", pair_in)
    v_x = lax.ppermute(v_send_x, "space", pair_x)
    common = (
        weights, across, source_cell, source_frac, wavelet, receiver_cell, receiver_frac, receiver_count, trace_owner,
        spread, place,
    )
    specs = [VMEM, VMEM, SMEM, SMEM, SMEM, SMEM, SMEM, SMEM, VMEM, VMEM, VMEM]
    gath_shape = ((8, STEPS, 128), f32)
    send = ((PL + 1,) + plane, bf16)
    ext16 = ((16,) + plane, f32)
    own8 = ((PL,) + plane, f32)
    rows = pltpu.VMEM((SLOTS, COLS), f32)
    prev, u, coef, send_in, send_x, gath = call(
        first_round_kernel, [ext16, own8, ext16, send, send, gath_shape], specs + [VMEM] * 10,
        [pltpu.VMEM(*own8), rows], limit=24 * MIB,
    )(*common, total, current_field, cur_in, cur_x, prior_field, pri_in, pri_x, v, v_in, v_x)
    for r in range(1, 4):
        got_in = lax.ppermute(send_in, "space", pair_in)
        got_x = lax.ppermute(send_x, "space", pair_x)
        args = (*common, u, got_in, got_x, prev, coef, gath)
        scratch = [pltpu.VMEM((24,) + plane, f32), pltpu.VMEM(*ext16), rows]
        if r < 3:
            prev, u, send_in, send_x, gath = call(
                lambda *refs, r=r: round_kernel(2 * r, *refs), [ext16, own8, send, send, gath_shape],
                specs + [VMEM] * 6, scratch, limit=28 * MIB,
            )(*args)
        else:
            u, gath = call(
                lambda *refs, r=r: last_round_kernel(2 * r, *refs), [own8, gath_shape],
                specs + [VMEM] * 6, [pltpu.VMEM(*ext16)] + scratch, limit=28 * MIB,
            )(*args)
    back = lax.all_to_all(gath, "shot", split_axis=0, concat_axis=0, tiled=True)
    return u[None], jnp.sum(back, axis=0)[None, None]


def solution(mesh):
    placed = (
        P("shot", "space", None, None),
        P("shot", "space", None, None),
        P("shot", "space", None, None),
        P(),
        P(),
        P("shot", None),
        P("shot", None),
        P("shot", None),
        P("shot", "space", None, None),
        P("shot", "space", None, None),
        P("shot", "space"),
        P("shot", "space", None, None),
    )
    return jax.shard_map(
        on_device,
        mesh=mesh,
        in_specs=placed,
        out_specs=(P("shot", "space", None, None), P("shot", "space", None, None)),
        check_vma=False,
    )
```

profile of v0, /device:TPU:16, one launch (start us, length us, event | category | flops | bytes accessed | tf_op | source)
XLA Modules:
  0.0 146.6 jit_solution(17197297397556944329)
XLA Ops:
  0.6 0.0 copy-start.1
  0.6 0.0 copy-start.3
  0.7 1.3 copy-done.3
  1.9 0.0 copy-start.7
  1.9 0.7 copy-done.7
  2.6 0.7 copy-done.12
  3.3 4.3 %shard_map.151 = bf16[8,8,64,128]{3,2,1,0:T(8,128)(2,1)} custom-call(s32[64]{0:T(128)S(1)} %copy-done.12, s32[8,8]{1,0:T(8,128)S(1)} %copy-done.7, bf16[8,8,64,64]{3,2,1,0:T(8,128)(2,1)S(1)} %copy-done.3), custom_call_target="tpu_custom_call" | custom-call | tf_op jit(solution)/shard_map/pallas_call | solution.py:364
  7.5 0.0 copy-start.2
  7.6 4.9 %all-to-all-start = ((bf16[8,8,64,128]{3,2,1,0:T(8,128)(2,1)}), bf16[8,8,64,128]{3,2,1,0:T(8,128)(2,1)S(1)}, u32[]{:S(2)}, u32[]{:S(2)}) async-start(bf16[8,8,64,128]{3,2,1,0:T(8,128)(2,1)} %shard_map.151), calls=%async_computation | async-start | bytes 2097152 | tf_op jit(solution)/shard_map/all_to_all | solution.py:367
  12.4 0.0 copy-done.1
  12.4 5.2 %collective-permute-start.1 = (bf16[1,8,128,256]{3,2,1,0:T(8,128)(2,1)S(1)}, bf16[1,8,128,256]{3,2,1,0:T(8,128)(2,1)S(1)}, u32[]{:S(2)}, u32[]{:S(2)}) collective-permute-start(bf16[1,8,128,256]{3,2,1,0:T(8,128)(2,1)S(1)} %copy-done.1), channel_id=1, source_target_pairs={{1,2},{3,4},{5,6},{7,8},{9,10},{11,12},{13,14},{2,1},{4,3},{6,5},{... | collective-permute-start | bytes 1572872 | tf_op jit(solution)/shard_map/ppermute | solution.py:361
  17.6 0.1 collective-permute-start
  17.7 0.0 copy-done.4
  17.7 0.5 collective-permute-start.2
  18.2 4.0 %collective-permute-start.3 = (bf16[1,8,128,256]{3,2,1,0:T(8,128)(2,1)S(1)}, bf16[1,8,128,256]{3,2,1,0:T(8,128)(2,1)}, u32[]{:S(2)}, u32[]{:S(2)}) collective-permute-start(bf16[1,8,128,256]{3,2,1,0:T(8,128)(2,1)S(1)} %copy-done.4), channel_id=1, source_target_pairs={{1,2},{3,4},{5,6},{7,8},{9,10},{11,12},{13,14},{2,1},{4,3},{6,5},{... | collective-permute-start | bytes 1572872 | tf_op jit(solution)/shard_map/ppermute | solution.py:361
  22.2 6.0 %all-to-all-done.arrived = bf16[8,8,64,128]{3,2,1,0:T(8,128)(2,1)S(1)} async-done(((bf16[8,8,64,128]{3,2,1,0:T(8,128)(2,1)}), bf16[8,8,64,128]{3,2,1,0:T(8,128)(2,1)S(1)}, u32[]{:S(2)}, u32[]{:S(2)}) %all-to-all-start) | async-done | bytes 1048608 | tf_op jit(solution)/shard_map/all_to_all | solution.py:367
  28.2 0.0 copy-done.8
  28.2 0.0 copy-done.13
  28.2 4.1 %shard_map.152 = (bf16[8,128,256]{2,1,0:T(8,128)(2,1)S(1)}, bf16[4,128,256]{2,1,0:T(8,128)(2,1)}, bf16[4,128,256]{2,1,0:T(8,128)(2,1)}) custom-call(s32[64]{0:T(128)S(1)} %copy-done.13, s32[8,8]{1,0:T(8,128)S(1)} %copy-done.8, bf16[8,8,64,128]{3,2,1,0:T(8,128)(2,1)S(1)} %all-to-all-done.arrived), custom_call_target="tpu_custom_call" | custom-call | tf_op jit(solution)/shard_map/pallas_call | solution.py:377
  32.4 0.8 copy-done.5
  33.1 0.0 collective-permute-start.4
  33.1 1.2 collective-permute-done.1.got_x.cur_x
  34.3 4.9 %collective-permute-start.5 = (bf16[4,128,256]{2,1,0:T(8,128)(2,1)}, bf16[4,128,256]{2,1,0:T(8,128)(2,1)}, u32[]{:S(2)}, u32[]{:S(2)}) collective-permute-start(bf16[4,128,256]{2,1,0:T(8,128)(2,1)} %get-tuple-element.29), channel_id=1, source_target_pairs={{1,2},{3,4},{5,6},{7,8},{9,10},{11,12},{13,14},{2,1},{4,3},{6,5},{... | collective-permute-start | bytes 786440 | tf_op jit(solution)/shard_map/ppermute | solution.py:381
  39.9 0.0 copy-done.14
  39.9 0.0 copy-start.6
  39.9 0.0 copy-start.9
  40.0 0.0 copy-start.10
  40.0 0.0 copy-start.11
  40.0 0.1 copy.28.cells.refs_5_
  40.1 0.0 copy-done.15
  40.1 0.1 copy.29.fracs.refs_6_
  40.2 0.0 copy-done.16
  40.2 0.1 copy.30.owner.refs_8_
  40.3 0.3 shard_map.149
  40.6 0.0 collective-permute-done.got_in.cur_in
  40.6 0.0 copy-done
  40.6 0.0 copy-done.2
  40.6 4.7 %shard_map.150.total = f32[16,128,256]{2,1,0:T(8,128)S(1)} custom-call(bf16[512,256]{1,0:T(8,128)(2,1)S(1)} %copy-done, bf16[128,256]{1,0:T(8,128)(2,1)S(1)} %copy-done.2, bf16[1,8,128,256]{3,2,1,0:T(8,128)(2,1)S(1)} %copy-done.1, bf16[1,8,128,256]{3,2,1,0:T(8,128)(2,1)S(1)} %collective-permute-done.got_in.cur_in, ...), custom_call_target="tpu_custom_call" | custom-call | tf_op jit(solution)/shard_map/pallas_call | solution.py:374
  45.3 0.0 collective-permute-done.2.pri_in
  45.3 0.0 collective-permute-done.3.pri_x
  45.3 0.0 collective-permute-done.4.v_in
  45.3 0.6 collective-permute-done.5.v_x
  46.0 0.0 copy-done.6
  46.0 0.0 copy-done.9
  46.0 0.0 copy-done.10
  46.0 0.0 copy-done.11
  46.0 5.9 %shard_map.153 = (f32[16,128,256]{2,1,0:T(8,128)S(1)}, f32[8,128,256]{2,1,0:T(8,128)S(1)}, f32[16,128,256]{2,1,0:T(8,128)S(1)}, bf16[9,128,256]{2,1,0:T(8,128)(2...) custom-call(bf16[512,256]{1,0:T(8,128)(2,1)S(1)} %copy-done, bf16[128,256]{1,0:T(8,128)(2,1)S(1)} %copy-done.2, ...), custom_call_target="tpu_custom_call" | custom-call | tf_op jit(solution)/shard_map/pallas_call | solution.py:392
  51.9 0.1 collective-permute-start.6
  52.0 5.1 %collective-permute-start.7 = (bf16[9,128,256]{2,1,0:T(8,128)(2,1)S(1)}, bf16[9,128,256]{2,1,0:T(8,128)(2,1)S(1)}, u32[]{:S(2)}, u32[]{:S(2)}) collective-permute-start(bf16[9,128,256]{2,1,0:T(8,128)(2,1)S(1)} %get-tuple-element.32), channel_id=1, source_target_pairs={{1,2},{3,4},{5,6},{7,8},{9,10},{11,12},{13,14},{2,1},{4,3},{6,5},{... | collective-permute-start | bytes 1769480 | tf_op jit(solution)/shard_map/ppermute | solution.py:398
  57.1 0.0 collective-permute-done.6.refs_12_
  57.1 9.7 %collective-permute-done.7.refs_13_ = bf16[9,128,256]{2,1,0:T(8,128)(2,1)S(1)} collective-permute-done((bf16[9,128,256]{2,1,0:T(8,128)(2,1)S(1)}, bf16[9,128,256]{2,1,0:T(8,128)(2,1)S(1)}, u32[]{:S(2)}, u32[]{:S(2)}) %collective-permute-start.7) | collective-permute-done | bytes 589856 | tf_op jit(solution)/shard_map/ppermute | solution.py:398
  66.8 10.1 %shard_map.154 = (f32[16,128,256]{2,1,0:T(8,128)S(1)}, f32[8,128,256]{2,1,0:T(8,128)S(1)}, bf16[9,128,256]{2,1,0:T(8,128)(2,1)S(1)}, bf16[9,128,256]{2,1,0:T(8,128)(2,1)S(1)}, f32[8,8,128]{2,1,0:T(8,128)S(1)}) custom-call(bf16[512,256]{1,0:T(8,128)(2,1)S(1)} %copy-done, bf16[128,256]{1,0:T(8,128)(2,1)S(1)} %copy-done.2, s32[1,3]{1,0:T(1,128)S(1)} %copy-done.9, ...), custom_call_target="tpu_custom_call" | custom-call | tf_op jit(solution)/shard_map/pallas_call | solution.py:402
  76.9 0.1 collective-permute-start.8
  77.0 5.3 %collective-permute-start.9 = (bf16[9,128,256]{2,1,0:T(8,128)(2,1)S(1)}, bf16[9,128,256]{2,1,0:T(8,128)(2,1)S(1)}, u32[]{:S(2)}, u32[]{:S(2)}) collective-permute-start(bf16[9,128,256]{2,1,0:T(8,128)(2,1)S(1)} %get-tuple-element.38), channel_id=1, source_target_pairs={{1,2},{3,4},{5,6},{7,8},{9,10},{11,12},{13,14},{2,1},{4,3},{6,5},{... | collective-permute-start | bytes 1769480 | tf_op jit(solution)/shard_map/ppermute | solution.py:398
  82.3 0.0 collective-permute-done.8.refs_12_
  82.3 9.5 %collective-permute-done.9.refs_13_ = bf16[9,128,256]{2,1,0:T(8,128)(2,1)S(1)} collective-permute-done((bf16[9,128,256]{2,1,0:T(8,128)(2,1)S(1)}, bf16[9,128,256]{2,1,0:T(8,128)(2,1)S(1)}, u32[]{:S(2)}, u32[]{:S(2)}) %collective-permute-start.9) | collective-permute-done | bytes 589856 | tf_op jit(solution)/shard_map/ppermute | solution.py:398
  91.8 10.1 %shard_map.155 = (f32[16,128,256]{2,1,0:T(8,128)S(1)}, f32[8,128,256]{2,1,0:T(8,128)S(1)}, bf16[9,128,256]{2,1,0:T(8,128)(2,1)S(1)}, bf16[9,128,256]{2,1,0:T(8,128)(2,1)S(1)}, f32[8,8,128]{2,1,0:T(8,128)S(1)}) custom-call(bf16[512,256]{1,0:T(8,128)(2,1)S(1)} %copy-done, bf16[128,256]{1,0:T(8,128)(2,1)S(1)} %copy-done.2, s32[1,3]{1,0:T(1,128)S(1)} %copy-done.9, ...), custom_call_target="tpu_custom_call" | custom-call | tf_op jit(solution)/shard_map/pallas_call | solution.py:402
  101.9 0.1 collective-permute-start.10
  102.0 5.5 %collective-permute-start.11 = (bf16[9,128,256]{2,1,0:T(8,128)(2,1)S(1)}, bf16[9,128,256]{2,1,0:T(8,128)(2,1)S(1)}, u32[]{:S(2)}, u32[]{:S(2)}) collective-permute-start(bf16[9,128,256]{2,1,0:T(8,128)(2,1)S(1)} %get-tuple-element.43), channel_id=1, source_target_pairs={{1,2},{3,4},{5,6},{7,8},{9,10},{11,12},{13,14},{2,1},{4,3},{6,5},{... | collective-permute-start | bytes 1769480 | tf_op jit(solution)/shard_map/ppermute | solution.py:398
  107.5 0.0 collective-permute-done.10.refs_12_
  107.6 9.3 %collective-permute-done.11.refs_13_ = bf16[9,128,256]{2,1,0:T(8,128)(2,1)S(1)} collective-permute-done((bf16[9,128,256]{2,1,0:T(8,128)(2,1)S(1)}, bf16[9,128,256]{2,1,0:T(8,128)(2,1)S(1)}, u32[]{:S(2)}, u32[]{:S(2)}) %collective-permute-start.11) | collective-permute-done | bytes 589856 | tf_op jit(solution)/shard_map/ppermute | solution.py:398
  116.8 10.9 %shard_map.156 = (f32[8,128,256]{2,1,0:T(8,128)}, f32[8,8,128]{2,1,0:T(8,128)S(1)}) custom-call(bf16[512,256]{1,0:T(8,128)(2,1)S(1)} %copy-done, bf16[128,256]{1,0:T(8,128)(2,1)S(1)} %copy-done.2, s32[1,3]{1,0:T(1,128)S(1)} %copy-done.9, s32[1,3]{1,0:T(1,128)S(1)} %copy-done.10, f32[1,8]{1,0:T(1,128)S(1)} %copy-done.11, ...), custom_call_target="tpu_custom_call" | custom-call | tf_op jit(solution)/shard_map/pallas_call | solution.py:407
  127.8 18.2 %all_to_all.10 = f32[8,8,128]{2,1,0:T(8,128)S(1)} all-to-all(f32[8,8,128]{2,1,0:T(8,128)S(1)} %get-tuple-element.47), channel_id=1, replica_groups=mesh['shot'=8,'space'=16] {'shot'}, dimensions={0} | all-to-all | bytes 65536 | tf_op jit(solution)/shard_map/all_to_all | solution.py:411
  146.0 0.6 reduce_sum.9
  (9 shorter events, 0.0 us)
Async XLA Ops:
  0.6 11.8 %copy-start.1 = (bf16[1,8,128,256]{3,2,1,0:T(8,128)(2,1)S(1)}, bf16[1,8,128,256]{3,2,1,0:T(8,128)(2,1)}, u32[]{:S(2)}) copy-start(bf16[1,8,128,256]{3,2,1,0:T(8,128)(2,1)} %cur.1) | copy-start | bytes 1572868
  0.6 1.3 copy-start.3
  1.9 0.7 copy-start.7
  2.6 0.7 copy-start.12
  3.3 14.5 %copy-start.4 = (bf16[1,8,128,256]{3,2,1,0:T(8,128)(2,1)S(1)}, bf16[1,8,128,256]{3,2,1,0:T(8,128)(2,1)}, u32[]{:S(2)}) copy-start(bf16[1,8,128,256]{3,2,1,0:T(8,128)(2,1)} %pri.1) | copy-start | bytes 1572868
  3.3 25.0 %copy-start.8 = (s32[8,8]{1,0:T(8,128)S(1)}, s32[8,8]{1,0:T(8,128)}, u32[]{:S(2)}) copy-start(s32[8,8]{1,0:T(8,128)} %wanted.3) | copy-start | bytes 772
  3.3 25.0 %copy-start.13 = (s32[64]{0:T(128)S(1)}, s32[64]{0:T(128)}, u32[]{:S(2)}) copy-start(s32[64]{0:T(128)} %home.3) | copy-start | bytes 772
  7.5 32.4 %copy-start.14 = (s32[1,1,64,3]{2,1,3,0:T(1,128)S(1)}, s32[1,1,64,3]{2,1,3,0:T(1,128)}, u32[]{:S(2)}) copy-start(s32[1,1,64,3]{2,1,3,0:T(1,128)} %param.22) | copy-start | bytes 2308
  7.5 32.5 %copy-start.15 = (s32[1,1,64,3]{2,1,3,0:T(1,128)S(1)}, s32[1,1,64,3]{2,1,3,0:T(1,128)}, u32[]{:S(2)}) copy-start(s32[1,1,64,3]{2,1,3,0:T(1,128)} %param.23) | copy-start | bytes 2308
  7.5 32.6 %copy-start.16 = (s32[1,1,64,1]{2,3,1,0:T(1,128)S(1)}, s32[1,1,64,1]{2,3,1,0:T(1,128)}, u32[]{:S(2)}) copy-start(s32[1,1,64,1]{2,3,1,0:T(1,128)} %param.25) | copy-start | bytes 772
  7.5 33.0 %copy-start = (bf16[512,256]{1,0:T(8,128)(2,1)S(1)}, bf16[512,256]{1,0:T(8,128)(2,1)}, u32[]{:S(2)}) copy-start(bf16[512,256]{1,0:T(8,128)(2,1)} %constant.6.clone.weights.refs_0_) | copy-start | bytes 786436
  7.5 33.0 %copy-start.2 = (bf16[128,256]{1,0:T(8,128)(2,1)S(1)}, bf16[128,256]{1,0:T(8,128)(2,1)}, u32[]{:S(2)}) copy-start(bf16[128,256]{1,0:T(8,128)(2,1)} %constant.7.clone.across.refs_1_) | copy-start | bytes 196612
  7.6 20.7 %all-to-all-start = ((bf16[8,8,64,128]{3,2,1,0:T(8,128)(2,1)}), bf16[8,8,64,128]{3,2,1,0:T(8,128)(2,1)S(1)}, u32[]{:S(2)}, u32[]{:S(2)}) async-start(bf16[8,8,64,128]{3,2,1,0:T(8,128)(2,1)} %shard_map.151), calls=%async_computation | async-start | bytes 2097152 | tf_op jit(solution)/shard_map/all_to_all | solution.py:367
  12.4 21.9 %collective-permute-start.1 = (bf16[1,8,128,256]{3,2,1,0:T(8,128)(2,1)S(1)}, bf16[1,8,128,256]{3,2,1,0:T(8,128)(2,1)S(1)}, u32[]{:S(2)}, u32[]{:S(2)}) collective-permute-start(bf16[1,8,128,256]{3,2,1,0:T(8,128)(2,1)S(1)} %copy-done.1), channel_id=1, source_target_pairs={{1,2},{3,4},{5,6},{7,8},{9,10},{11,12},{13,14},{2,1},{4,3},{6,5},{... | collective-permute-start | bytes 1572872 | tf_op jit(solution)/shard_map/ppermute | solution.py:361
  17.6 22.9 %collective-permute-start = (bf16[1,8,128,256]{3,2,1,0:T(8,128)(2,1)S(1)}, bf16[1,8,128,256]{3,2,1,0:T(8,128)(2,1)S(1)}, u32[]{:S(2)}, u32[]{:S(2)}) collective-permute-start(bf16[1,8,128,256]{3,2,1,0:T(8,128)(2,1)S(1)} %copy-done.1), channel_id=1, source_target_pairs={{0,1},{1,0},{2,3},{3,2},{4,5},{5,4},{6,7},{7,6},{8,9},{9,8},{10,11... | collective-permute-start | bytes 1572872 | tf_op jit(solution)/shard_map/ppermute | solution.py:361
  17.7 27.6 %collective-permute-start.2 = (bf16[1,8,128,256]{3,2,1,0:T(8,128)(2,1)S(1)}, bf16[1,8,128,256]{3,2,1,0:T(8,128)(2,1)}, u32[]{:S(2)}, u32[]{:S(2)}) collective-permute-start(bf16[1,8,128,256]{3,2,1,0:T(8,128)(2,1)S(1)} %copy-done.4), channel_id=1, source_target_pairs={{0,1},{1,0},{2,3},{3,2},{4,5},{5,4},{6,7},{7,6},{8,9},{9,8},{10,11... | collective-permute-start | bytes 1572872 | tf_op jit(solution)/shard_map/ppermute | solution.py:361
  18.2 27.1 %collective-permute-start.3 = (bf16[1,8,128,256]{3,2,1,0:T(8,128)(2,1)S(1)}, bf16[1,8,128,256]{3,2,1,0:T(8,128)(2,1)}, u32[]{:S(2)}, u32[]{:S(2)}) collective-permute-start(bf16[1,8,128,256]{3,2,1,0:T(8,128)(2,1)S(1)} %copy-done.4), channel_id=1, source_target_pairs={{1,2},{3,4},{5,6},{7,8},{9,10},{11,12},{13,14},{2,1},{4,3},{6,5},{... | collective-permute-start | bytes 1572872 | tf_op jit(solution)/shard_map/ppermute | solution.py:361
  32.3 0.8 copy-start.5
  33.1 12.2 %collective-permute-start.4 = (bf16[4,128,256]{2,1,0:T(8,128)(2,1)}, bf16[4,128,256]{2,1,0:T(8,128)(2,1)S(1)}, u32[]{:S(2)}, u32[]{:S(2)}) collective-permute-start(bf16[4,128,256]{2,1,0:T(8,128)(2,1)} %get-tuple-element.28), channel_id=1, source_target_pairs={{0,1},{1,0},{2,3},{3,2},{4,5},{5,4},{6,7},{7,6},{8,9},{9,8},{10,11... | collective-permute-start | bytes 786440 | tf_op jit(solution)/shard_map/ppermute | solution.py:380
  34.3 11.6 %collective-permute-start.5 = (bf16[4,128,256]{2,1,0:T(8,128)(2,1)}, bf16[4,128,256]{2,1,0:T(8,128)(2,1)}, u32[]{:S(2)}, u32[]{:S(2)}) collective-permute-start(bf16[4,128,256]{2,1,0:T(8,128)(2,1)} %get-tuple-element.29), channel_id=1, source_target_pairs={{1,2},{3,4},{5,6},{7,8},{9,10},{11,12},{13,14},{2,1},{4,3},{6,5},{... | collective-permute-start | bytes 786440 | tf_op jit(solution)/shard_map/ppermute | solution.py:381
  39.9 6.0 %copy-start.6 = (bf16[8,128,256]{2,1,0:T(8,128)(2,1)S(1)}, bf16[8,128,256]{2,1,0:T(8,128)(2,1)}, u32[]{:S(2)}) copy-start(bf16[8,128,256]{2,1,0:T(8,128)(2,1)} %copy-done.5) | copy-start | bytes 1572868
  39.9 6.0 %copy-start.9 = (s32[1,3]{1,0:T(1,128)S(1)}, s32[1,3]{1,0:T(1,128)}, u32[]{:S(2)}) copy-start(s32[1,3]{1,0:T(1,128)} %refs_2_.5) | copy-start | bytes 40
  40.0 6.0 %copy-start.10 = (s32[1,3]{1,0:T(1,128)S(1)}, s32[1,3]{1,0:T(1,128)}, u32[]{:S(2)}) copy-start(s32[1,3]{1,0:T(1,128)} %refs_3_.5) | copy-start | bytes 40
  40.0 6.0 %copy-start.11 = (f32[1,8]{1,0:T(1,128)S(1)}, f32[1,8]{1,0:T(1,128)}, u32[]{:S(2)}) copy-start(f32[1,8]{1,0:T(1,128)} %refs_4_.5) | copy-start | bytes 100
  51.9 5.2 %collective-permute-start.6 = (bf16[9,128,256]{2,1,0:T(8,128)(2,1)S(1)}, bf16[9,128,256]{2,1,0:T(8,128)(2,1)S(1)}, u32[]{:S(2)}, u32[]{:S(2)}) collective-permute-start(bf16[9,128,256]{2,1,0:T(8,128)(2,1)S(1)} %get-tuple-element.31), channel_id=1, source_target_pairs={{0,1},{1,0},{2,3},{3,2},{4,5},{5,4},{6,7},{7,6},{8,9},{9,8},{10,11... | collective-permute-start | bytes 1769480 | tf_op jit(solution)/shard_map/ppermute | solution.py:397
  52.0 14.8 %collective-permute-start.7 = (bf16[9,128,256]{2,1,0:T(8,128)(2,1)S(1)}, bf16[9,128,256]{2,1,0:T(8,128)(2,1)S(1)}, u32[]{:S(2)}, u32[]{:S(2)}) collective-permute-start(bf16[9,128,256]{2,1,0:T(8,128)(2,1)S(1)} %get-tuple-element.32), channel_id=1, source_target_pairs={{1,2},{3,4},{5,6},{7,8},{9,10},{11,12},{13,14},{2,1},{4,3},{6,5},{... | collective-permute-start | bytes 1769480 | tf_op jit(solution)/shard_map/ppermute | solution.py:398
  76.9 5.4 %collective-permute-start.8 = (bf16[9,128,256]{2,1,0:T(8,128)(2,1)S(1)}, bf16[9,128,256]{2,1,0:T(8,128)(2,1)S(1)}, u32[]{:S(2)}, u32[]{:S(2)}) collective-permute-start(bf16[9,128,256]{2,1,0:T(8,128)(2,1)S(1)} %get-tuple-element.37), channel_id=1, source_target_pairs={{0,1},{1,0},{2,3},{3,2},{4,5},{5,4},{6,7},{7,6},{8,9},{9,8},{10,11... | collective-permute-start | bytes 1769480 | tf_op jit(solution)/shard_map/ppermute | solution.py:397
  77.0 14.8 %collective-permute-start.9 = (bf16[9,128,256]{2,1,0:T(8,128)(2,1)S(1)}, bf16[9,128,256]{2,1,0:T(8,128)(2,1)S(1)}, u32[]{:S(2)}, u32[]{:S(2)}) collective-permute-start(bf16[9,128,256]{2,1,0:T(8,128)(2,1)S(1)} %get-tuple-element.38), channel_id=1, source_target_pairs={{1,2},{3,4},{5,6},{7,8},{9,10},{11,12},{13,14},{2,1},{4,3},{6,5},{... | collective-permute-start | bytes 1769480 | tf_op jit(solution)/shard_map/ppermute | solution.py:398
  101.9 5.6 %collective-permute-start.10 = (bf16[9,128,256]{2,1,0:T(8,128)(2,1)S(1)}, bf16[9,128,256]{2,1,0:T(8,128)(2,1)S(1)}, u32[]{:S(2)}, u32[]{:S(2)}) collective-permute-start(bf16[9,128,256]{2,1,0:T(8,128)(2,1)S(1)} %get-tuple-element.42), channel_id=1, source_target_pairs={{0,1},{1,0},{2,3},{3,2},{4,5},{5,4},{6,7},{7,6},{8,9},{9,8},{10,11... | collective-permute-start | bytes 1769480 | tf_op jit(solution)/shard_map/ppermute | solution.py:397
  102.0 14.8 %collective-permute-start.11 = (bf16[9,128,256]{2,1,0:T(8,128)(2,1)S(1)}, bf16[9,128,256]{2,1,0:T(8,128)(2,1)S(1)}, u32[]{:S(2)}, u32[]{:S(2)}) collective-permute-start(bf16[9,128,256]{2,1,0:T(8,128)(2,1)S(1)} %get-tuple-element.43), channel_id=1, source_target_pairs={{1,2},{3,4},{5,6},{7,8},{9,10},{11,12},{13,14},{2,1},{4,3},{6,5},{... | collective-permute-start | bytes 1769480 | tf_op jit(solution)/shard_map/ppermute | solution.py:398
where the time goes:
time: 146 us; the launch traced here: 147 us
  Pallas kernels  50.4 us (35%)
  waiting for transfers between devices  36.3 us (25%)
  starting transfers between devices  35.7 us (24%)
  blocking collectives  18.2 us (12%)
  local copies, waits for them, and re-layouts  3.76 us (3%)
  between operations  1.57 us (1%)
    ppermute x3, waiting for transfers between devices, on_device(): got_x = lax.ppermute(send_x, 'space', pair_x)  28.5 us
    pallas_call x2, Pallas kernels, on_device(): call(lambda *refs, r=r: round_kernel(2 * r, *refs), [ext16, own8, send, s...  20.2 us
    all_to_all x1, blocking collectives, on_device(): back = lax.all_to_all(gath, 'shot', split_axis=0, concat_axis=0, tiled=True)  18.2 us
    ppermute x3, starting transfers between devices, on_device(): got_x = lax.ppermute(send_x, 'space', pair_x)  15.9 us
    pallas_call x1, Pallas kernels, on_device(): call(lambda *refs, r=r: last_round_kernel(2 * r, *refs), [own8, gath_shap...  10.9 us
    ppermute x4, starting transfers between devices, swap(): return (lax.ppermute(x, 'space', pair_in), lax.ppermute(x, 'space', pair_x))  9.74 us
    all_to_all x1, waiting for transfers between devices, on_device(): lax.all_to_all(out, 'shot', split_axis=0, concat_axis=0, tiled=True)  6.02 us
    pallas_call x1, Pallas kernels, on_device(): call(first_round_kernel, [ext16, own8, ext16, send, send, gath_shape], sp...  5.87 us
  transfers between devices with their start and end apart: 13, of which 6 were waited for; matrix products, arithmetic and copies ran while one was open for 0% of the time, Pallas kernels for 6%

commit v1 on v0

v1 whole, which is shorter than its diff:
```python
import jax
import jax.numpy as jnp
import numpy as np
from jax import lax
from jax.experimental import pallas as pl
from jax.experimental.pallas import tpu as pltpu
from jax.sharding import PartitionSpec as P

STEPS = 8
CAPR = 16
PL = 8
ROWS = 128
COLS = 256
EDGE = 64
SLOTS = 64
SCALE = 5040.0
TAPS = (8064.0, -1008.0, 128.0, -9.0)
CENTRE_COLS = -43008.0
CENTRE_ROWS = -42.0
COURANT = 0.09

VMEM = pl.BlockSpec(memory_space=pltpu.VMEM)
SMEM = pl.BlockSpec(memory_space=pltpu.SMEM)
HBM = pl.BlockSpec(memory_space=pltpu.HBM)
f32 = jnp.float32
bf16 = jnp.bfloat16


def band_matrix(size, centre):
    gap = np.abs(np.arange(size)[:, None] - np.arange(size)[None, :])
    out = np.where(gap == 0, centre, 0.0)
    for k in range(1, 5):
        out = np.where(gap == k, TAPS[k - 1], out)
    return out


def constants():
    cols = band_matrix(COLS, CENTRE_COLS)
    rows = band_matrix(ROWS, CENTRE_ROWS)
    return (
        jnp.asarray(np.concatenate([cols, cols], 0), bf16),
        jnp.asarray(np.concatenate([rows, rows], 1), bf16),
    )


def call(body, outs, ins, scratch=(), limit=None, cost=None, alias=None):
    return pl.pallas_call(
        body,
        out_shape=[jax.ShapeDtypeStruct(s, d) for s, d in outs],
        in_specs=ins,
        out_specs=[VMEM] * len(outs),
        scratch_shapes=list(scratch),
        input_output_aliases=alias or {},
        compiler_params=pltpu.CompilerParams(vmem_limit_bytes=limit),
        cost_estimate=pl.CostEstimate(flops=cost[0], bytes_accessed=cost[1], transcendentals=0) if cost else None,
    )


def pack_kernel(home_hbm, wanted_hbm, store_hbm, out, home, wanted, store, sems):
    copies = [
        pltpu.make_async_copy(src, dst, sems.at[i])
        for i, (src, dst) in enumerate(((home_hbm, home), (wanted_hbm, wanted), (store_hbm, store)))
    ]
    for copy in copies:
        copy.start()
    copies[0].wait()
    copies[1].wait()
    me = lax.axis_index("shot")
    chosen = []
    for s in range(8):
        count = jnp.int32(0)
        slots = [jnp.int32(0), jnp.int32(0)]
        for j in range(8):
            row = home[wanted[s, j]]
            mine = lax.shift_right_logical(row, 3) == me
            for rank in range(2):
                slots[rank] = jnp.where(mine & (count == rank), row & 7, slots[rank])
            count = count + mine.astype(jnp.int32)
        chosen.append(slots)
    copies[2].wait()
    for s in range(8):
        for p in range(PL):
            out[s, p] = jnp.concatenate([store[chosen[s][0], p], store[chosen[s][1], p]], 1)


def assemble_kernel(home, wanted, arrived, own, send_in, send_x):
    me = lax.axis_index("shot")
    even = lax.rem(lax.axis_index("space"), 2) == 0
    owners = []
    ranks = []
    for j in range(8):
        owners.append(lax.shift_right_logical(home[wanted[me, j]], 3))
        rank = jnp.int32(0)
        for i in range(j):
            rank = rank + (owners[i] == owners[j]).astype(jnp.int32)
        ranks.append(rank)
    for j in range(0, 8, 2):
        rows = slice(j // 4 * EDGE, (j // 4 + 1) * EDGE)
        lanes = slice(j % 4 * EDGE, (j % 4 + 2) * EDGE)
        for p in range(PL):
            halves = []
            for i in (j, j + 1):
                x = arrived[owners[i], p]
                halves.append(jnp.where(ranks[i] == 0, x[:, :EDGE], x[:, EDGE:]))
            own[p, rows, lanes] = jnp.concatenate(halves, 1)
    send_in[...] = own[pl.ds(jnp.where(even, 4, 0), 4)]
    send_x[...] = own[pl.ds(jnp.where(even, 0, 4), 4)]


CHUNK = 16


def product(weights, across, u):
    hi = u.astype(bf16)
    lo = (u - hi.astype(f32)).astype(bf16)
    return jnp.dot(
        jnp.concatenate([hi, lo, across[...]], 1),
        jnp.concatenate([weights[...], hi, lo], 0),
        preferred_element_type=f32,
    )


def chunks():
    return [slice(r, r + CHUNK) for r in range(0, ROWS, CHUNK)]


def depth(get, e, low, high, r, acc):
    for k in range(1, 5):
        parts = [get(p, r) for p in (e + k, e - k) if low <= p < high]
        if parts:
            acc = acc + TAPS[k - 1] * sum(parts[1:], parts[0])
    return acc


def hat(frac):
    share = frac.astype(f32) * 0.125
    return 1.0 - share, share


def add_source(dst, first_plane, count, cell, frac, pulse):
    lane = lax.broadcasted_iota(jnp.int32, (1, COLS), 1)
    wd, wr, wc = hat(frac[0, 0]), hat(frac[0, 1]), hat(frac[0, 2])
    column = jnp.where(lane == cell[0, 2], wc[0], 0.0) + jnp.where(lane == cell[0, 2] + 1, wc[1], 0.0)
    for dp in range(2):
        at = cell[0, 0] + dp - first_plane

        @pl.when((at >= 0) & (at < count))
        def _():
            for dr in range(2):
                row = pl.ds(cell[0, 1] + dr, 1)
                dst[at, row, :] = dst[at, row, :] + pulse * (wd[dp] * wr[dr] * column)


GROUP = 8


def sample(fields, codes, count, spread, place, owner, rows, out):
    def group(g, _):
        for j in range(GROUP):
            r = g * GROUP + j
            code = codes[r]
            wr = hat(code & 7)
            wd = hat(lax.shift_right_logical(code, 3) & 7)
            y = lax.shift_right_logical(code, 6) & 127
            p = lax.shift_right_logical(code, 13)
            for f, (src, off, _) in enumerate(fields):
                acc = None
                for dp in range(2):
                    for dr in range(2):
                        term = (wd[dp] * wr[dr]) * src[p + off + dp, pl.ds(y + dr, 1), :]
                        acc = term if acc is None else acc + term
                rows[f, pl.ds(r, 1), :] = acc
        return 0

    lax.fori_loop(0, lax.div(count[0, 0] + GROUP - 1, GROUP), group, 0)
    live = lax.broadcasted_iota(jnp.int32, (SLOTS, 1), 0) < count[0, 0]
    for f, (_, _, n) in enumerate(fields):
        values = jnp.where(live, jnp.sum(rows[f] * spread[...], axis=1, keepdims=True), 0.0)
        placed = values * place[...]
        for q in range(8):
            out[q, n : n + 1, :] = jnp.sum(jnp.where(owner[0, 0] == q, placed, 0.0), axis=0, keepdims=True)


def receiver_kernel(cells, fracs, count, owner, spread, place):
    lane = lax.broadcasted_iota(jnp.int32, (SLOTS, COLS), 1)
    share = fracs[0, 0, :, 2:3].astype(f32) * 0.125
    at = cells[0, 0, :, 2:3]
    spread[...] = jnp.where(lane == at, 1.0 - share, 0.0) + jnp.where(lane == at + 1, share, 0.0)
    me = lax.axis_index("shot")
    slot = lax.broadcasted_iota(jnp.int32, (SLOTS, 1), 0)
    live = slot < count[0, 0]
    group = lax.broadcasted_iota(jnp.int32, (SLOTS, 128), 1)
    chosen = jnp.where((owner[0, 0] == group) & live, 1.0, 0.0)
    earlier = jnp.where(
        lax.broadcasted_iota(jnp.int32, (SLOTS, SLOTS), 1) < lax.broadcasted_iota(jnp.int32, (SLOTS, SLOTS), 0), 1.0, 0.0
    )
    before = jnp.dot(earlier.astype(bf16), chosen.astype(bf16), preferred_element_type=f32)
    rank = jnp.sum(before * chosen, axis=1, keepdims=True).astype(jnp.int32)
    place[...] = jnp.where((group == rank + me * CAPR) & live, 1.0, 0.0)


def position(even, first, second):
    return jnp.where(even, second, first), jnp.where(even, first, second)


def open_kernel(weights, across, own, got_in, got_x, total, ext):
    even = lax.rem(lax.axis_index("space"), 2) == 0
    at_in, at_x = position(even, 0, 16)
    for p in range(PL):
        ext[8 + p] = own[0, p].astype(f32)
        ext[at_in + p] = got_in[0, p].astype(f32)
        ext[at_x + p] = got_x[0, p].astype(f32)

    def some(g, _):
        for j in range(8):
            i = g * 8 + j
            m = product(weights, across, ext[i + 4])
            for r in chunks():
                total[i, r] = depth(lambda p, r: ext[i + 4 + p, r], 0, -4, 5, r, m[r])
        return 0

    lax.fori_loop(0, 2, some, 0)


def factor(x):
    scaled = x.astype(f32) * COURANT
    return scaled * scaled * (1.0 / SCALE)


def near_kernel(weights, across, cell, frac, pulses, total, cur, pri, v, coef, next_ext, base):
    band = lax.axis_index("space")
    for p in range(PL):
        for r in chunks():
            c = factor(v[p, r])
            coef[4 + p, r] = c
            next_ext[4 + p, r] = 2.0 * cur[0, p, r].astype(f32) - pri[0, p, r].astype(f32) + c * total[4 + p, r]
    add_source(next_ext.at[pl.ds(4, PL)], band * PL, PL, cell, frac, pulses[0, 0])
    for p in range(PL):
        m = product(weights, across, next_ext[4 + p])
        for r in chunks():
            acc = depth(lambda e, r: next_ext[4 + e, r], p, 0, PL, r, m[r])
            base[p, r] = 2.0 * next_ext[4 + p, r] - cur[0, p, r].astype(f32) + coef[4 + p, r] * acc


def add_far(dst, base, coef, far):
    for p in range(PL):
        for r in chunks():
            acc = None
            for k in range(1, 5):
                for e in (p + k, p - k):
                    if not 0 <= e < PL:
                        term = TAPS[k - 1] * far(e, r)
                        acc = term if acc is None else acc + term
            dst(p, r, base[p, r] + coef[4 + p, r] * acc)


def pack_send(u, send_in, send_x):
    even = lax.rem(lax.axis_index("space"), 2) == 0
    for p in range(PL):
        hi = u[p].astype(bf16)
        send_in[p] = hi
        send_x[p] = hi
    near_in, near_x = position(even, 0, PL - 1)
    for ref, near in ((send_in, near_in), (send_x, near_x)):
        edge = u[near]
        ref[PL] = (edge - edge.astype(bf16).astype(f32)).astype(bf16)


def far_kernel(
    cell, frac, pulses, total, cur_in, cur_x, pri_in, pri_x, v_in, v_x, base, coef_in, next_in,
    coef, next_ext, last, send_in, send_x,
):
    band = lax.axis_index("space")
    even = lax.rem(band, 2) == 0
    at_in, at_x = position(even, 0, 12)
    half_in, half_x = position(even, 4, 0)
    for at, half, vel, now, before in ((at_in, half_in, v_in, cur_in, pri_in), (at_x, half_x, v_x, cur_x, pri_x)):
        for p in range(4):
            for r in chunks():
                c = factor(vel[p, r])
                coef[at + p, r] = c
                next_ext[at + p, r] = (
                    2.0 * now[0, half + p, r].astype(f32) - before[0, half + p, r].astype(f32) + c * total[at + p, r]
                )
    add_source(next_ext.at[pl.ds(0, 4)], band * PL - 4, 4, cell, frac, pulses[0, 0])
    add_source(next_ext.at[pl.ds(12, 4)], band * PL + PL, 4, cell, frac, pulses[0, 0])

    def store(p, r, x):
        last[p, r] = x

    add_far(store, base, coef, lambda e, r: next_ext[4 + e, r])
    add_source(last, band * PL, PL, cell, frac, pulses[0, 1])
    pack_send(last, send_in, send_x)


def during_kernel(first_step, weights, across, codes, count, owner, spread, place, u, prev, coef, *rest):
    part, gath, rows = rest[-3:]
    for p in range(PL):
        m = product(weights, across, u[p])
        for r in chunks():
            acc = depth(lambda e, r: u[e, r], p, 0, PL, r, m[r])
            part[p, r] = 2.0 * u[p, r] - prev[4 + p, r] + coef[4 + p, r] * acc
    sample(((prev, 4, first_step - 2), (u, 0, first_step - 1)), codes, count, spread, place, owner, rows, gath)


def after_kernel(
    first_step, weights, across, cell, frac, pulses, u, got_in, got_x, prev, coef, part,
    next_ext, last, halo,
):
    band = lax.axis_index("space")
    even = lax.rem(band, 2) == 0
    at_in, at_x = position(even, 0, PL)
    near_in, near_x = position(even, PL - 1, PL)
    for p in range(PL):
        halo[at_in + p] = got_in[p].astype(f32)
        halo[at_x + p] = got_x[p].astype(f32)
    halo[near_in] = halo[near_in] + got_in[PL].astype(f32)
    halo[near_x] = halo[near_x] + got_x[PL].astype(f32)

    def now(e, r):
        return halo[e + PL, r] if e < 0 else (u[e, r] if e < PL else halo[e, r])

    for e in (-4, -3, -2, -1, 8, 9, 10, 11):
        i = e + 4
        m = product(weights, across, now(e, slice(0, ROWS)))
        for r in chunks():
            acc = depth(now, e, -8, 16, r, m[r])
            next_ext[i, r] = 2.0 * now(e, r) - prev[i, r] + coef[i, r] * acc

    def store(p, r, x):
        next_ext[4 + p, r] = x

    add_far(store, part, coef, now)
    add_source(next_ext, band * PL - 4, 16, cell, frac, pulses[0, first_step])
    for p in range(PL):
        m = product(weights, across, next_ext[4 + p])
        for r in chunks():
            acc = depth(lambda e, r: next_ext[4 + e, r], p, -4, 12, r, m[r])
            last[p, r] = 2.0 * next_ext[4 + p, r] - u[p, r] + coef[4 + p, r] * acc
    add_source(last, band * PL, PL, cell, frac, pulses[0, first_step + 1])


def middle_kernel(first_step, *refs):
    (next_ext, last, send_in, send_x, halo), ins = refs[-5:], refs[:-5]
    after_kernel(first_step, *ins, next_ext, last, halo)
    pack_send(last, send_in, send_x)


def last_kernel(first_step, codes, count, owner, spread, place, gath_in, *refs):
    (last, gath, next_ext, halo, rows), ins = refs[-5:], refs[:-5]
    after_kernel(first_step, *ins, next_ext, last, halo)
    sample(((next_ext, 4, first_step), (last, 0, first_step + 1)), codes, count, spread, place, owner, rows, gath)


MIB = 1 << 20


def on_device(
    prior_field, current_field, model_store, tile_home, aperture, source_cell, source_frac,
    wavelet, receiver_cell, receiver_frac, receiver_count, trace_owner,
):
    size = lax.axis_size("space")
    pair_in = [(i, i ^ 1) for i in range(size)]
    pair_x = [(i, i + 1) for i in range(1, size - 1, 2)] + [(i + 1, i) for i in range(1, size - 1, 2)]

    def swap(in_chip, across_chips):
        return lax.ppermute(in_chip, "space", pair_in), lax.ppermute(across_chips, "space", pair_x)

    weights, across = constants()
    out = call(
        pack_kernel, [((8, PL, EDGE, 2 * EDGE), bf16)], [HBM] * 3,
        [pltpu.SMEM((64,), jnp.int32), pltpu.SMEM((8, 8), jnp.int32), pltpu.VMEM((8, PL, EDGE, EDGE), bf16),
         pltpu.SemaphoreType.DMA((3,))],
        limit=8 * MIB,
    )(tile_home, aperture, model_store)[0]
    arrived = lax.all_to_all(out, "shot", split_axis=0, concat_axis=0, tiled=True)
    cur_in, cur_x = swap(current_field, current_field)
    pri_in, pri_x = swap(prior_field, prior_field)
    spread, place = call(
        receiver_kernel, [((SLOTS, COLS), f32), ((SLOTS, 128), f32)], [VMEM, VMEM, SMEM, VMEM], limit=4 * MIB
    )(receiver_cell, receiver_frac, receiver_count, trace_owner)
    cells, fracs = receiver_cell[0, 0], receiver_frac[0, 0]
    codes = ((cells[:, 0] * ROWS + cells[:, 1]) * 8 + fracs[:, 0]) * 8 + fracs[:, 1]
    plane = (ROWS, COLS)
    own8 = ((PL,) + plane, f32)
    ext16 = ((16,) + plane, f32)
    send = ((PL + 1,) + plane, bf16)
    gath_shape = ((8, STEPS, 128), f32)
    halo = pltpu.VMEM(*ext16)
    rows = pltpu.VMEM((2, SLOTS, COLS), f32)
    total = call(
        open_kernel, [ext16], [VMEM] * 5, [pltpu.VMEM((24,) + plane, f32)], limit=16 * MIB
    )(weights, across, current_field, cur_in, cur_x)[0]
    v, v_send_in, v_send_x = call(
        assemble_kernel, [((PL,) + plane, bf16), ((4,) + plane, bf16), ((4,) + plane, bf16)], [SMEM, SMEM, VMEM], limit=8 * MIB
    )(tile_home, aperture, arrived)
    v_in, v_x = swap(v_send_in, v_send_x)
    source = (source_cell, source_frac, wavelet)
    receivers = (codes, receiver_count, trace_owner, spread, place)
    receiver_specs = [SMEM, SMEM, VMEM, VMEM, VMEM]
    coef, prev, base = call(
        near_kernel, [ext16, ext16, own8], [VMEM] * 2 + [SMEM] * 3 + [VMEM] * 4, limit=16 * MIB
    )(weights, across, *source, total, current_field, prior_field, v)
    coef, prev, u, send_in, send_x = call(
        far_kernel, [ext16, ext16, own8, send, send], [SMEM] * 3 + [VMEM] * 10, limit=24 * MIB, alias={11: 0, 12: 1}
    )(*source, total, cur_in, cur_x, pri_in, pri_x, v_in, v_x, base, coef, prev)
    gath = None
    for n in (2, 4, 6):
        got_in, got_x = swap(send_in, send_x)
        first = gath is None
        part, gath = call(
            lambda *refs, n=n: during_kernel(n, *refs), [own8, gath_shape],
            [VMEM] * 2 + receiver_specs + [VMEM] * (3 if first else 4), [rows], limit=16 * MIB,
            alias={} if first else {10: 1},
        )(weights, across, *receivers, u, prev, coef, *(() if first else (gath,)))
        common = (weights, across, *source, u, got_in, got_x, prev, coef, part)
        common_specs = [VMEM] * 2 + [SMEM] * 3 + [VMEM] * 6
        if n < 6:
            prev, u, send_in, send_x = call(
                lambda *refs, n=n: middle_kernel(n, *refs), [ext16, own8, send, send], common_specs, [halo], limit=24 * MIB
            )(*common)
        else:
            u, gath = call(
                lambda *refs, n=n: last_kernel(n, *refs), [own8, gath_shape],
                receiver_specs + [VMEM] + common_specs, [halo, halo, rows], limit=24 * MIB, alias={5: 1},
            )(*receivers, gath, *common)
    back = lax.all_to_all(gath, "shot", split_axis=0, concat_axis=0, tiled=True)
    return u[None], jnp.sum(back, axis=0)[None, None]


def solution(mesh):
    placed = (
        P("shot", "space", None, None),
        P("shot", "space", None, None),
        P("shot", "space", None, None),
        P(),
        P(),
        P("shot", None),
        P("shot", None),
        P("shot", None),
        P("shot", "space", None, None),
        P("shot", "space", None, None),
        P("shot", "space"),
        P("shot", "space", None, None),
    )
    return jax.shard_map(
        on_device,
        mesh=mesh,
        in_specs=placed,
        out_specs=(P("shot", "space", None, None), P("shot", "space", None, None)),
        check_vma=False,
    )
```

time: 146 us -> 115 us (0.79)
  Pallas kernels: 50.4 us -> 29.4 us
  waiting for transfers between devices: 36.3 us -> 24 us
  blocking collectives: 18.2 us -> 12.3 us
  local copies, waits for them, and re-layouts: 3.76 us -> 8.66 us
  starting transfers between devices: 35.7 us -> 38 us
    pallas_call x6 -> x10, Pallas kernels: 46 us -> 26.3 us  [the longest x2 7.16 us: on_device(): call(lambda *refs, n=n: middle_kernel(n, *refs), [ext16, own8, send, send...]
    ppermute x12, waiting for transfers between devices: 30.3 us -> 17.6 us  [the longest x6 17.5 us: swap(): lax.ppermute(across_chips, 'space', pair_x)]
    all_to_all x1, blocking collectives: 18.2 us -> 12.3 us  [on_device(): back = lax.all_to_all(gath, 'shot', split_axis=0, concat_axis=0, tiled=True)]
    unnamed x37 -> x48, local copies, waits for them, and re-layouts: 3.76 us -> 8.66 us
    ppermute x12, starting transfers between devices: 30.8 us -> 32.9 us  [the longest x6 32.4 us: swap(): lax.ppermute(across_chips, 'space', pair_x)]
  transfers between devices with their start and end apart: 13 -> 13, of which waited for: 6 -> 5; matrix products, arithmetic and copies ran while one was open for 0% -> 2% of each run, Pallas kernels for 6% -> 11%
where the time goes in v1:
time: 115 us
  starting transfers between devices  38 us (33%)
  Pallas kernels  29.4 us (26%)
  waiting for transfers between devices  24 us (21%)
  blocking collectives  12.3 us (11%)
  local copies, waits for them, and re-layouts  8.66 us (8%)
  between operations  1.68 us (1%)
    ppermute x6, starting transfers between devices, swap(): lax.ppermute(across_chips, 'space', pair_x)  32.4 us
    ppermute x6, waiting for transfers between devices, swap(): lax.ppermute(across_chips, 'space', pair_x)  17.5 us
    all_to_all x1, blocking collectives, on_device(): back = lax.all_to_all(gath, 'shot', split_axis=0, concat_axis=0, tiled=True)  12.3 us
    unnamed x48, local copies, waits for them, and re-layouts  8.66 us
    pallas_call x2, Pallas kernels, on_device(): call(lambda *refs, n=n: middle_kernel(n, *refs), [ext16, own8, send, send...  7.16 us
    all_to_all x1, waiting for transfers between devices, on_device(): lax.all_to_all(out, 'shot', split_axis=0, concat_axis=0, tiled=True)  6.41 us
    pallas_call x3, Pallas kernels, on_device(): call(lambda *refs, n=n: during_kernel(n, *refs), [own8, gath_shape], [VME...  6 us
    all_to_all x1, starting transfers between devices, on_device(): lax.all_to_all(out, 'shot', split_axis=0, concat_axis=0, tiled=True)  5.16 us
  transfers between devices with their start and end apart: 13, of which 5 were waited for; matrix products, arithmetic and copies ran while one was open for 2% of the time, Pallas kernels for 11%

profile of v1, /device:TPU:16, one launch (start us, length us, event | category | flops | bytes accessed | tf_op | source)
XLA Modules:
  0.0 114.6 jit_solution(3129223242214438137)
XLA Ops:
  0.6 0.0 copy-start.5
  0.6 0.0 copy-start.10
  0.7 1.3 %copy-done.10 = bf16[8,8,64,64]{3,2,1,0:T(8,128)(2,1)S(1)} copy-done((bf16[8,8,64,64]{3,2,1,0:T(8,128)(2,1)S(1)}, bf16[8,8,64,64]{3,2,1,0:T(8,128)(2,1)}, u32[]{:S(2)}) %copy-start.10) | copy-done | bytes 524312
  1.9 0.7 copy-done.13
  2.6 0.7 copy-done.18
  3.3 2.2 %shard_map.151 = bf16[8,8,64,128]{3,2,1,0:T(8,128)(2,1)} custom-call(s32[64]{0:T(128)S(1)} %copy-done.18, s32[8,8]{1,0:T(8,128)S(1)} %copy-done.13, bf16[8,8,64,64]{3,2,1,0:T(8,128)(2,1)S(1)} %copy-done.10), custom_call_target="tpu_custom_call" | custom-call | tf_op jit(solution)/shard_map/pallas_call | solution.py:370
  5.4 0.0 copy-start.3
  5.5 0.0 copy-start.4
  5.5 5.2 %all-to-all-start = ((bf16[8,8,64,128]{3,2,1,0:T(8,128)(2,1)}), bf16[8,8,64,128]{3,2,1,0:T(8,128)(2,1)S(1)}, u32[]{:S(2)}, u32[]{:S(2)}) async-start(bf16[8,8,64,128]{3,2,1,0:T(8,128)(2,1)} %shard_map.151), calls=%async_computation | async-start | bytes 2097152 | tf_op jit(solution)/shard_map/all_to_all | solution.py:376
  10.6 0.0 copy-done.5
  10.6 0.1 collective-permute-start
  10.7 6.1 %collective-permute-start.1 = (bf16[1,8,128,256]{3,2,1,0:T(8,128)(2,1)S(1)}, bf16[1,8,128,256]{3,2,1,0:T(8,128)(2,1)S(1)}, u32[]{:S(2)}, u32[]{:S(2)}) collective-permute-start(bf16[1,8,128,256]{3,2,1,0:T(8,128)(2,1)S(1)} %copy-done.5), channel_id=1, source_target_pairs={{1,2},{3,4},{5,6},{7,8},{9,10},{11,12},{13,14},{2,1},{4,3},{6,5},{... | collective-permute-start | bytes 1572872 | tf_op jit(solution)/shard_map/ppermute | solution.py:367
  16.8 0.0 copy-done.11
  16.8 0.1 collective-permute-start.2
  16.9 3.1 %collective-permute-start.3 = (bf16[1,8,128,256]{3,2,1,0:T(8,128)(2,1)S(1)}, bf16[1,8,128,256]{3,2,1,0:T(8,128)(2,1)}, u32[]{:S(2)}, u32[]{:S(2)}) collective-permute-start(bf16[1,8,128,256]{3,2,1,0:T(8,128)(2,1)S(1)} %copy-done.11), channel_id=1, source_target_pairs={{1,2},{3,4},{5,6},{7,8},{9,10},{11,12},{13,14},{2,1},{4,3},{6,5},{... | collective-permute-start | bytes 1572872 | tf_op jit(solution)/shard_map/ppermute | solution.py:367
  20.0 6.4 %all-to-all-done.arrived = bf16[8,8,64,128]{3,2,1,0:T(8,128)(2,1)S(1)} async-done(((bf16[8,8,64,128]{3,2,1,0:T(8,128)(2,1)}), bf16[8,8,64,128]{3,2,1,0:T(8,128)(2,1)S(1)}, u32[]{:S(2)}, u32[]{:S(2)}) %all-to-all-start) | async-done | bytes 1048608 | tf_op jit(solution)/shard_map/all_to_all | solution.py:376
  26.4 0.0 copy-done.14
  26.4 0.0 copy-done.19
  26.4 2.8 %shard_map.152 = (bf16[8,128,256]{2,1,0:T(8,128)(2,1)S(1)}, bf16[4,128,256]{2,1,0:T(8,128)(2,1)S(1)}, bf16[4,128,256]{2,1,0:T(8,128)(2,1)S(1)}) custom-call(s32[64]{0:T(128)S(1)} %copy-done.19, s32[8,8]{1,0:T(8,128)S(1)} %copy-done.14, bf16[8,8,64,128]{3,2,1,0:T(8,128)(2,1)S(1)} %all-to-all-done.arrived), custom_call_target="tpu_custom_call" | custom-call | tf_op jit(solution)/shard_map/pallas_call | solution.py:394
  29.2 0.0 copy-start.15
  29.2 0.0 copy-start.16
  29.2 0.0 copy-start.17
  29.2 0.1 collective-permute-start.4
  29.3 0.0 collective-permute-done.got_in.cur_in
  29.3 0.0 copy-start.6
  29.4 6.1 %collective-permute-start.5 = (bf16[4,128,256]{2,1,0:T(8,128)(2,1)S(1)}, bf16[4,128,256]{2,1,0:T(8,128)(2,1)S(1)}, u32[]{:S(2)}, u32[]{:S(2)}) collective-permute-start(bf16[4,128,256]{2,1,0:T(8,128)(2,1)S(1)} %get-tuple-element.34), channel_id=1, source_target_pairs={{1,2},{3,4},{5,6},{7,8},{9,10},{11,12},{13,14},{2,1},{4,3},{6,5},{... | collective-permute-start | bytes 786440 | tf_op jit(solution)/shard_map/ppermute | solution.py:367
  35.5 0.0 collective-permute-done.1.got_x.cur_x
  35.5 0.0 copy-done.3
  35.5 2.0 %shard_map.150.total = f32[16,128,256]{2,1,0:T(8,128)S(1)} custom-call(bf16[512,256]{1,0:T(8,128)(2,1)S(1)} %copy-done.3, bf16[128,256]{1,0:T(8,128)(2,1)S(1)} %copy-done.4, bf16[1,8,128,256]{3,2,1,0:T(8,128)(2,1)S(1)} %copy-done.5, bf16[1,8,128,256]{3,2,1,0:T(8,128)(2,1)S(1)} %collective-permute-done.got_in.cur_in, ...), custom_call_target="tpu_custom_call" | custom-call | tf_op jit(solution)/shard_map/pallas_call | solution.py:391
  37.5 0.0 copy-start.7
  37.5 1.8 %shard_map.153 = (f32[16,128,256]{2,1,0:T(8,128)S(1)}, f32[16,128,256]{2,1,0:T(8,128)S(1)}, f32[8,128,256]{2,1,0:T(8,128)S(1)}) custom-call(bf16[512,256]{1,0:T(8,128)(2,1)S(1)} %copy-done.3, bf16[128,256]{1,0:T(8,128)(2,1)S(1)} %copy-done.4, s32[1,3]{1,0:T(1,128)S(1)} %copy-done.15, s32[1,3]{1,0:T(1,128)S(1)} %copy-done.16, f32[1,8]{1,0:T(1,128)S(1)} %copy-done.17, ...), custom_call_target="tpu_custom_call" | custom-call | tf_op jit(solution)/shard_map/pallas_call | solution.py:401
  39.4 0.0 collective-permute-done.2.pri_in
  39.4 0.0 collective-permute-done.3.pri_x
  39.4 0.0 collective-permute-done.4.v_in
  39.4 1.6 %collective-permute-done.5.v_x = bf16[4,128,256]{2,1,0:T(8,128)(2,1)S(1)} collective-permute-done((bf16[4,128,256]{2,1,0:T(8,128)(2,1)S(1)}, bf16[4,128,256]{2,1,0:T(8,128)(2,1)S(1)}, u32[]{:S(2)}, u32[]{:S(2)}) %collective-permute-start.5) | collective-permute-done | bytes 262176 | tf_op jit(solution)/shard_map/ppermute | solution.py:367
  41.0 3.0 %shard_map.154 = (f32[16,128,256]{2,1,0:T(8,128)S(1)}, f32[16,128,256]{2,1,0:T(8,128)S(1)}, f32[8,128,256]{2,1,0:T(8,128)S(1)}, bf16[9,128,256]{2,1,0:T(8,128)(2,1)}, bf16[9,128,256]{2,1,0:T(8,128)(2,1)}) custom-call(s32[1,3]{1,0:T(1,128)S(1)} %copy-done.15, s32[1,3]{1,0:T(1,128)S(1)} %copy-done.16, ...), custom_call_target="tpu_custom_call", output_to_operand_aliasing={{0}: (11, {}), {1}: (12, {})} | custom-call | tf_op jit(solution)/shard_map/pallas_call | solution.py:404
  44.0 1.4 %copy-done = f32[16,128,256]{2,1,0:T(8,128)} copy-done((f32[16,128,256]{2,1,0:T(8,128)}, f32[16,128,256]{2,1,0:T(8,128)S(1)}, u32[]{:S(2)}) %copy-start) | copy-done | bytes 2097176
  45.3 0.0 collective-permute-start.6
  45.3 5.7 %collective-permute-start.7 = (bf16[9,128,256]{2,1,0:T(8,128)(2,1)}, bf16[9,128,256]{2,1,0:T(8,128)(2,1)}, u32[]{:S(2)}, u32[]{:S(2)}) collective-permute-start(bf16[9,128,256]{2,1,0:T(8,128)(2,1)} %get-tuple-element.41), channel_id=1, source_target_pairs={{1,2},{3,4},{5,6},{7,8},{9,10},{11,12},{13,14},{2,1},{4,3},{6,5},{... | collective-permute-start | bytes 1769480 | tf_op jit(solution)/shard_map/ppermute | solution.py:367
  51.1 0.1 copy.27.owner.refs_4_.refs_2_
  51.8 0.8 copy.21.cells
  52.6 0.7 copy.22.fracs
  53.3 0.8 copy-done.12
  54.1 0.3 shard_map.149
  54.4 0.7 copy_bitcast_fusion
  55.1 1.6 %copy-done.1 = f32[16,128,256]{2,1,0:T(8,128)S(1)} copy-done((f32[16,128,256]{2,1,0:T(8,128)S(1)}, f32[16,128,256]{2,1,0:T(8,128)}, u32[]{:S(2)}) %copy-start.1) | copy-done | bytes 2097176
  56.7 2.0 %shard_map.155 = (f32[8,128,256]{2,1,0:T(8,128)S(1)}, f32[8,8,128]{2,1,0:T(8,128)S(1)}) custom-call(bf16[512,256]{1,0:T(8,128)(2,1)S(1)} %copy-done.3, bf16[128,256]{1,0:T(8,128)(2,1)S(1)} %copy-done.4, s32[64]{0:T(128)S(1)} %add_bitcast_fusion.refs_2_.refs_0_, s32[1,1]{1,0:T(1,128)S(6)} %copy.37.count.refs_3_.refs_1_, ...), custom_call_target="tpu_custom_call" | custom-call | tf_op jit(solution)/shard_map/pallas_call | solution.py:411
  58.7 0.0 collective-permute-done.6.refs_6_
  58.7 1.8 %collective-permute-done.7.refs_7_ = bf16[9,128,256]{2,1,0:T(8,128)(2,1)} collective-permute-done((bf16[9,128,256]{2,1,0:T(8,128)(2,1)}, bf16[9,128,256]{2,1,0:T(8,128)(2,1)}, u32[]{:S(2)}, u32[]{:S(2)}) %collective-permute-start.7) | collective-permute-done | bytes 589856 | tf_op jit(solution)/shard_map/ppermute | solution.py:367
  60.5 4.0 %shard_map.156 = (f32[16,128,256]{2,1,0:T(8,128)S(1)}, f32[8,128,256]{2,1,0:T(8,128)S(1)}, bf16[9,128,256]{2,1,0:T(8,128)(2,1)S(1)}, bf16[9,128,256]{2,1,0:T(8,128)(2,1)S(1)}) custom-call(bf16[512,256]{1,0:T(8,128)(2,1)S(1)} %copy-done.3, bf16[128,256]{1,0:T(8,128)(2,1)S(1)} %copy-done.4, s32[1,3]{1,0:T(1,128)S(1)} %copy-done.15, s32[1,3]{1,0:T(1,128)S(1)} %copy-done.16, ...), custom_call_target="tpu_custom_call" | custom-call | tf_op jit(solution)/shard_map/pallas_call | solution.py:419
  64.5 0.1 collective-permute-start.8
  64.6 5.7 %collective-permute-start.9 = (bf16[9,128,256]{2,1,0:T(8,128)(2,1)S(1)}, bf16[9,128,256]{2,1,0:T(8,128)(2,1)S(1)}, u32[]{:S(2)}, u32[]{:S(2)}) collective-permute-start(bf16[9,128,256]{2,1,0:T(8,128)(2,1)S(1)} %get-tuple-element.47), channel_id=1, source_target_pairs={{1,2},{3,4},{5,6},{7,8},{9,10},{11,12},{13,14},{2,1},{4,3},{6,5},{... | collective-permute-start | bytes 1769480 | tf_op jit(solution)/shard_map/ppermute | solution.py:367
  70.3 2.1 %shard_map.157 = (f32[8,128,256]{2,1,0:T(8,128)S(1)}, f32[8,8,128]{2,1,0:T(8,128)S(1)}) custom-call(bf16[512,256]{1,0:T(8,128)(2,1)S(1)} %copy-done.3, bf16[128,256]{1,0:T(8,128)(2,1)S(1)} %copy-done.4, s32[64]{0:T(128)S(1)} %add_bitcast_fusion.refs_2_.refs_0_, s32[1,1]{1,0:T(1,128)S(6)} %copy.37.count.refs_3_.refs_1_, ...), custom_call_target="tpu_custom_call", output_to_operand_aliasing={{1}: (10, {})} | custom-call | tf_op jit(solution)/shard_map/pallas_call | solution.py:411
  72.4 0.0 collective-permute-done.8.refs_6_
  72.4 7.0 %collective-permute-done.9.refs_7_ = bf16[9,128,256]{2,1,0:T(8,128)(2,1)S(1)} collective-permute-done((bf16[9,128,256]{2,1,0:T(8,128)(2,1)S(1)}, bf16[9,128,256]{2,1,0:T(8,128)(2,1)S(1)}, u32[]{:S(2)}, u32[]{:S(2)}) %collective-permute-start.9) | collective-permute-done | bytes 589856 | tf_op jit(solution)/shard_map/ppermute | solution.py:367
  79.4 3.1 %shard_map.158 = (f32[16,128,256]{2,1,0:T(8,128)S(1)}, f32[8,128,256]{2,1,0:T(8,128)S(1)}, bf16[9,128,256]{2,1,0:T(8,128)(2,1)S(1)}, bf16[9,128,256]{2,1,0:T(8,128)(2,1)S(1)}) custom-call(bf16[512,256]{1,0:T(8,128)(2,1)S(1)} %copy-done.3, bf16[128,256]{1,0:T(8,128)(2,1)S(1)} %copy-done.4, s32[1,3]{1,0:T(1,128)S(1)} %copy-done.15, s32[1,3]{1,0:T(1,128)S(1)} %copy-done.16, ...), custom_call_target="tpu_custom_call" | custom-call | tf_op jit(solution)/shard_map/pallas_call | solution.py:419
  82.6 0.1 collective-permute-start.10
  82.6 5.7 %collective-permute-start.11 = (bf16[9,128,256]{2,1,0:T(8,128)(2,1)S(1)}, bf16[9,128,256]{2,1,0:T(8,128)(2,1)S(1)}, u32[]{:S(2)}, u32[]{:S(2)}) collective-permute-start(bf16[9,128,256]{2,1,0:T(8,128)(2,1)S(1)} %get-tuple-element.56), channel_id=1, source_target_pairs={{1,2},{3,4},{5,6},{7,8},{9,10},{11,12},{13,14},{2,1},{4,3},{6,5},{... | collective-permute-start | bytes 1769480 | tf_op jit(solution)/shard_map/ppermute | solution.py:367
  88.4 1.9 %shard_map.159 = (f32[8,128,256]{2,1,0:T(8,128)S(1)}, f32[8,8,128]{2,1,0:T(8,128)S(1)}) custom-call(bf16[512,256]{1,0:T(8,128)(2,1)S(1)} %copy-done.3, bf16[128,256]{1,0:T(8,128)(2,1)S(1)} %copy-done.4, s32[64]{0:T(128)S(1)} %add_bitcast_fusion.refs_2_.refs_0_, s32[1,1]{1,0:T(1,128)S(6)} %copy.37.count.refs_3_.refs_1_, ...), custom_call_target="tpu_custom_call", output_to_operand_aliasing={{1}: (10, {})} | custom-call | tf_op jit(solution)/shard_map/pallas_call | solution.py:411
  90.3 0.0 collective-permute-done.10.refs_12_
  90.3 7.2 %collective-permute-done.11.refs_13_ = bf16[9,128,256]{2,1,0:T(8,128)(2,1)S(1)} collective-permute-done((bf16[9,128,256]{2,1,0:T(8,128)(2,1)S(1)}, bf16[9,128,256]{2,1,0:T(8,128)(2,1)S(1)}, u32[]{:S(2)}, u32[]{:S(2)}) %collective-permute-start.11) | collective-permute-done | bytes 589856 | tf_op jit(solution)/shard_map/ppermute | solution.py:367
  97.5 4.3 %shard_map.160 = (f32[8,128,256]{2,1,0:T(8,128)}, f32[8,8,128]{2,1,0:T(8,128)S(1)}) custom-call(s32[64]{0:T(128)S(1)} %add_bitcast_fusion.refs_2_.refs_0_, s32[1,1]{1,0:T(1,128)S(6)} %copy.37.count.refs_3_.refs_1_, s32[1,1,64,1]{3,2,1,0:T(8,128)S(1)} %copy.27.owner.refs_4_.refs_2_, ...), custom_call_target="tpu_custom_call", output_to_operand_aliasing={{1}: (5, {})} | custom-call | tf_op jit(solution)/shard_map/pallas_call | solution.py:423
  101.7 12.3 %all_to_all.10 = f32[8,8,128]{2,1,0:T(8,128)S(1)} all-to-all(f32[8,8,128]{2,1,0:T(8,128)S(1)} %get-tuple-element.59), channel_id=1, replica_groups=mesh['shot'=8,'space'=16] {'shot'}, dimensions={0} | all-to-all | bytes 65536 | tf_op jit(solution)/shard_map/all_to_all | solution.py:427
  114.0 0.6 reduce_sum.9
  (25 shorter events, 0.1 us)
Async XLA Ops:
  0.6 10.0 %copy-start.5 = (bf16[1,8,128,256]{3,2,1,0:T(8,128)(2,1)S(1)}, bf16[1,8,128,256]{3,2,1,0:T(8,128)(2,1)}, u32[]{:S(2)}) copy-start(bf16[1,8,128,256]{3,2,1,0:T(8,128)(2,1)} %cur.1) | copy-start | bytes 1572868
  0.6 1.3 %copy-start.10 = (bf16[8,8,64,64]{3,2,1,0:T(8,128)(2,1)S(1)}, bf16[8,8,64,64]{3,2,1,0:T(8,128)(2,1)}, u32[]{:S(2)}) copy-start(bf16[8,8,64,64]{3,2,1,0:T(8,128)(2,1)} %store_hbm.1) | copy-start | bytes 1572868
  1.9 0.7 copy-start.13
  2.6 0.7 copy-start.18
  3.3 13.6 %copy-start.11 = (bf16[1,8,128,256]{3,2,1,0:T(8,128)(2,1)S(1)}, bf16[1,8,128,256]{3,2,1,0:T(8,128)(2,1)}, u32[]{:S(2)}) copy-start(bf16[1,8,128,256]{3,2,1,0:T(8,128)(2,1)} %pri.1) | copy-start | bytes 1572868
  3.3 23.2 %copy-start.14 = (s32[8,8]{1,0:T(8,128)S(1)}, s32[8,8]{1,0:T(8,128)}, u32[]{:S(2)}) copy-start(s32[8,8]{1,0:T(8,128)} %wanted.1) | copy-start | bytes 772
  3.3 23.2 %copy-start.19 = (s32[64]{0:T(128)S(1)}, s32[64]{0:T(128)}, u32[]{:S(2)}) copy-start(s32[64]{0:T(128)} %home.1) | copy-start | bytes 772
  5.4 30.0 %copy-start.3 = (bf16[512,256]{1,0:T(8,128)(2,1)S(1)}, bf16[512,256]{1,0:T(8,128)(2,1)}, u32[]{:S(2)}) copy-start(bf16[512,256]{1,0:T(8,128)(2,1)} %constant.10.clone.weights.refs_0_.refs_6_) | copy-start | bytes 786436
  5.5 30.0 %copy-start.4 = (bf16[128,256]{1,0:T(8,128)(2,1)S(1)}, bf16[128,256]{1,0:T(8,128)(2,1)}, u32[]{:S(2)}) copy-start(bf16[128,256]{1,0:T(8,128)(2,1)} %constant.11.clone.across.refs_1_.refs_7_) | copy-start | bytes 196612
  5.5 21.0 %all-to-all-start = ((bf16[8,8,64,128]{3,2,1,0:T(8,128)(2,1)}), bf16[8,8,64,128]{3,2,1,0:T(8,128)(2,1)S(1)}, u32[]{:S(2)}, u32[]{:S(2)}) async-start(bf16[8,8,64,128]{3,2,1,0:T(8,128)(2,1)} %shard_map.151), calls=%async_computation | async-start | bytes 2097152 | tf_op jit(solution)/shard_map/all_to_all | solution.py:376
  10.6 18.7 %collective-permute-start = (bf16[1,8,128,256]{3,2,1,0:T(8,128)(2,1)S(1)}, bf16[1,8,128,256]{3,2,1,0:T(8,128)(2,1)S(1)}, u32[]{:S(2)}, u32[]{:S(2)}) collective-permute-start(bf16[1,8,128,256]{3,2,1,0:T(8,128)(2,1)S(1)} %copy-done.5), channel_id=1, source_target_pairs={{0,1},{1,0},{2,3},{3,2},{4,5},{5,4},{6,7},{7,6},{8,9},{9,8},{10,11... | collective-permute-start | bytes 1572872 | tf_op jit(solution)/shard_map/ppermute | solution.py:367
  10.7 24.7 %collective-permute-start.1 = (bf16[1,8,128,256]{3,2,1,0:T(8,128)(2,1)S(1)}, bf16[1,8,128,256]{3,2,1,0:T(8,128)(2,1)S(1)}, u32[]{:S(2)}, u32[]{:S(2)}) collective-permute-start(bf16[1,8,128,256]{3,2,1,0:T(8,128)(2,1)S(1)} %copy-done.5), channel_id=1, source_target_pairs={{1,2},{3,4},{5,6},{7,8},{9,10},{11,12},{13,14},{2,1},{4,3},{6,5},{... | collective-permute-start | bytes 1572872 | tf_op jit(solution)/shard_map/ppermute | solution.py:367
  16.8 22.5 %collective-permute-start.2 = (bf16[1,8,128,256]{3,2,1,0:T(8,128)(2,1)S(1)}, bf16[1,8,128,256]{3,2,1,0:T(8,128)(2,1)}, u32[]{:S(2)}, u32[]{:S(2)}) collective-permute-start(bf16[1,8,128,256]{3,2,1,0:T(8,128)(2,1)S(1)} %copy-done.11), channel_id=1, source_target_pairs={{0,1},{1,0},{2,3},{3,2},{4,5},{5,4},{6,7},{7,6},{8,9},{9,8},{10,11... | collective-permute-start | bytes 1572872 | tf_op jit(solution)/shard_map/ppermute | solution.py:367
  16.9 22.5 %collective-permute-start.3 = (bf16[1,8,128,256]{3,2,1,0:T(8,128)(2,1)S(1)}, bf16[1,8,128,256]{3,2,1,0:T(8,128)(2,1)}, u32[]{:S(2)}, u32[]{:S(2)}) collective-permute-start(bf16[1,8,128,256]{3,2,1,0:T(8,128)(2,1)S(1)} %copy-done.11), channel_id=1, source_target_pairs={{1,2},{3,4},{5,6},{7,8},{9,10},{11,12},{13,14},{2,1},{4,3},{6,5},{... | collective-permute-start | bytes 1572872 | tf_op jit(solution)/shard_map/ppermute | solution.py:367
  29.2 8.3 %copy-start.15 = (s32[1,3]{1,0:T(1,128)S(1)}, s32[1,3]{1,0:T(1,128)}, u32[]{:S(2)}) copy-start(s32[1,3]{1,0:T(1,128)} %refs_8_.1) | copy-start | bytes 40
  29.2 8.3 %copy-start.16 = (s32[1,3]{1,0:T(1,128)S(1)}, s32[1,3]{1,0:T(1,128)}, u32[]{:S(2)}) copy-start(s32[1,3]{1,0:T(1,128)} %refs_9_.1) | copy-start | bytes 40
  29.2 8.3 %copy-start.17 = (f32[1,8]{1,0:T(1,128)S(1)}, f32[1,8]{1,0:T(1,128)}, u32[]{:S(2)}) copy-start(f32[1,8]{1,0:T(1,128)} %refs_10_.1) | copy-start | bytes 100
  29.2 10.2 %collective-permute-start.4 = (bf16[4,128,256]{2,1,0:T(8,128)(2,1)S(1)}, bf16[4,128,256]{2,1,0:T(8,128)(2,1)S(1)}, u32[]{:S(2)}, u32[]{:S(2)}) collective-permute-start(bf16[4,128,256]{2,1,0:T(8,128)(2,1)S(1)} %get-tuple-element.33), channel_id=1, source_target_pairs={{0,1},{1,0},{2,3},{3,2},{4,5},{5,4},{6,7},{7,6},{8,9},{9,8},{10,11... | collective-permute-start | bytes 786440 | tf_op jit(solution)/shard_map/ppermute | solution.py:367
  29.3 8.1 %copy-start.6 = (bf16[1,8,128,256]{3,2,1,0:T(8,128)(2,1)}, bf16[1,8,128,256]{3,2,1,0:T(8,128)(2,1)S(1)}, u32[]{:S(2)}) copy-start(bf16[1,8,128,256]{3,2,1,0:T(8,128)(2,1)S(1)} %collective-permute-done.got_in.cur_in) | copy-start | bytes 1572868
  29.4 11.7 %collective-permute-start.5 = (bf16[4,128,256]{2,1,0:T(8,128)(2,1)S(1)}, bf16[4,128,256]{2,1,0:T(8,128)(2,1)S(1)}, u32[]{:S(2)}, u32[]{:S(2)}) collective-permute-start(bf16[4,128,256]{2,1,0:T(8,128)(2,1)S(1)} %get-tuple-element.34), channel_id=1, source_target_pairs={{1,2},{3,4},{5,6},{7,8},{9,10},{11,12},{13,14},{2,1},{4,3},{6,5},{... | collective-permute-start | bytes 786440 | tf_op jit(solution)/shard_map/ppermute | solution.py:367
  35.5 2.0 %copy-start.8 = (bf16[1,8,128,256]{3,2,1,0:T(8,128)(2,1)}, bf16[1,8,128,256]{3,2,1,0:T(8,128)(2,1)S(1)}, u32[]{:S(2)}) copy-start(bf16[1,8,128,256]{3,2,1,0:T(8,128)(2,1)S(1)} %collective-permute-done.1.got_x.cur_x) | copy-start | bytes 1572868
  37.5 3.5 %copy-start.7 = (bf16[1,8,128,256]{3,2,1,0:T(8,128)(2,1)S(1)}, bf16[1,8,128,256]{3,2,1,0:T(8,128)(2,1)}, u32[]{:S(2)}) copy-start(bf16[1,8,128,256]{3,2,1,0:T(8,128)(2,1)} %copy-done.6) | copy-start | bytes 1572868
  37.5 3.5 %copy-start.9 = (bf16[1,8,128,256]{3,2,1,0:T(8,128)(2,1)S(1)}, bf16[1,8,128,256]{3,2,1,0:T(8,128)(2,1)}, u32[]{:S(2)}) copy-start(bf16[1,8,128,256]{3,2,1,0:T(8,128)(2,1)} %copy-done.8) | copy-start | bytes 1572868
  41.0 10.1 %copy-start.21 = (s32[1,1,64,1]{2,3,1,0:T(1,128)S(1)}, s32[1,1,64,1]{2,3,1,0:T(1,128)}, u32[]{:S(2)}) copy-start(s32[1,1,64,1]{2,3,1,0:T(1,128)} %param.25) | copy-start | bytes 772
  41.0 11.6 %copy-start.20 = (s32[1,1,64,3]{2,1,3,0:T(1,128)S(1)}, s32[1,1,64,3]{2,1,3,0:T(1,128)}, u32[]{:S(2)}) copy-start(s32[1,1,64,3]{2,1,3,0:T(1,128)} %param.23) | copy-start | bytes 2308
  44.0 1.4 %copy-start = (f32[16,128,256]{2,1,0:T(8,128)}, f32[16,128,256]{2,1,0:T(8,128)S(1)}, u32[]{:S(2)}) copy-start(f32[16,128,256]{2,1,0:T(8,128)S(1)} %get-tuple-element.42.refs_8_) | copy-start | bytes 6291460
  45.3 13.3 %collective-permute-start.6 = (bf16[9,128,256]{2,1,0:T(8,128)(2,1)}, bf16[9,128,256]{2,1,0:T(8,128)(2,1)}, u32[]{:S(2)}, u32[]{:S(2)}) collective-permute-start(bf16[9,128,256]{2,1,0:T(8,128)(2,1)} %get-tuple-element.40), channel_id=1, source_target_pairs={{0,1},{1,0},{2,3},{3,2},{4,5},{5,4},{6,7},{7,6},{8,9},{9,8},{10,11... | collective-permute-start | bytes 1769480 | tf_op jit(solution)/shard_map/ppermute | solution.py:367
  45.3 15.1 %collective-permute-start.7 = (bf16[9,128,256]{2,1,0:T(8,128)(2,1)}, bf16[9,128,256]{2,1,0:T(8,128)(2,1)}, u32[]{:S(2)}, u32[]{:S(2)}) collective-permute-start(bf16[9,128,256]{2,1,0:T(8,128)(2,1)} %get-tuple-element.41), channel_id=1, source_target_pairs={{1,2},{3,4},{5,6},{7,8},{9,10},{11,12},{13,14},{2,1},{4,3},{6,5},{... | collective-permute-start | bytes 1769480 | tf_op jit(solution)/shard_map/ppermute | solution.py:367
  53.3 0.8 copy-start.12
  55.1 1.6 %copy-start.1 = (f32[16,128,256]{2,1,0:T(8,128)S(1)}, f32[16,128,256]{2,1,0:T(8,128)}, u32[]{:S(2)}) copy-start(f32[16,128,256]{2,1,0:T(8,128)} %copy-done) | copy-start | bytes 6291460
  56.7 3.8 %copy-start.2 = (f32[16,128,256]{2,1,0:T(8,128)S(1)}, f32[16,128,256]{2,1,0:T(8,128)}, u32[]{:S(2)}) copy-start(f32[16,128,256]{2,1,0:T(8,128)} %copy-done) | copy-start | bytes 6291460
  64.5 7.9 %collective-permute-start.8 = (bf16[9,128,256]{2,1,0:T(8,128)(2,1)S(1)}, bf16[9,128,256]{2,1,0:T(8,128)(2,1)S(1)}, u32[]{:S(2)}, u32[]{:S(2)}) collective-permute-start(bf16[9,128,256]{2,1,0:T(8,128)(2,1)S(1)} %get-tuple-element.46), channel_id=1, source_target_pairs={{0,1},{1,0},{2,3},{3,2},{4,5},{5,4},{6,7},{7,6},{8,9},{9,8},{10,11... | collective-permute-start | bytes 1769480 | tf_op jit(solution)/shard_map/ppermute | solution.py:367
  64.6 14.8 %collective-permute-start.9 = (bf16[9,128,256]{2,1,0:T(8,128)(2,1)S(1)}, bf16[9,128,256]{2,1,0:T(8,128)(2,1)S(1)}, u32[]{:S(2)}, u32[]{:S(2)}) collective-permute-start(bf16[9,128,256]{2,1,0:T(8,128)(2,1)S(1)} %get-tuple-element.47), channel_id=1, source_target_pairs={{1,2},{3,4},{5,6},{7,8},{9,10},{11,12},{13,14},{2,1},{4,3},{6,5},{... | collective-permute-start | bytes 1769480 | tf_op jit(solution)/shard_map/ppermute | solution.py:367
  82.6 7.7 %collective-permute-start.10 = (bf16[9,128,256]{2,1,0:T(8,128)(2,1)S(1)}, bf16[9,128,256]{2,1,0:T(8,128)(2,1)S(1)}, u32[]{:S(2)}, u32[]{:S(2)}) collective-permute-start(bf16[9,128,256]{2,1,0:T(8,128)(2,1)S(1)} %get-tuple-element.55), channel_id=1, source_target_pairs={{0,1},{1,0},{2,3},{3,2},{4,5},{5,4},{6,7},{7,6},{8,9},{9,8},{10,11... | collective-permute-start | bytes 1769480 | tf_op jit(solution)/shard_map/ppermute | solution.py:367
  82.6 14.8 %collective-permute-start.11 = (bf16[9,128,256]{2,1,0:T(8,128)(2,1)S(1)}, bf16[9,128,256]{2,1,0:T(8,128)(2,1)S(1)}, u32[]{:S(2)}, u32[]{:S(2)}) collective-permute-start(bf16[9,128,256]{2,1,0:T(8,128)(2,1)S(1)} %get-tuple-element.56), channel_id=1, source_target_pairs={{1,2},{3,4},{5,6},{7,8},{9,10},{11,12},{13,14},{2,1},{4,3},{6,5},{... | collective-permute-start | bytes 1769480 | tf_op jit(solution)/shard_map/ppermute | solution.py:367

commit v2 on v1

v2 whole, which is shorter than its diff:
```python
import jax
import jax.numpy as jnp
import numpy as np
from jax import lax
from jax.experimental import pallas as pl
from jax.experimental.pallas import tpu as pltpu
from jax.sharding import PartitionSpec as P

STEPS = 8
CAPR = 16
PL = 8
ROWS = 128
COLS = 256
EDGE = 64
SLOTS = 64
SCALE = 5040.0
TAPS = (8064.0, -1008.0, 128.0, -9.0)
CENTRE_COLS = -43008.0
CENTRE_ROWS = -42.0
COURANT = 0.09
PACK_LIMIT = 56

VMEM = pl.BlockSpec(memory_space=pltpu.VMEM)
SMEM = pl.BlockSpec(memory_space=pltpu.SMEM)
HBM = pl.BlockSpec(memory_space=pltpu.HBM)
f32 = jnp.float32
bf16 = jnp.bfloat16


def band_matrix(size, centre):
    gap = np.abs(np.arange(size)[:, None] - np.arange(size)[None, :])
    out = np.where(gap == 0, centre, 0.0)
    for k in range(1, 5):
        out = np.where(gap == k, TAPS[k - 1], out)
    return out


def constants():
    cols = band_matrix(COLS, CENTRE_COLS)
    rows = band_matrix(ROWS, CENTRE_ROWS)
    return (
        jnp.asarray(np.concatenate([cols, cols], 0), bf16),
        jnp.asarray(np.concatenate([rows, rows], 1), bf16),
    )


def call(body, outs, ins, scratch=(), limit=None, cost=None, alias=None):
    return pl.pallas_call(
        body,
        out_shape=[jax.ShapeDtypeStruct(s, d) for s, d in outs],
        in_specs=ins,
        out_specs=[VMEM] * len(outs),
        scratch_shapes=list(scratch),
        input_output_aliases=alias or {},
        compiler_params=pltpu.CompilerParams(vmem_limit_bytes=limit),
        cost_estimate=pl.CostEstimate(flops=cost[0], bytes_accessed=cost[1], transcendentals=0) if cost else None,
    )


def is_even():
    return lax.rem(lax.axis_index("space"), 2) == 0


def mirrored4(even, plane):
    return jnp.where(even, plane, 3 - plane)


def mirrored(even, plane):
    return jnp.where(even, plane, PL - 1 - plane)


def pack_kernel(home_hbm, wanted_hbm, store_hbm, out, home, wanted, store, sems):
    copies = [
        pltpu.make_async_copy(src, dst, sems.at[i])
        for i, (src, dst) in enumerate(((home_hbm, home), (wanted_hbm, wanted), (store_hbm, store)))
    ]
    for copy in copies:
        copy.start()
    copies[0].wait()
    copies[1].wait()
    me = lax.axis_index("shot")
    even = is_even()
    chosen = []
    for s in range(8):
        count = jnp.int32(0)
        slots = [jnp.int32(0), jnp.int32(0)]
        for j in range(8):
            row = home[wanted[s, j]]
            mine = lax.shift_right_logical(row, 3) == me
            for rank in range(2):
                slots[rank] = jnp.where(mine & (count == rank), row & 7, slots[rank])
            count = count + mine.astype(jnp.int32)
        chosen.append(slots)
    copies[2].wait()
    for s in range(8):
        for q in range(PL):
            p = mirrored(even, q)
            out[s, q] = jnp.concatenate([store[chosen[s][0], p], store[chosen[s][1], p]], 1)


def swapped(x):
    return jnp.concatenate([x[:, EDGE:], x[:, :EDGE]], 1)


def assemble_kernel(home, wanted, arrived, v_x, v_in):
    left = lax.broadcasted_iota(jnp.int32, (EDGE, 2 * EDGE), 1) < EDGE
    me = lax.axis_index("shot")
    owners = []
    ranks = []
    for j in range(8):
        owners.append(lax.shift_right_logical(home[wanted[me, j]], 3))
        rank = jnp.int32(0)
        for i in range(j):
            rank = rank + (owners[i] == owners[j]).astype(jnp.int32)
        ranks.append(rank)
    for j in range(0, 8, 2):
        rows = slice(j // 4 * EDGE, (j // 4 + 1) * EDGE)
        lanes = slice(j % 4 * EDGE, (j % 4 + 2) * EDGE)
        for q in range(PL):
            x = arrived[owners[j], q]
            y = arrived[owners[j + 1], q]
            x = jnp.where(ranks[j] == 0, x, swapped(x))
            y = jnp.where(ranks[j + 1] == 0, swapped(y), y)
            out = v_x if q < 4 else v_in
            out[q % 4, rows, lanes] = jnp.where(left, x, y)


CHUNK = 16


def product(weights, across, u):
    hi = u.astype(bf16)
    lo = (u - hi.astype(f32)).astype(bf16)
    return jnp.dot(
        jnp.concatenate([hi, lo, across[...]], 1),
        jnp.concatenate([weights[...], hi, lo], 0),
        preferred_element_type=f32,
    )


def chunks():
    return [slice(r, r + CHUNK) for r in range(0, ROWS, CHUNK)]


def depth(get, e, low, high, r, acc):
    for k in range(1, 5):
        parts = [get(p, r) for p in (e + k, e - k) if low <= p < high]
        if parts:
            acc = acc + TAPS[k - 1] * sum(parts[1:], parts[0])
    return acc


def hat(frac):
    share = frac.astype(f32) * 0.125
    return 1.0 - share, share


def add_source(parts, even, cell, frac, pulse):
    lane = lax.broadcasted_iota(jnp.int32, (1, COLS), 1)
    wd, wr, wc = hat(frac[0, 0]), hat(frac[0, 1]), hat(frac[0, 2])
    column = jnp.where(lane == cell[0, 2], wc[0], 0.0) + jnp.where(lane == cell[0, 2] + 1, wc[1], 0.0)
    for dp in range(2):
        plane = mirrored(even, cell[0, 0] + dp - lax.axis_index("space") * PL)
        for ref, first, down in parts:
            at = first - plane if down else plane - first

            @pl.when((at >= 0) & (at < ref.shape[0]))
            def _():
                for dr in range(2):
                    row = pl.ds(cell[0, 1] + dr, 1)
                    ref[at, row, :] = ref[at, row, :] + pulse * (wd[dp] * wr[dr] * column)


GROUP = 8


def sample(fields, codes, count, spread, place, owner, rows, out):
    even = is_even()

    def group(g, _):
        for j in range(GROUP):
            r = g * GROUP + j
            code = codes[r]
            wr = hat(code & 7)
            wd = hat(lax.shift_right_logical(code, 3) & 7)
            y = lax.shift_right_logical(code, 6) & 127
            p = lax.shift_right_logical(code, 13)
            for f, (src, mirror, _) in enumerate(fields):
                acc = None
                for dp in range(2):
                    plane = mirrored(even, p + dp) if mirror else p + dp
                    for dr in range(2):
                        term = (wd[dp] * wr[dr]) * src[plane, pl.ds(y + dr, 1), :]
                        acc = term if acc is None else acc + term
                rows[f, pl.ds(r, 1), :] = acc
        return 0

    lax.fori_loop(0, lax.div(count[0, 0] + GROUP - 1, GROUP), group, 0)
    live = lax.broadcasted_iota(jnp.int32, (SLOTS, 1), 0) < count[0, 0]
    for f, (_, _, n) in enumerate(fields):
        values = jnp.where(live, jnp.sum(rows[f] * spread[...], axis=1, keepdims=True), 0.0)
        placed = values * place[...]
        for q in range(8):
            out[q, n : n + 1, :] = jnp.sum(jnp.where(owner[0, 0] == q, placed, 0.0), axis=0, keepdims=True)


def receiver_kernel(cells, fracs, count, owner, spread, place):
    lane = lax.broadcasted_iota(jnp.int32, (SLOTS, COLS), 1)
    share = fracs[0, 0, :, 2:3].astype(f32) * 0.125
    at = cells[0, 0, :, 2:3]
    spread[...] = jnp.where(lane == at, 1.0 - share, 0.0) + jnp.where(lane == at + 1, share, 0.0)
    me = lax.axis_index("shot")
    slot = lax.broadcasted_iota(jnp.int32, (SLOTS, 1), 0)
    live = slot < count[0, 0]
    group = lax.broadcasted_iota(jnp.int32, (SLOTS, 128), 1)
    chosen = jnp.where((owner[0, 0] == group) & live, 1.0, 0.0)
    earlier = jnp.where(
        lax.broadcasted_iota(jnp.int32, (SLOTS, SLOTS), 1) < lax.broadcasted_iota(jnp.int32, (SLOTS, SLOTS), 0), 1.0, 0.0
    )
    before = jnp.dot(earlier.astype(bf16), chosen.astype(bf16), preferred_element_type=f32)
    rank = jnp.sum(before * chosen, axis=1, keepdims=True).astype(jnp.int32)
    place[...] = jnp.where((group == rank + me * CAPR) & live, 1.0, 0.0)


def factor(x):
    scaled = x.astype(f32) * COURANT
    return scaled * scaled * (1.0 / SCALE)


def near_kernel(
    weights, across, cell, frac, pulses, cur, cur_x, cur_in, pri, pri_x, pri_in, own_v_x, own_v_in, v_in,
    coef, coef_in, own, inner, base, outer_lead, outer_sum, halo_x, halo_in,
):
    even = is_even()
    for j in range(PL):
        halo_in[j] = cur_in[0, mirrored(even, j)].astype(f32)
        halo_x[j] = cur_x[0, mirrored(even, PL - 1 - j)].astype(f32)
        base[j] = cur[0, mirrored(even, j)].astype(f32)

    def now(e, r):
        return halo_x[-1 - e, r] if e < 0 else (base[e, r] if e < PL else halo_in[e - PL, r])

    whole = slice(0, ROWS)
    for e in range(-4, 12):
        m = product(weights, across, now(e, whole))
        j = -1 - e if e < 0 else (e if e < PL else e - PL)
        for r in chunks():
            acc = depth(now, e, -8, 16, r, m[r])
            if e < 0:
                outer_sum[j, r] = acc
                outer_lead[j, r] = 2.0 * now(e, r) - pri_x[mirrored4(even, 3 - j), r].astype(f32)
            elif e < PL:
                c = factor((own_v_x if e < 4 else own_v_in)[e % 4, r])
                coef[e, r] = c
                own[e, r] = 2.0 * now(e, r) - pri[0, mirrored(even, e), r].astype(f32) + c * acc
            else:
                c = factor(v_in[3 - j, r])
                coef_in[j, r] = c
                inner[j, r] = 2.0 * now(e, r) - pri_in[mirrored4(even, j), r].astype(f32) + c * acc
    add_source(((own, 0, False), (inner, PL, False)), even, cell, frac, pulses[0, 0])
    for q in range(PL):
        m = product(weights, across, own[q])
        for r in chunks():
            acc = depth(lambda e, r: own[e, r] if e < PL else inner[e - PL, r], q, 0, 12, r, m[r])
            base[q, r] = 2.0 * own[q, r] - base[q, r] + coef[q, r] * acc


def pack_send(u, send_x, send_in):
    for q in range(PL):
        hi = u[q].astype(bf16)
        send_x[q] = hi
        send_in[q] = hi
    for ref, near in ((send_x, 0), (send_in, PL - 1)):
        edge = u[near]
        ref[PL] = (edge - edge.astype(bf16).astype(f32)).astype(bf16)


def far_kernel(
    cell, frac, pulses, outer_lead, outer_sum, v_x, base, coef,
    coef_x, outer, last, send_x, send_in,
):
    even = is_even()
    for j in range(4):
        for r in chunks():
            c = factor(v_x[j, r])
            coef_x[j, r] = c
            outer[j, r] = outer_lead[j, r] + c * outer_sum[j, r]
    add_source(((outer, -1, True),), even, cell, frac, pulses[0, 0])
    for q in range(PL):
        for r in chunks():
            x = base[q, r]
            if q < 4:
                x = x + coef[q, r] * depth(lambda e, r: outer[-1 - e, r], q, -4, 0, r, 0.0)
            last[q, r] = x
    add_source(((last, 0, False),), even, cell, frac, pulses[0, 1])
    pack_send(last, send_x, send_in)


def during_kernel(
    step, weights, across, cell, frac, pulses, codes, count, owner, spread, place, u, prev, prev_in, coef, coef_in, got_in,
    part, own_hi, inner, base, gath, halo, rows,
):
    even = is_even()
    for j in range(PL):
        x = got_in[PL - 1 - j].astype(f32)
        halo[j] = x + got_in[PL].astype(f32) if j == 0 else x

    def now(e, r):
        return u[e, r] if e < PL else halo[e - PL, r]

    whole = slice(0, ROWS)
    for e in range(12):
        m = product(weights, across, now(e, whole))
        for r in chunks():
            acc = depth(now, e, 0, 16, r, m[r])
            if e < PL:
                x = 2.0 * u[e, r] - prev[e, r] + coef[e, r] * acc
                if e < 4:
                    part[e, r] = x
                else:
                    own_hi[e - 4, r] = x
            else:
                inner[e - PL, r] = 2.0 * now(e, r) - prev_in[e - PL, r] + coef_in[e - PL, r] * acc
    add_source(((own_hi, 4, False), (inner, PL, False)), even, cell, frac, pulses[0, step])
    for q in range(4, PL):
        m = product(weights, across, own_hi[q - 4])
        for r in chunks():
            acc = depth(lambda e, r: own_hi[e - 4, r] if e < PL else inner[e - PL, r], q, 4, 12, r, m[r])
            base[q - 4, r] = 2.0 * own_hi[q - 4, r] - u[q, r] + coef[q, r] * acc
    sample(((prev, True, 0), (u, True, 1)), codes, count, spread, place, owner, rows, gath)


def after_kernel(
    step, weights, across, cell, frac, pulses, u, prev, prev_x, coef, coef_x, got_x, part, own_hi, base,
    own, outer, last, halo, place_of,
):
    even = is_even()
    for j in range(PL):
        x = got_x[j].astype(f32)
        halo[j] = x + got_x[PL].astype(f32) if j == 0 else x

    def now(e, r):
        return halo[-1 - e, r] if e < 0 else u[e, r]

    whole = slice(0, ROWS)
    for e in range(-4, 0):
        j = -1 - e
        m = product(weights, across, halo[j])
        for r in chunks():
            acc = depth(now, e, -8, 8, r, m[r])
            outer[j, r] = 2.0 * halo[j, r] - prev_x[j, r] + coef_x[j, r] * acc
    for q in range(4):
        for r in chunks():
            own[q, r] = part[q, r] + coef[q, r] * depth(now, q, -8, 0, r, 0.0)
            own[q + 4, r] = own_hi[q, r]
    add_source(((outer, -1, True), (own.at[pl.ds(0, 4)], 0, False)), even, cell, frac, pulses[0, step])

    def following(e, r):
        return outer[-1 - e, r] if e < 0 else own[e, r]

    for q in range(4):
        m = product(weights, across, own[q])
        for r in chunks():
            acc = depth(following, q, -4, 8, r, m[r])
            last[place_of(q), r] = 2.0 * own[q, r] - u[q, r] + coef[q, r] * acc
    for q in range(4, PL):
        for r in chunks():
            last[place_of(q), r] = base[q - 4, r] + coef[q, r] * depth(following, q, 0, 4, r, 0.0)


def middle_kernel(step, *refs):
    (own, outer, last, send_x, send_in, halo), ins = refs[-6:], refs[:-6]
    after_kernel(step, *ins, own, outer, last, halo, lambda q: q)
    cell, frac, pulses = ins[2:5]
    add_source(((last, 0, False),), is_even(), cell, frac, pulses[0, step + 1])
    pack_send(last, send_x, send_in)


def last_kernel(step, codes, count, owner, spread, place, gath_a, gath_b, gath_c, *refs):
    (final, gath, own, outer, halo, rows), ins = refs[-6:], refs[:-6]
    even = is_even()
    last = final.at[0]
    after_kernel(step, *ins, own, outer, last, halo, lambda q: mirrored(even, q))
    cell, frac, pulses = ins[2:5]
    add_source(((last, 0, False),), True, cell, frac, pulses[0, step + 1])
    for i, some in enumerate((gath_a, gath_b, gath_c)):
        gath[:, 2 * i : 2 * i + 2, :] = some[...]
    sample(((own, True, step), (last, False, step + 1)), codes, count, spread, place, owner, rows, gath)


MIB = 1 << 20


def on_device(
    prior_field, current_field, model_store, tile_home, aperture, source_cell, source_frac,
    wavelet, receiver_cell, receiver_frac, receiver_count, trace_owner,
):
    size = lax.axis_size("space")
    pair_in = [(i, i ^ 1) for i in range(size)]
    pair_x = [(i, i + 1) for i in range(1, size - 1, 2)] + [(i + 1, i) for i in range(1, size - 1, 2)]

    def swap(across_chips, in_chip):
        return lax.ppermute(across_chips, "space", pair_x), lax.ppermute(in_chip, "space", pair_in)

    weights, across = constants()
    plane = (ROWS, COLS)
    four = ((4,) + plane, f32)
    eight = ((PL,) + plane, f32)
    tile_planes = ((4,) + plane, bf16)
    send = ((PL + 1,) + plane, bf16)
    scratch8 = pltpu.VMEM(*eight)
    rows = pltpu.VMEM((2, SLOTS, COLS), f32)

    out = call(
        pack_kernel, [((8, PL, EDGE, 2 * EDGE), bf16)], [HBM] * 3,
        [pltpu.SMEM((64,), jnp.int32), pltpu.SMEM((8, 8), jnp.int32), pltpu.VMEM((8, PL, EDGE, EDGE), bf16),
         pltpu.SemaphoreType.DMA((3,))],
        limit=PACK_LIMIT * MIB,
    )(tile_home, aperture, model_store)[0]
    arrived = lax.all_to_all(out, "shot", split_axis=0, concat_axis=0, tiled=True)
    cur_x, cur_in = swap(current_field, current_field)
    prior = prior_field[0]
    first = jnp.where(is_even(), 0, 4)
    pri_x, pri_in = swap(
        lax.dynamic_slice_in_dim(prior, first, 4, 0), lax.dynamic_slice_in_dim(prior, 4 - first, 4, 0)
    )
    spread, place = call(
        receiver_kernel, [((SLOTS, COLS), f32), ((SLOTS, 128), f32)], [VMEM, VMEM, SMEM, VMEM], limit=4 * MIB
    )(receiver_cell, receiver_frac, receiver_count, trace_owner)
    cells, fracs = receiver_cell[0, 0], receiver_frac[0, 0]
    codes = ((cells[:, 0] * ROWS + cells[:, 1]) * 8 + fracs[:, 0]) * 8 + fracs[:, 1]
    arrived, spread, place, codes = lax.optimization_barrier((arrived, spread, place, codes))
    own_v_x, own_v_in = call(
        assemble_kernel, [tile_planes, tile_planes], [SMEM, SMEM, VMEM], limit=8 * MIB
    )(tile_home, aperture, arrived)
    v_x, v_in = swap(own_v_x, own_v_in)
    source = (source_cell, source_frac, wavelet)
    source_specs = [SMEM] * 3
    receivers = (codes, receiver_count, trace_owner, spread, place)
    receiver_specs = [SMEM, SMEM, VMEM, VMEM, VMEM]
    coef, coef_in, prev, prev_in, base, lead, total = call(
        near_kernel, [eight, four, eight, four, eight, four, four], [VMEM] * 2 + source_specs + [VMEM] * 9,
        [scratch8, scratch8], limit=16 * MIB,
    )(weights, across, *source, current_field, cur_x, cur_in, prior_field, pri_x, pri_in, own_v_x, own_v_in, v_in)
    coef_x, prev_x, u, send_x, send_in = call(
        far_kernel, [four, four, eight, send, send], source_specs + [VMEM] * 5, limit=16 * MIB
    )(*source, lead, total, v_x, base, coef)
    gaths = []
    for n in (2, 4, 6):
        got_x, got_in = swap(send_x, send_in)
        part, own_hi, inner, base, gath = call(
            lambda *refs, n=n: during_kernel(n, *refs), [four, four, four, four, ((8, 2, 128), f32)],
            [VMEM] * 2 + source_specs + receiver_specs + [VMEM] * 6, [scratch8, rows], limit=16 * MIB,
        )(weights, across, *source, *receivers, u, prev, prev_in, coef, coef_in, got_in)
        gaths.append(gath)
        common = (weights, across, *source, u, prev, prev_x, coef, coef_x, got_x, part, own_hi, base)
        common_specs = [VMEM] * 2 + source_specs + [VMEM] * 9
        if n < 6:
            prev, prev_x, u, send_x, send_in = call(
                lambda *refs, n=n: middle_kernel(n, *refs), [eight, four, eight, send, send], common_specs, [scratch8], limit=16 * MIB
            )(*common)
            prev_in = inner
        else:
            final, gath = call(
                lambda *refs, n=n: last_kernel(n, *refs), [((1, PL) + plane, f32), ((8, STEPS, 128), f32)],
                receiver_specs + [VMEM] * 3 + common_specs, [scratch8, pltpu.VMEM(*four), scratch8, rows], limit=20 * MIB,
            )(*receivers, *gaths, *common)
    back = lax.all_to_all(gath, "shot", split_axis=0, concat_axis=0, tiled=True)
    return final, jnp.sum(back, axis=0)[None, None]


def solution(mesh):
    placed = (
        P("shot", "space", None, None),
        P("shot", "space", None, None),
        P("shot", "space", None, None),
        P(),
        P(),
        P("shot", None),
        P("shot", None),
        P("shot", None),
        P("shot", "space", None, None),
        P("shot", "space", None, None),
        P("shot", "space"),
        P("shot", "space", None, None),
    )
    return jax.shard_map(
        on_device,
        mesh=mesh,
        in_specs=placed,
        out_specs=(P("shot", "space", None, None), P("shot", "space", None, None)),
        check_vma=False,
    )
```

time: 115 us -> 104 us (0.904)
  waiting for transfers between devices: 24 us -> 18.9 us
  local copies, waits for them, and re-layouts: 8.66 us -> 4.55 us
  Pallas kernels: 29.4 us -> 26.7 us
    all_to_all x1, waiting for transfers between devices: 6.41 us -> 1.16 us  [on_device(): lax.all_to_all(out, 'shot', split_axis=0, concat_axis=0, tiled=True)]
    unnamed x48 -> x32, local copies, waits for them, and re-layouts: 8.66 us -> 3.72 us
    pallas_call x10 -> x9, Pallas kernels: 26.9 us -> 23.8 us  [the longest x3 10.3 us: on_device(): call(lambda *refs, n=n: during_kernel(n, *refs), [four, four, four, four,...]
  transfers between devices with their start and end apart: 13 -> 13, of which waited for: 5 -> 5; matrix products, arithmetic and copies ran while one was open for 2% -> 2% of each run, Pallas kernels for 11% -> 15%
where the time goes in v2:
time: 104 us; the launch traced here: 103 us
  starting transfers between devices  38.8 us (37%)
  Pallas kernels  26.7 us (26%)
  waiting for transfers between devices  18.9 us (18%)
  blocking collectives  11.8 us (11%)
  local copies, waits for them, and re-layouts  4.55 us (4%)
  between operations  1.64 us (2%)
    ppermute x6, starting transfers between devices, swap(): lax.ppermute(across_chips, 'space', pair_x)  32.8 us
    ppermute x6, waiting for transfers between devices, swap(): lax.ppermute(across_chips, 'space', pair_x)  17.8 us
    all_to_all x1, blocking collectives, on_device(): back = lax.all_to_all(gath, 'shot', split_axis=0, concat_axis=0, tiled=True)  11.8 us
    pallas_call x3, Pallas kernels, on_device(): call(lambda *refs, n=n: during_kernel(n, *refs), [four, four, four, four,...  10.3 us
    all_to_all x1, starting transfers between devices, on_device(): lax.all_to_all(out, 'shot', split_axis=0, concat_axis=0, tiled=True)  5.16 us
    pallas_call x2, Pallas kernels, on_device(): call(lambda *refs, n=n: middle_kernel(n, *refs), [eight, four, eight, sen...  4.21 us
    pallas_call x1, Pallas kernels, on_device(): call(near_kernel, [eight, four, eight, four, eight, four, four], [VMEM] *...  4.17 us
    unnamed x32, local copies, waits for them, and re-layouts  3.72 us
  transfers between devices with their start and end apart: 13, of which 5 were waited for; matrix products, arithmetic and copies ran while one was open for 2% of the time, Pallas kernels for 15%

profile of v2, /device:TPU:16, one launch (start us, length us, event | category | flops | bytes accessed | tf_op | source)
XLA Modules:
  0.0 103.0 jit_solution(1029243836474325036)
XLA Ops:
  0.6 2.6 %shard_map.149 = bf16[8,8,64,128]{3,2,1,0:T(8,128)(2,1)} custom-call(s32[64]{0:T(128)} %home.1, s32[8,8]{1,0:T(8,128)} %wanted.1, bf16[8,8,64,64]{3,2,1,0:T(8,128)(2,1)} %store_hbm.1), custom_call_target="tpu_custom_call" | custom-call | tf_op jit(solution)/shard_map/pallas_call | solution.py:414
  3.2 0.0 copy-start.3
  3.2 0.0 copy-start.2
  3.2 5.2 %all-to-all-start = ((bf16[8,8,64,128]{3,2,1,0:T(8,128)(2,1)}), bf16[8,8,64,128]{3,2,1,0:T(8,128)(2,1)S(1)}, u32[]{:S(2)}, u32[]{:S(2)}) async-start(bf16[8,8,64,128]{3,2,1,0:T(8,128)(2,1)} %shard_map.149), calls=%async_computation | async-start | bytes 2097152 | tf_op jit(solution)/shard_map/all_to_all | solution.py:420
  8.4 0.0 copy-done.3
  8.4 5.2 %collective-permute-start = (bf16[1,8,128,256]{3,2,1,0:T(8,128)(2,1)S(1)}, bf16[1,8,128,256]{3,2,1,0:T(8,128)(2,1)S(1)}, u32[]{:S(2)}, u32[]{:S(2)}) collective-permute-start(bf16[1,8,128,256]{3,2,1,0:T(8,128)(2,1)S(1)} %copy-done.3), channel_id=1, source_target_pairs={{1,2},{3,4},{5,6},{7,8},{9,10},{11,12},{13,14},{2,1},{4,3},{6,5},{... | collective-permute-start | bytes 1572872 | tf_op jit(solution)/shard_map/ppermute | solution.py:403
  13.6 0.1 collective-permute-start.1
  13.7 0.0 copy-done.2
  13.7 0.8 dynamic-slice_bitcast_fusion
  14.5 0.0 copy-start.11
  14.5 0.5 collective-permute-start.3
  15.0 4.0 %collective-permute-start.2 = (bf16[4,128,256]{2,1,0:T(8,128)(2,1)}, bf16[4,128,256]{2,1,0:T(8,128)(2,1)}, u32[]{:S(2)}, u32[]{:S(2)}) collective-permute-start(bf16[4,128,256]{2,1,0:T(8,128)(2,1)} %get-tuple-element.95), channel_id=1, source_target_pairs={{1,2},{3,4},{5,6},{7,8},{9,10},{11,12},{13,14},{2,1},{4,3},{6,5},{... | collective-permute-start | bytes 786440 | tf_op jit(solution)/shard_map/ppermute | solution.py:403
  19.0 0.0 copy-done.11
  19.0 0.0 copy-done.12
  19.0 0.7 copy.16.cells
  19.7 0.7 copy.17.fracs
  21.1 0.0 copy-done.13
  21.1 0.1 copy.18.owner.refs_7_.refs_2_
  21.2 0.8 copy-done.4
  22.0 0.8 copy-done.5
  22.7 0.3 shard_map.150
  23.0 0.0 copy-start.9
  23.0 1.2 %all-to-all-done.arrived = bf16[8,8,64,128]{3,2,1,0:T(8,128)(2,1)S(1)} async-done(((bf16[8,8,64,128]{3,2,1,0:T(8,128)(2,1)}), bf16[8,8,64,128]{3,2,1,0:T(8,128)(2,1)S(1)}, u32[]{:S(2)}, u32[]{:S(2)}) %all-to-all-start) | async-done | bytes 1048608 | tf_op jit(solution)/shard_map/all_to_all | solution.py:420
  24.2 0.0 copy-done.9
  24.2 0.7 copy-done.10
  24.9 0.9 shard_map.151
  25.8 0.0 copy-start.6
  25.8 0.0 copy-start.7
  25.8 0.0 copy-start.8
  25.8 0.1 collective-permute-start.4
  25.9 0.0 collective-permute-done.3.pri_in
  25.9 6.1 %collective-permute-start.5 = (bf16[4,128,256]{2,1,0:T(8,128)(2,1)S(1)}, bf16[4,128,256]{2,1,0:T(8,128)(2,1)S(1)}, u32[]{:S(2)}, u32[]{:S(2)}) collective-permute-start(bf16[4,128,256]{2,1,0:T(8,128)(2,1)S(1)} %get-tuple-element.54.own_v_x), channel_id=1, source_target_pairs={{1,2},{3,4},{5,6},{7,8},{9,10},{11,12},{13,14},{2,1},{4,3},{6,5},{... | collective-permute-start | bytes 786440 | tf_op jit(solution)/shard_map/ppermute | solution.py:403
  32.0 1.2 %collective-permute-done.2.pri_x = bf16[4,128,256]{2,1,0:T(8,128)(2,1)} collective-permute-done((bf16[4,128,256]{2,1,0:T(8,128)(2,1)}, bf16[4,128,256]{2,1,0:T(8,128)(2,1)}, u32[]{:S(2)}, u32[]{:S(2)}) %collective-permute-start.2) | collective-permute-done | bytes 262176 | tf_op jit(solution)/shard_map/ppermute | solution.py:403
  33.2 0.0 collective-permute-done.cur_x
  33.2 0.0 collective-permute-done.1.cur_in
  33.2 0.0 collective-permute-done.4.v_in
  33.2 0.0 copy-done
  33.2 0.0 copy-done.1
  33.2 0.0 copy-done.6
  33.3 0.0 copy-done.7
  33.3 0.0 copy-done.8
  33.3 4.2 %shard_map.152 = (f32[8,128,256]{2,1,0:T(8,128)S(1)}, f32[4,128,256]{2,1,0:T(8,128)S(1)}, f32[8,128,256]{2,1,0:T(8,128)S(1)}, f32[4,128,256]{2,1,0:T(8,128)S(1)}...) custom-call(bf16[512,256]{1,0:T(8,128)(2,1)S(1)} %copy-done, ...), custom_call_target="tpu_custom_call" | custom-call | tf_op jit(solution)/shard_map/pallas_call | solution.py:441
  37.5 0.0 collective-permute-done.5.v_x
  37.5 1.0 shard_map.153
  38.4 0.1 collective-permute-start.6
  38.5 5.8 %collective-permute-start.7 = (bf16[9,128,256]{2,1,0:T(8,128)(2,1)S(1)}, bf16[9,128,256]{2,1,0:T(8,128)(2,1)S(1)}, u32[]{:S(2)}, u32[]{:S(2)}) collective-permute-start(bf16[9,128,256]{2,1,0:T(8,128)(2,1)S(1)} %get-tuple-element.68), channel_id=1, source_target_pairs={{1,2},{3,4},{5,6},{7,8},{9,10},{11,12},{13,14},{2,1},{4,3},{6,5},{... | collective-permute-start | bytes 1769480 | tf_op jit(solution)/shard_map/ppermute | solution.py:403
  44.4 0.0 collective-permute-done.6.refs_15_
  44.4 3.2 %shard_map.154 = (f32[4,128,256]{2,1,0:T(8,128)S(1)}, f32[4,128,256]{2,1,0:T(8,128)S(1)}, f32[4,128,256]{2,1,0:T(8,128)S(1)}, f32[4,128,256]{2,1,0:T(8,128)S(1)}, f32[8,2,128]{2,1,0:T(2,128)S(1)}) custom-call(bf16[512,256]{1,0:T(8,128)(2,1)S(1)} %copy-done, bf16[128,256]{1,0:T(8,128)(2,1)S(1)} %copy-done.1, s32[1,3]{1,0:T(1,128)S(1)} %copy-done.6, ...), custom_call_target="tpu_custom_call" | custom-call | tf_op jit(solution)/shard_map/pallas_call | solution.py:451
  47.6 5.8 %collective-permute-done.7.refs_10_ = bf16[9,128,256]{2,1,0:T(8,128)(2,1)S(1)} collective-permute-done((bf16[9,128,256]{2,1,0:T(8,128)(2,1)S(1)}, bf16[9,128,256]{2,1,0:T(8,128)(2,1)S(1)}, u32[]{:S(2)}, u32[]{:S(2)}) %collective-permute-start.7) | collective-permute-done | bytes 589856 | tf_op jit(solution)/shard_map/ppermute | solution.py:403
  53.4 2.1 %shard_map.155 = (f32[8,128,256]{2,1,0:T(8,128)S(1)}, f32[4,128,256]{2,1,0:T(8,128)S(1)}, f32[8,128,256]{2,1,0:T(8,128)S(1)}, bf16[9,128,256]{2,1,0:T(8,128)(2,1)S(1)}, bf16[9,128,256]{2,1,0:T(8,128)(2,1)S(1)}) custom-call(bf16[512,256]{1,0:T(8,128)(2,1)S(1)} %copy-done, bf16[128,256]{1,0:T(8,128)(2,1)S(1)} %copy-done.1, s32[1,3]{1,0:T(1,128)S(1)} %copy-done.6, ...), custom_call_target="tpu_custom_call" | custom-call | tf_op jit(solution)/shard_map/pallas_call | solution.py:459
  55.5 0.1 collective-permute-start.8
  55.6 5.8 %collective-permute-start.9 = (bf16[9,128,256]{2,1,0:T(8,128)(2,1)S(1)}, bf16[9,128,256]{2,1,0:T(8,128)(2,1)S(1)}, u32[]{:S(2)}, u32[]{:S(2)}) collective-permute-start(bf16[9,128,256]{2,1,0:T(8,128)(2,1)S(1)} %get-tuple-element.78), channel_id=1, source_target_pairs={{1,2},{3,4},{5,6},{7,8},{9,10},{11,12},{13,14},{2,1},{4,3},{6,5},{... | collective-permute-start | bytes 1769480 | tf_op jit(solution)/shard_map/ppermute | solution.py:403
  61.4 0.0 collective-permute-done.8.refs_15_
  61.4 3.4 %shard_map.156 = (f32[4,128,256]{2,1,0:T(8,128)S(1)}, f32[4,128,256]{2,1,0:T(8,128)S(1)}, f32[4,128,256]{2,1,0:T(8,128)S(1)}, f32[4,128,256]{2,1,0:T(8,128)S(1)}, f32[8,2,128]{2,1,0:T(2,128)S(1)}) custom-call(bf16[512,256]{1,0:T(8,128)(2,1)S(1)} %copy-done, bf16[128,256]{1,0:T(8,128)(2,1)S(1)} %copy-done.1, s32[1,3]{1,0:T(1,128)S(1)} %copy-done.6, ...), custom_call_target="tpu_custom_call" | custom-call | tf_op jit(solution)/shard_map/pallas_call | solution.py:451
  64.8 5.6 %collective-permute-done.9.refs_10_ = bf16[9,128,256]{2,1,0:T(8,128)(2,1)S(1)} collective-permute-done((bf16[9,128,256]{2,1,0:T(8,128)(2,1)S(1)}, bf16[9,128,256]{2,1,0:T(8,128)(2,1)S(1)}, u32[]{:S(2)}, u32[]{:S(2)}) %collective-permute-start.9) | collective-permute-done | bytes 589856 | tf_op jit(solution)/shard_map/ppermute | solution.py:403
  70.4 2.1 %shard_map.157 = (f32[8,128,256]{2,1,0:T(8,128)S(1)}, f32[4,128,256]{2,1,0:T(8,128)S(1)}, f32[8,128,256]{2,1,0:T(8,128)S(1)}, bf16[9,128,256]{2,1,0:T(8,128)(2,1)S(1)}, bf16[9,128,256]{2,1,0:T(8,128)(2,1)S(1)}) custom-call(bf16[512,256]{1,0:T(8,128)(2,1)S(1)} %copy-done, bf16[128,256]{1,0:T(8,128)(2,1)S(1)} %copy-done.1, s32[1,3]{1,0:T(1,128)S(1)} %copy-done.6, ...), custom_call_target="tpu_custom_call" | custom-call | tf_op jit(solution)/shard_map/pallas_call | solution.py:459
  72.5 0.1 collective-permute-start.10
  72.6 5.8 %collective-permute-start.11 = (bf16[9,128,256]{2,1,0:T(8,128)(2,1)S(1)}, bf16[9,128,256]{2,1,0:T(8,128)(2,1)S(1)}, u32[]{:S(2)}, u32[]{:S(2)}) collective-permute-start(bf16[9,128,256]{2,1,0:T(8,128)(2,1)S(1)} %get-tuple-element.88), channel_id=1, source_target_pairs={{1,2},{3,4},{5,6},{7,8},{9,10},{11,12},{13,14},{2,1},{4,3},{6,5},{... | collective-permute-start | bytes 1769480 | tf_op jit(solution)/shard_map/ppermute | solution.py:403
  78.4 0.0 collective-permute-done.10.refs_15_
  78.4 3.8 %shard_map.158 = (f32[4,128,256]{2,1,0:T(8,128)S(1)}, f32[4,128,256]{2,1,0:T(8,128)S(1)}, f32[4,128,256]{2,1,0:T(8,128)}, f32[4,128,256]{2,1,0:T(8,128)S(1)}, f32[8,2,128]{2,1,0:T(2,128)S(1)}) custom-call(bf16[512,256]{1,0:T(8,128)(2,1)S(1)} %copy-done, bf16[128,256]{1,0:T(8,128)(2,1)S(1)} %copy-done.1, s32[1,3]{1,0:T(1,128)S(1)} %copy-done.6, ...), custom_call_target="tpu_custom_call" | custom-call | tf_op jit(solution)/shard_map/pallas_call | solution.py:451
  82.2 5.2 %collective-permute-done.11.refs_18_ = bf16[9,128,256]{2,1,0:T(8,128)(2,1)S(1)} collective-permute-done((bf16[9,128,256]{2,1,0:T(8,128)(2,1)S(1)}, bf16[9,128,256]{2,1,0:T(8,128)(2,1)S(1)}, u32[]{:S(2)}, u32[]{:S(2)}) %collective-permute-start.11) | collective-permute-done | bytes 589856 | tf_op jit(solution)/shard_map/ppermute | solution.py:403
  87.4 3.2 %shard_map.159 = (f32[1,8,128,256]{3,2,1,0:T(8,128)}, f32[8,8,128]{2,1,0:T(8,128)S(1)}) custom-call(s32[64]{0:T(128)S(1)} %add_bitcast_fusion.refs_5_.refs_0_, s32[1,1]{1,0:T(1,128)S(6)} %copy.27.count.refs_6_.refs_1_, s32[1,1,64,1]{3,2,1,0:T(8,128)S(1)} %copy.18.owner.refs_7_.refs_2_, f32[64,256]{1,0:T(8,128)S(1)} %get-tuple-element.51.refs_8_.refs_3_, ...), custom_call_target="tpu_custom_call" | custom-call | tf_op jit(solution)/shard_map/pallas_call | solution.py:464
  90.6 11.8 %all_to_all.10 = f32[8,8,128]{2,1,0:T(8,128)S(1)} all-to-all(f32[8,8,128]{2,1,0:T(8,128)S(1)} %get-tuple-element.93), channel_id=1, replica_groups=mesh['shot'=8,'space'=16] {'shot'}, dimensions={0} | all-to-all | bytes 65536 | tf_op jit(solution)/shard_map/all_to_all | solution.py:468
  102.4 0.6 reduce_sum.9
  (9 shorter events, 0.0 us)
Async XLA Ops:
  3.2 5.2 %copy-start.3 = (bf16[1,8,128,256]{3,2,1,0:T(8,128)(2,1)S(1)}, bf16[1,8,128,256]{3,2,1,0:T(8,128)(2,1)}, u32[]{:S(2)}) copy-start(bf16[1,8,128,256]{3,2,1,0:T(8,128)(2,1)} %cur.1) | copy-start | bytes 1572868
  3.2 10.5 %copy-start.2 = (bf16[1,8,128,256]{3,2,1,0:T(8,128)(2,1)S(1)}, bf16[1,8,128,256]{3,2,1,0:T(8,128)(2,1)}, u32[]{:S(2)}) copy-start(bf16[1,8,128,256]{3,2,1,0:T(8,128)(2,1)} %pri.1) | copy-start | bytes 1572868
  3.2 21.0 %all-to-all-start = ((bf16[8,8,64,128]{3,2,1,0:T(8,128)(2,1)}), bf16[8,8,64,128]{3,2,1,0:T(8,128)(2,1)S(1)}, u32[]{:S(2)}, u32[]{:S(2)}) async-start(bf16[8,8,64,128]{3,2,1,0:T(8,128)(2,1)} %shard_map.149), calls=%async_computation | async-start | bytes 2097152 | tf_op jit(solution)/shard_map/all_to_all | solution.py:420
  8.4 24.8 %collective-permute-start = (bf16[1,8,128,256]{3,2,1,0:T(8,128)(2,1)S(1)}, bf16[1,8,128,256]{3,2,1,0:T(8,128)(2,1)S(1)}, u32[]{:S(2)}, u32[]{:S(2)}) collective-permute-start(bf16[1,8,128,256]{3,2,1,0:T(8,128)(2,1)S(1)} %copy-done.3), channel_id=1, source_target_pairs={{1,2},{3,4},{5,6},{7,8},{9,10},{11,12},{13,14},{2,1},{4,3},{6,5},{... | collective-permute-start | bytes 1572872 | tf_op jit(solution)/shard_map/ppermute | solution.py:403
  13.6 19.6 %collective-permute-start.1 = (bf16[1,8,128,256]{3,2,1,0:T(8,128)(2,1)S(1)}, bf16[1,8,128,256]{3,2,1,0:T(8,128)(2,1)S(1)}, u32[]{:S(2)}, u32[]{:S(2)}) collective-permute-start(bf16[1,8,128,256]{3,2,1,0:T(8,128)(2,1)S(1)} %copy-done.3), channel_id=1, source_target_pairs={{0,1},{1,0},{2,3},{3,2},{4,5},{5,4},{6,7},{7,6},{8,9},{9,8},{10,11... | collective-permute-start | bytes 1572872 | tf_op jit(solution)/shard_map/ppermute | solution.py:403
  14.5 4.5 %copy-start.11 = (s32[1,1,64,3]{2,1,3,0:T(1,128)S(1)}, s32[1,1,64,3]{2,1,3,0:T(1,128)}, u32[]{:S(2)}) copy-start(s32[1,1,64,3]{2,1,3,0:T(1,128)} %param.22) | copy-start | bytes 2308
  14.5 4.5 %copy-start.12 = (s32[1,1,64,3]{2,1,3,0:T(1,128)S(1)}, s32[1,1,64,3]{2,1,3,0:T(1,128)}, u32[]{:S(2)}) copy-start(s32[1,1,64,3]{2,1,3,0:T(1,128)} %param.23) | copy-start | bytes 2308
  14.5 11.4 %collective-permute-start.3 = (bf16[4,128,256]{2,1,0:T(8,128)(2,1)}, bf16[4,128,256]{2,1,0:T(8,128)(2,1)S(1)}, u32[]{:S(2)}, u32[]{:S(2)}) collective-permute-start(bf16[4,128,256]{2,1,0:T(8,128)(2,1)} %get-tuple-element.94), channel_id=1, source_target_pairs={{0,1},{1,0},{2,3},{3,2},{4,5},{5,4},{6,7},{7,6},{8,9},{9,8},{10,11... | collective-permute-start | bytes 786440 | tf_op jit(solution)/shard_map/ppermute | solution.py:403
  15.0 18.2 %collective-permute-start.2 = (bf16[4,128,256]{2,1,0:T(8,128)(2,1)}, bf16[4,128,256]{2,1,0:T(8,128)(2,1)}, u32[]{:S(2)}, u32[]{:S(2)}) collective-permute-start(bf16[4,128,256]{2,1,0:T(8,128)(2,1)} %get-tuple-element.95), channel_id=1, source_target_pairs={{1,2},{3,4},{5,6},{7,8},{9,10},{11,12},{13,14},{2,1},{4,3},{6,5},{... | collective-permute-start | bytes 786440 | tf_op jit(solution)/shard_map/ppermute | solution.py:403
  20.4 0.7 copy-start.13
  21.2 0.8 copy-start.4
  22.0 0.8 copy-start.5
  23.0 1.2 %copy-start.9 = (s32[8,8]{1,0:T(8,128)S(1)}, s32[8,8]{1,0:T(8,128)}, u32[]{:S(2)}) copy-start(s32[8,8]{1,0:T(8,128)} %wanted.1) | copy-start | bytes 772
  24.2 0.7 copy-start.10
  24.8 8.4 %copy-start = (bf16[512,256]{1,0:T(8,128)(2,1)S(1)}, bf16[512,256]{1,0:T(8,128)(2,1)}, u32[]{:S(2)}) copy-start(bf16[512,256]{1,0:T(8,128)(2,1)} %constant.28.clone.weights.refs_0_.refs_8_) | copy-start | bytes 786436
  24.8 8.4 %copy-start.1 = (bf16[128,256]{1,0:T(8,128)(2,1)S(1)}, bf16[128,256]{1,0:T(8,128)(2,1)}, u32[]{:S(2)}) copy-start(bf16[128,256]{1,0:T(8,128)(2,1)} %constant.29.clone.across.refs_1_.refs_9_) | copy-start | bytes 196612
  25.8 7.5 %copy-start.6 = (s32[1,3]{1,0:T(1,128)S(1)}, s32[1,3]{1,0:T(1,128)}, u32[]{:S(2)}) copy-start(s32[1,3]{1,0:T(1,128)} %refs_10_.1) | copy-start | bytes 40
  25.8 7.5 %copy-start.7 = (s32[1,3]{1,0:T(1,128)S(1)}, s32[1,3]{1,0:T(1,128)}, u32[]{:S(2)}) copy-start(s32[1,3]{1,0:T(1,128)} %refs_11_.1) | copy-start | bytes 40
  25.8 7.5 %copy-start.8 = (f32[1,8]{1,0:T(1,128)S(1)}, f32[1,8]{1,0:T(1,128)}, u32[]{:S(2)}) copy-start(f32[1,8]{1,0:T(1,128)} %refs_12_.1) | copy-start | bytes 100
  25.8 7.4 %collective-permute-start.4 = (bf16[4,128,256]{2,1,0:T(8,128)(2,1)S(1)}, bf16[4,128,256]{2,1,0:T(8,128)(2,1)S(1)}, u32[]{:S(2)}, u32[]{:S(2)}) collective-permute-start(bf16[4,128,256]{2,1,0:T(8,128)(2,1)S(1)} %get-tuple-element.55.own_v_in), channel_id=1, source_target_pairs={{0,1},{1,0},{2,3},{3,2},{4,5},{5,4},{6,7},{7,6},{8,9},{9,8},{10,11... | collective-permute-start | bytes 786440 | tf_op jit(solution)/shard_map/ppermute | solution.py:403
  25.9 11.5 %collective-permute-start.5 = (bf16[4,128,256]{2,1,0:T(8,128)(2,1)S(1)}, bf16[4,128,256]{2,1,0:T(8,128)(2,1)S(1)}, u32[]{:S(2)}, u32[]{:S(2)}) collective-permute-start(bf16[4,128,256]{2,1,0:T(8,128)(2,1)S(1)} %get-tuple-element.54.own_v_x), channel_id=1, source_target_pairs={{1,2},{3,4},{5,6},{7,8},{9,10},{11,12},{13,14},{2,1},{4,3},{6,5},{... | collective-permute-start | bytes 786440 | tf_op jit(solution)/shard_map/ppermute | solution.py:403
  38.4 6.0 %collective-permute-start.6 = (bf16[9,128,256]{2,1,0:T(8,128)(2,1)S(1)}, bf16[9,128,256]{2,1,0:T(8,128)(2,1)S(1)}, u32[]{:S(2)}, u32[]{:S(2)}) collective-permute-start(bf16[9,128,256]{2,1,0:T(8,128)(2,1)S(1)} %get-tuple-element.64), channel_id=1, source_target_pairs={{0,1},{1,0},{2,3},{3,2},{4,5},{5,4},{6,7},{7,6},{8,9},{9,8},{10,11... | collective-permute-start | bytes 1769480 | tf_op jit(solution)/shard_map/ppermute | solution.py:403
  38.5 14.8 %collective-permute-start.7 = (bf16[9,128,256]{2,1,0:T(8,128)(2,1)S(1)}, bf16[9,128,256]{2,1,0:T(8,128)(2,1)S(1)}, u32[]{:S(2)}, u32[]{:S(2)}) collective-permute-start(bf16[9,128,256]{2,1,0:T(8,128)(2,1)S(1)} %get-tuple-element.68), channel_id=1, source_target_pairs={{1,2},{3,4},{5,6},{7,8},{9,10},{11,12},{13,14},{2,1},{4,3},{6,5},{... | collective-permute-start | bytes 1769480 | tf_op jit(solution)/shard_map/ppermute | solution.py:403
  55.5 5.9 %collective-permute-start.8 = (bf16[9,128,256]{2,1,0:T(8,128)(2,1)S(1)}, bf16[9,128,256]{2,1,0:T(8,128)(2,1)S(1)}, u32[]{:S(2)}, u32[]{:S(2)}) collective-permute-start(bf16[9,128,256]{2,1,0:T(8,128)(2,1)S(1)} %get-tuple-element.75), channel_id=1, source_target_pairs={{0,1},{1,0},{2,3},{3,2},{4,5},{5,4},{6,7},{7,6},{8,9},{9,8},{10,11... | collective-permute-start | bytes 1769480 | tf_op jit(solution)/shard_map/ppermute | solution.py:403
  55.6 14.8 %collective-permute-start.9 = (bf16[9,128,256]{2,1,0:T(8,128)(2,1)S(1)}, bf16[9,128,256]{2,1,0:T(8,128)(2,1)S(1)}, u32[]{:S(2)}, u32[]{:S(2)}) collective-permute-start(bf16[9,128,256]{2,1,0:T(8,128)(2,1)S(1)} %get-tuple-element.78), channel_id=1, source_target_pairs={{1,2},{3,4},{5,6},{7,8},{9,10},{11,12},{13,14},{2,1},{4,3},{6,5},{... | collective-permute-start | bytes 1769480 | tf_op jit(solution)/shard_map/ppermute | solution.py:403
  72.5 5.9 %collective-permute-start.10 = (bf16[9,128,256]{2,1,0:T(8,128)(2,1)S(1)}, bf16[9,128,256]{2,1,0:T(8,128)(2,1)S(1)}, u32[]{:S(2)}, u32[]{:S(2)}) collective-permute-start(bf16[9,128,256]{2,1,0:T(8,128)(2,1)S(1)} %get-tuple-element.85), channel_id=1, source_target_pairs={{0,1},{1,0},{2,3},{3,2},{4,5},{5,4},{6,7},{7,6},{8,9},{9,8},{10,11... | collective-permute-start | bytes 1769480 | tf_op jit(solution)/shard_map/ppermute | solution.py:403
  72.6 14.8 %collective-permute-start.11 = (bf16[9,128,256]{2,1,0:T(8,128)(2,1)S(1)}, bf16[9,128,256]{2,1,0:T(8,128)(2,1)S(1)}, u32[]{:S(2)}, u32[]{:S(2)}) collective-permute-start(bf16[9,128,256]{2,1,0:T(8,128)(2,1)S(1)} %get-tuple-element.88), channel_id=1, source_target_pairs={{1,2},{3,4},{5,6},{7,8},{9,10},{11,12},{13,14},{2,1},{4,3},{6,5},{... | collective-permute-start | bytes 1769480 | tf_op jit(solution)/shard_map/ppermute | solution.py:403

commit v3 on v2

v3 whole, which is shorter than its diff:
```python
import jax
import jax.numpy as jnp
import numpy as np
from jax import lax
from jax.experimental import pallas as pl
from jax.experimental.pallas import tpu as pltpu
from jax.sharding import PartitionSpec as P

STEPS = 8
CAPR = 16
PL = 8
ROWS = 128
COLS = 256
EDGE = 64
SLOTS = 64
SCALE = 5040.0
TAPS = (8064.0, -1008.0, 128.0, -9.0)
CENTRE_COLS = -43008.0
CENTRE_ROWS = -42.0
COURANT = 0.09
PACK_LIMIT = 56

VMEM = pl.BlockSpec(memory_space=pltpu.VMEM)
SMEM = pl.BlockSpec(memory_space=pltpu.SMEM)
HBM = pl.BlockSpec(memory_space=pltpu.HBM)
ANY = pl.BlockSpec(memory_space=pl.ANY)
f32 = jnp.float32
bf16 = jnp.bfloat16


def band_matrix(size, centre):
    gap = np.abs(np.arange(size)[:, None] - np.arange(size)[None, :])
    out = np.where(gap == 0, centre, 0.0)
    for k in range(1, 5):
        out = np.where(gap == k, TAPS[k - 1], out)
    return out


def constants():
    cols = band_matrix(COLS, CENTRE_COLS)
    rows = band_matrix(ROWS, CENTRE_ROWS)
    return (
        jnp.asarray(np.concatenate([cols, cols], 0), bf16),
        jnp.asarray(np.concatenate([rows, rows], 1), bf16),
    )


def call(body, outs, ins, scratch=(), limit=None, cost=None, alias=None, places=None):
    return pl.pallas_call(
        body,
        out_shape=[jax.ShapeDtypeStruct(s, d) for s, d in outs],
        in_specs=ins,
        out_specs=places or [VMEM] * len(outs),
        scratch_shapes=list(scratch),
        input_output_aliases=alias or {},
        compiler_params=pltpu.CompilerParams(vmem_limit_bytes=limit),
        cost_estimate=pl.CostEstimate(flops=cost[0], bytes_accessed=cost[1], transcendentals=0) if cost else None,
    )


def is_even():
    return lax.rem(lax.axis_index("space"), 2) == 0


def mirrored4(even, plane):
    return jnp.where(even, plane, 3 - plane)


def mirrored(even, plane):
    return jnp.where(even, plane, PL - 1 - plane)


def fetch(pairs, sems):
    copies = [pltpu.make_async_copy(src, dst, sems.at[i]) for i, (src, dst) in enumerate(pairs)]
    for copy in copies:
        copy.start()
    return copies


def wait(copies):
    for copy in copies:
        copy.wait()


def pack_kernel(home_hbm, wanted_hbm, store_hbm, out_hbm, home, wanted, store, out, sems, out_sems):
    copies = fetch(((home_hbm, home), (wanted_hbm, wanted), (store_hbm, store)), sems)
    wait(copies[:2])
    me = lax.axis_index("shot")
    even = is_even()
    chosen = []
    for s in range(8):
        count = jnp.int32(0)
        slots = [jnp.int32(0), jnp.int32(0)]
        for j in range(8):
            row = home[wanted[s, j]]
            mine = lax.shift_right_logical(row, 3) == me
            for rank in range(2):
                slots[rank] = jnp.where(mine & (count == rank), row & 7, slots[rank])
            count = count + mine.astype(jnp.int32)
        chosen.append(slots)
    copies[2].wait()
    back = []
    for s in range(8):
        for q in range(PL):
            p = mirrored(even, q)
            out[s, q] = jnp.concatenate([store[chosen[s][0], p], store[chosen[s][1], p]], 1)
        copy = pltpu.make_async_copy(out.at[s], out_hbm.at[s], out_sems.at[s])
        copy.start()
        back.append(copy)
    wait(back)


def plan_kernel(home, wanted, plan):
    me = lax.axis_index("shot")
    spot = lax.broadcasted_iota(jnp.int32, (1, 128), 1)
    listed = jnp.zeros((1, 128), jnp.int32)
    homes = []
    for j in range(8):
        homes.append(lax.shift_right_logical(home[wanted[me, j]], 3))
        nth = jnp.int32(0)
        for i in range(j):
            nth = nth + (homes[i] == homes[j]).astype(jnp.int32)
        listed = jnp.where(spot == j, homes[j], jnp.where(spot == 8 + j, nth, listed))
    plan[...] = listed


def swapped(x):
    return jnp.concatenate([x[:, EDGE:], x[:, :EDGE]], 1)


def assemble_kernel(plan, arrived, v_x, v_in):
    left = lax.broadcasted_iota(jnp.int32, (EDGE, 2 * EDGE), 1) < EDGE
    owners = [plan[0, j] for j in range(8)]
    ranks = [plan[0, 8 + j] for j in range(8)]
    for j in range(0, 8, 2):
        rows = slice(j // 4 * EDGE, (j // 4 + 1) * EDGE)
        lanes = slice(j % 4 * EDGE, (j % 4 + 2) * EDGE)
        for q in range(PL):
            x = arrived[owners[j], q]
            y = arrived[owners[j + 1], q]
            x = jnp.where(ranks[j] == 0, x, swapped(x))
            y = jnp.where(ranks[j + 1] == 0, swapped(y), y)
            out = v_x if q < 4 else v_in
            out[q % 4, rows, lanes] = jnp.where(left, x, y)


CHUNK = 16


def product(weights, across, u):
    hi = u.astype(bf16)
    lo = (u - hi.astype(f32)).astype(bf16)
    return jnp.dot(
        jnp.concatenate([hi, lo, across[...]], 1),
        jnp.concatenate([weights[...], hi, lo], 0),
        preferred_element_type=f32,
    )


def chunks():
    return [slice(r, r + CHUNK) for r in range(0, ROWS, CHUNK)]


def depth(get, e, low, high, r, acc):
    for k in range(1, 5):
        parts = [get(p, r) for p in (e + k, e - k) if low <= p < high]
        if parts:
            acc = acc + TAPS[k - 1] * sum(parts[1:], parts[0])
    return acc


def hat(frac):
    share = frac.astype(f32) * 0.125
    return 1.0 - share, share


def add_source(parts, even, cell, frac, pulse):
    lane = lax.broadcasted_iota(jnp.int32, (1, COLS), 1)
    wd, wr, wc = hat(frac[0, 0]), hat(frac[0, 1]), hat(frac[0, 2])
    column = jnp.where(lane == cell[0, 2], wc[0], 0.0) + jnp.where(lane == cell[0, 2] + 1, wc[1], 0.0)
    for dp in range(2):
        plane = mirrored(even, cell[0, 0] + dp - lax.axis_index("space") * PL)
        for ref, first, down in parts:
            at = first - plane if down else plane - first

            @pl.when((at >= 0) & (at < ref.shape[0]))
            def _():
                for dr in range(2):
                    row = pl.ds(cell[0, 1] + dr, 1)
                    ref[at, row, :] = ref[at, row, :] + pulse * (wd[dp] * wr[dr] * column)


GROUP = 8


def sample(fields, codes, count, spread, place, owner, rows, out):
    even = is_even()

    def group(g, _):
        for j in range(GROUP):
            r = g * GROUP + j
            code = codes[0, r]
            wr = hat(code & 7)
            wd = hat(lax.shift_right_logical(code, 3) & 7)
            y = lax.shift_right_logical(code, 6) & 127
            p = lax.shift_right_logical(code, 13)
            for f, (src, _) in enumerate(fields):
                acc = None
                for dp in range(2):
                    plane = mirrored(even, p + dp)
                    for dr in range(2):
                        term = (wd[dp] * wr[dr]) * src[plane, pl.ds(y + dr, 1), :]
                        acc = term if acc is None else acc + term
                rows[f, pl.ds(r, 1), :] = acc
        return 0

    lax.fori_loop(0, lax.div(count[0, 0] + GROUP - 1, GROUP), group, 0)
    live = lax.broadcasted_iota(jnp.int32, (SLOTS, 1), 0) < count[0, 0]
    for f, (_, n) in enumerate(fields):
        values = jnp.where(live, jnp.sum(rows[f] * spread[...], axis=1, keepdims=True), 0.0)
        placed = values * place[...]
        for q in range(8):
            out[q, n : n + 1, :] = jnp.sum(jnp.where(owner[...] == q, placed, 0.0), axis=0, keepdims=True)


def column(row):
    same = lax.broadcasted_iota(jnp.int32, (SLOTS, SLOTS), 0) == lax.broadcasted_iota(jnp.int32, (SLOTS, SLOTS), 1)
    return jnp.sum(jnp.where(same, row, 0), axis=1, keepdims=True)


def receiver_kernel(count, cells, fracs, owner, spread, place, owners, codes):
    lane = lax.broadcasted_iota(jnp.int32, (SLOTS, COLS), 1)
    share = column(fracs[2:3, :]).astype(f32) * 0.125
    at = column(cells[2:3, :])
    spread[...] = jnp.where(lane == at, 1.0 - share, 0.0) + jnp.where(lane == at + 1, share, 0.0)
    me = lax.axis_index("shot")
    slot = lax.broadcasted_iota(jnp.int32, (SLOTS, 1), 0)
    live = slot < count[0, 0]
    group = lax.broadcasted_iota(jnp.int32, (SLOTS, 128), 1)
    mine = column(owner[...])
    owners[...] = mine
    chosen = jnp.where((mine == group) & live, 1.0, 0.0)
    earlier = jnp.where(
        lax.broadcasted_iota(jnp.int32, (SLOTS, SLOTS), 1) < lax.broadcasted_iota(jnp.int32, (SLOTS, SLOTS), 0), 1.0, 0.0
    )
    before = jnp.dot(earlier.astype(bf16), chosen.astype(bf16), preferred_element_type=f32)
    rank = jnp.sum(before * chosen, axis=1, keepdims=True).astype(jnp.int32)
    place[...] = jnp.where((group == rank + me * CAPR) & live, 1.0, 0.0)
    codes[...] = ((cells[0:1, :] * ROWS + cells[1:2, :]) * 8 + fracs[0:1, :]) * 8 + fracs[1:2, :]

def open_kernel(weights, across, cur, cur_in, pri, pri_in, sums, lead, sums_in, lead_in, u, halo):
    even = is_even()
    for j in range(PL):
        u[j] = cur[0, mirrored(even, j)].astype(f32)
        halo[j] = cur_in[0, mirrored(even, j)].astype(f32)

    def now(e, r):
        return u[e, r] if e < PL else halo[e - PL, r]

    for e in range(12):
        m = product(weights, across, now(e, slice(0, ROWS)))
        for r in chunks():
            acc = depth(now, e, 0, 16, r, m[r])
            if e < PL:
                sums[e, r] = acc
                lead[e, r] = 2.0 * now(e, r) - pri[0, mirrored(even, e), r].astype(f32)
            else:
                sums_in[e - PL, r] = acc
                lead_in[e - PL, r] = 2.0 * now(e, r) - pri_in[mirrored4(even, e - PL), r].astype(f32)


def factor(x):
    scaled = x.astype(f32) * COURANT
    return scaled * scaled * (1.0 / SCALE)


def near_kernel(
    weights, across, cell_any, frac_any, pulses_any, u, sums, lead, own_v_x, own_v_in,
    coef, part, own_hi, base, cell, frac, pulses, sems,
):
    source = fetch(((cell_any, cell), (frac_any, frac), (pulses_any, pulses)), sems)
    for e in range(PL):
        for r in chunks():
            c = factor((own_v_x if e < 4 else own_v_in)[e % 4, r])
            coef[e, r] = c
            x = lead[e, r] + c * sums[e, r]
            if e < 4:
                part[e, r] = x
            else:
                own_hi[e - 4, r] = x
    wait(source)
    add_source(((own_hi, 4, False),), is_even(), cell, frac, pulses[0, 0])
    half_step(weights, across, own_hi, None, u, coef, base)


def half_step(weights, across, own_hi, inner, u, coef, base):
    for q in range(4, PL):
        m = product(weights, across, own_hi[q - 4])
        for r in chunks():
            acc = depth(lambda e, r: own_hi[e - 4, r] if e < PL else inner[e - PL, r], q, 4, 12 if inner is not None else PL, r, m[r])
            base[q - 4, r] = 2.0 * own_hi[q - 4, r] - u[q, r] + coef[q, r] * acc


def cross_kernel(
    weights, across, cell_any, frac_any, pulses_any, u, got_x, coef, part, own_hi, base_hi,
    own, base, outer_lead, outer_sum, halo, cell, frac, pulses, sems,
):
    source = fetch(((cell_any, cell), (frac_any, frac), (pulses_any, pulses)), sems)
    even = is_even()
    for j in range(PL):
        halo[j] = got_x[mirrored(even, PL - 1 - j)].astype(f32)

    def now(e, r):
        return halo[-1 - e, r] if e < 0 else u[e, r]

    for q in range(4):
        for r in chunks():
            own[q, r] = part[q, r] + coef[q, r] * depth(now, q, -8, 0, r, 0.0)
            own[q + 4, r] = own_hi[q, r]
    for e in range(-4, 0):
        j = -1 - e
        m = product(weights, across, halo[j])
        for r in chunks():
            outer_sum[j, r] = depth(now, e, -8, PL, r, m[r])
            outer_lead[j, r] = 2.0 * halo[j, r] - got_x[PL + mirrored4(even, 3 - j), r].astype(f32)
    wait(source)
    add_source(((own.at[pl.ds(0, 4)], 0, False),), even, cell, frac, pulses[0, 0])

    def following(e, r):
        return own[e, r]

    for q in range(4):
        m = product(weights, across, own[q])
        for r in chunks():
            acc = depth(following, q, 0, PL, r, m[r])
            base[q, r] = 2.0 * own[q, r] - u[q, r] + coef[q, r] * acc
    for q in range(4, PL):
        for r in chunks():
            base[q, r] = base_hi[q - 4, r] + coef[q, r] * depth(following, q, 0, 4, r, 0.0)


def bundle_kernel(cur, pri, both, half, sems):
    first = jnp.where(is_even(), 0, 4)
    wait(
        fetch(
            (
                (cur.at[0], both.at[pl.ds(0, PL)]),
                (pri.at[0, pl.ds(first, 4)], both.at[pl.ds(PL, 4)]),
                (pri.at[0, pl.ds(4 - first, 4)], half),
            ),
            sems,
        )
    )


def send_kernel(near, u, out):
    for q in range(PL):
        out[q] = u[q].astype(bf16)
    edge = u[near]
    out[PL] = (edge - edge.astype(bf16).astype(f32)).astype(bf16)


def far_kernel(
    cell_any, frac_any, pulses_any, lead_x, sums_x, v_x, lead_in, sums_in, v_in, base, coef,
    coef_x, coef_in, outer, inner, last, send_x, cell, frac, pulses, sems,
):
    source = fetch(((cell_any, cell), (frac_any, frac), (pulses_any, pulses)), sems)
    even = is_even()
    for j in range(4):
        for r in chunks():
            c = factor(v_x[j, r])
            coef_x[j, r] = c
            outer[j, r] = lead_x[j, r] + c * sums_x[j, r]
            c = factor(v_in[3 - j, r])
            coef_in[j, r] = c
            inner[j, r] = lead_in[j, r] + c * sums_in[j, r]
    wait(source)
    add_source(((outer, -1, True), (inner, PL, False)), even, cell, frac, pulses[0, 0])
    for q in range(PL):
        for r in chunks():
            if q < 4:
                acc = depth(lambda e, r: outer[-1 - e, r], q, -4, 0, r, 0.0)
            else:
                acc = depth(lambda e, r: inner[e - PL, r], q, PL, 12, r, 0.0)
            last[q, r] = base[q, r] + coef[q, r] * acc
    add_source(((last, 0, False),), even, cell, frac, pulses[0, 1])
    send_kernel(0, last, send_x)


def during_kernel(
    step, weights, across, cell_any, frac_any, pulses_any, codes, count, owner, spread, place, u, prev, prev_in, coef, coef_in, got_in,
    part, own_hi, inner, base, gath, halo, rows, cell, frac, pulses, sems,
):
    source = fetch(((cell_any, cell), (frac_any, frac), (pulses_any, pulses)), sems)
    even = is_even()
    for j in range(PL):
        x = got_in[PL - 1 - j].astype(f32)
        halo[j] = x + got_in[PL].astype(f32) if j == 0 else x

    def now(e, r):
        return u[e, r] if e < PL else halo[e - PL, r]

    whole = slice(0, ROWS)
    for e in range(12):
        m = product(weights, across, now(e, whole))
        for r in chunks():
            acc = depth(now, e, 0, 16, r, m[r])
            if e < PL:
                x = 2.0 * u[e, r] - prev[e, r] + coef[e, r] * acc
                if e < 4:
                    part[e, r] = x
                else:
                    own_hi[e - 4, r] = x
            else:
                inner[e - PL, r] = 2.0 * now(e, r) - prev_in[e - PL, r] + coef_in[e - PL, r] * acc
    wait(source)
    add_source(((own_hi, 4, False), (inner, PL, False)), even, cell, frac, pulses[0, step])
    half_step(weights, across, own_hi, inner, u, coef, base)
    sample(((prev, 0), (u, 1)), codes, count, spread, place, owner, rows, gath)


def after_kernel(
    step, weights, across, source, u, prev, prev_x, coef, coef_x, got_x, part, own_hi, base,
    own, outer, last, halo,
):
    copies, cell, frac, pulses = source
    even = is_even()
    for j in range(PL):
        x = got_x[j].astype(f32)
        halo[j] = x + got_x[PL].astype(f32) if j == 0 else x

    def now(e, r):
        return halo[-1 - e, r] if e < 0 else u[e, r]

    whole = slice(0, ROWS)
    for e in range(-4, 0):
        j = -1 - e
        m = product(weights, across, halo[j])
        for r in chunks():
            acc = depth(now, e, -8, 8, r, m[r])
            outer[j, r] = 2.0 * halo[j, r] - prev_x[j, r] + coef_x[j, r] * acc
    for q in range(4):
        for r in chunks():
            own[q, r] = part[q, r] + coef[q, r] * depth(now, q, -8, 0, r, 0.0)
            own[q + 4, r] = own_hi[q, r]
    wait(copies)
    add_source(((outer, -1, True), (own.at[pl.ds(0, 4)], 0, False)), even, cell, frac, pulses[0, step])

    def following(e, r):
        return outer[-1 - e, r] if e < 0 else own[e, r]

    for q in range(4):
        m = product(weights, across, own[q])
        for r in chunks():
            acc = depth(following, q, -4, 8, r, m[r])
            last[q, r] = 2.0 * own[q, r] - u[q, r] + coef[q, r] * acc
    for q in range(4, PL):
        for r in chunks():
            last[q, r] = base[q - 4, r] + coef[q, r] * depth(following, q, 0, 4, r, 0.0)


def middle_kernel(step, weights, across, cell_any, frac_any, pulses_any, *refs):
    own, outer, last, send_x, halo, cell, frac, pulses, sems = refs[-9:]
    copies = fetch(((cell_any, cell), (frac_any, frac), (pulses_any, pulses)), sems)
    source = (copies, cell, frac, pulses)
    after_kernel(step, weights, across, source, *refs[:-9], own, outer, last, halo)
    add_source(((last, 0, False),), is_even(), cell, frac, pulses[0, step + 1])
    send_kernel(0, last, send_x)


def last_kernel(
    step, codes_any, count_any, owner, spread, place, gath_a, gath_b, gath_c,
    weights, across, cell_any, frac_any, pulses_any, *refs,
):
    final, gath, own, outer, last, halo, rows, cell, frac, pulses, sems, codes, count, more_sems, final_sems = refs[-15:]
    copies = fetch(((cell_any, cell), (frac_any, frac), (pulses_any, pulses)), sems)
    more = fetch(((codes_any, codes), (count_any, count)), more_sems)
    even = is_even()
    source = (copies, cell, frac, pulses)
    after_kernel(step, weights, across, source, *refs[:-15], own, outer, last, halo)
    add_source(((last, 0, False),), even, cell, frac, pulses[0, step + 1])
    back = fetch([(last.at[q], final.at[0, mirrored(even, q)]) for q in range(PL)], final_sems)
    for i, some in enumerate((gath_a, gath_b, gath_c)):
        gath[:, 2 * i : 2 * i + 2, :] = some[...]
    wait(more)
    sample(((own, step), (last, step + 1)), codes, count, spread, place, owner, rows, gath)
    wait(back)


MIB = 1 << 20


def on_device(
    prior_field, current_field, model_store, tile_home, aperture, source_cell, source_frac,
    wavelet, receiver_cell, receiver_frac, receiver_count, trace_owner,
):
    size = lax.axis_size("space")
    pair_in = [(i, i ^ 1) for i in range(size)]
    pair_x = [(i, i + 1) for i in range(1, size - 1, 2)] + [(i + 1, i) for i in range(1, size - 1, 2)]

    def swap(across_chips, in_chip):
        return lax.ppermute(across_chips, "space", pair_x), lax.ppermute(in_chip, "space", pair_in)

    weights, across = constants()
    plane = (ROWS, COLS)
    four = ((4,) + plane, f32)
    eight = ((PL,) + plane, f32)
    tile_planes = ((4,) + plane, bf16)
    send = ((PL + 1,) + plane, bf16)
    scratch8 = pltpu.VMEM(*eight)
    rows = pltpu.VMEM((2, SLOTS, COLS), f32)

    out = call(
        pack_kernel, [((8, PL, EDGE, 2 * EDGE), bf16)], [HBM] * 3,
        [pltpu.SMEM((64,), jnp.int32), pltpu.SMEM((8, 8), jnp.int32), pltpu.VMEM((8, PL, EDGE, EDGE), bf16),
         pltpu.VMEM((8, PL, EDGE, 2 * EDGE), bf16), pltpu.SemaphoreType.DMA((3,)), pltpu.SemaphoreType.DMA((8,))],
        limit=PACK_LIMIT * MIB, places=[HBM],
    )(tile_home, aperture, model_store)[0]
    plan = call(plan_kernel, [((1, 128), jnp.int32)], [SMEM, SMEM], limit=4 * MIB)(tile_home, aperture)[0]
    arrived = lax.all_to_all(out, "shot", split_axis=0, concat_axis=0, tiled=True)
    both, half = call(
        bundle_kernel, [((12,) + plane, bf16), tile_planes], [ANY, ANY], [pltpu.SemaphoreType.DMA((3,))],
        limit=4 * MIB, places=[ANY, ANY],
    )(current_field, prior_field)
    first_x, pri_in = swap(both, half)
    cur_in = lax.ppermute(current_field, "space", pair_in)
    spread, place, owners, codes = call(
        receiver_kernel,
        [((SLOTS, COLS), f32), ((SLOTS, 128), f32), ((SLOTS, 1), jnp.int32), ((1, SLOTS), jnp.int32)],
        [SMEM] + [VMEM] * 3, limit=4 * MIB,
    )(
        receiver_count, jnp.transpose(receiver_cell[0, 0]), jnp.transpose(receiver_frac[0, 0]),
        jnp.transpose(trace_owner[0, 0]),
    )
    sums, lead, sums_in, lead_in, u = call(
        open_kernel, [eight, eight, four, four, eight], [VMEM] * 6, [scratch8], limit=16 * MIB
    )(weights, across, current_field, cur_in, prior_field, pri_in)
    arrived, sums, lead, u = lax.optimization_barrier((arrived, sums, lead, u))
    own_v_x, own_v_in = call(
        assemble_kernel, [tile_planes, tile_planes], [SMEM, VMEM], limit=8 * MIB
    )(plan, arrived)
    v_x = lax.ppermute(own_v_x, "space", pair_x)
    source = (source_cell, source_frac, wavelet)
    source_specs = [ANY] * 3
    source_scratch = [
        pltpu.SMEM((1, 3), jnp.int32), pltpu.SMEM((1, 3), jnp.int32), pltpu.SMEM((1, STEPS), f32), pltpu.SemaphoreType.DMA((3,)),
    ]
    receivers = (codes, receiver_count, owners, spread, place)
    receiver_specs = [SMEM, SMEM, VMEM, VMEM, VMEM]
    coef, part, own_hi, base = call(
        near_kernel, [eight, four, four, four], [VMEM] * 2 + source_specs + [VMEM] * 5,
        source_scratch, limit=16 * MIB,
    )(weights, across, *source, u, sums, lead, own_v_x, own_v_in)
    own_v_in, part = lax.optimization_barrier((own_v_in, part))
    v_in = lax.ppermute(own_v_in, "space", pair_in)
    prev, base, lead, total = call(
        cross_kernel, [eight, eight, four, four], [VMEM] * 2 + source_specs + [VMEM] * 6,
        [scratch8] + source_scratch, limit=16 * MIB,
    )(weights, across, *source, u, first_x, coef, part, own_hi, base)
    coef_x, coef_in, prev_x, prev_in, u, send_x = call(
        far_kernel, [four, four, four, four, eight, send], source_specs + [VMEM] * 8, source_scratch, limit=16 * MIB
    )(*source, lead, total, v_x, lead_in, sums_in, v_in, base, coef)
    gaths = []
    for n in (2, 4, 6):
        send_in = call(lambda *refs: send_kernel(PL - 1, *refs), [send], [VMEM], limit=4 * MIB)(u)[0]
        got_x, got_in = swap(send_x, send_in)
        part, own_hi, inner, base, gath = call(
            lambda *refs, n=n: during_kernel(n, *refs), [four, four, four, four, ((8, 2, 128), f32)],
            [VMEM] * 2 + source_specs + receiver_specs + [VMEM] * 6, [scratch8, rows] + source_scratch, limit=16 * MIB,
        )(weights, across, *source, *receivers, u, prev, prev_in, coef, coef_in, got_in)
        gaths.append(gath)
        common = (weights, across, *source, u, prev, prev_x, coef, coef_x, got_x, part, own_hi, base)
        common_specs = [VMEM] * 2 + source_specs + [VMEM] * 9
        if n < 6:
            prev, prev_x, u, send_x = call(
                lambda *refs, n=n: middle_kernel(n, *refs), [eight, four, eight, send], common_specs, [scratch8] + source_scratch, limit=16 * MIB
            )(*common)
            prev_in = inner
        else:
            final, gath = call(
                lambda *refs, n=n: last_kernel(n, *refs), [((1, PL) + plane, f32), ((8, STEPS, 128), f32)],
                [ANY, ANY] + [VMEM] * 6 + common_specs,
                [scratch8, pltpu.VMEM(*four), scratch8, scratch8, rows] + source_scratch
                + [pltpu.SMEM((1, SLOTS), jnp.int32), pltpu.SMEM((1, 1), jnp.int32), pltpu.SemaphoreType.DMA((2,)),
                   pltpu.SemaphoreType.DMA((PL,))],
                limit=20 * MIB, places=[ANY, VMEM],
            )(*receivers, *gaths, *common)
    back = lax.all_to_all(gath, "shot", split_axis=0, concat_axis=0, tiled=True)
    return final, jnp.sum(back, axis=0)[None, None]


def solution(mesh):
    placed = (
        P("shot", "space", None, None),
        P("shot", "space", None, None),
        P("shot", "space", None, None),
        P(),
        P(),
        P("shot", None),
        P("shot", None),
        P("shot", None),
        P("shot", "space", None, None),
        P("shot", "space", None, None),
        P("shot", "space"),
        P("shot", "space", None, None),
    )
    return jax.shard_map(
        on_device,
        mesh=mesh,
        in_specs=placed,
        out_specs=(P("shot", "space", None, None), P("shot", "space", None, None)),
        check_vma=False,
    )
```

time: 104 us -> 100 us (0.962)
  starting transfers between devices: 38.8 us -> 32.8 us
  Pallas kernels: 26.7 us -> 30.9 us
  waiting for transfers between devices: 18.9 us -> 17.5 us
    ppermute x6 -> x4, starting transfers between devices: 32.8 us -> 21.8 us  [swap(): lax.ppermute(across_chips, 'space', pair_x)]
    ppermute x0 -> x3, starting transfers between devices: none -> 5.49 us  [the longest x1 5.32 us: on_device(): v_x = lax.ppermute(own_v_x, 'space', pair_x)]
    ppermute x6 -> x4, waiting for transfers between devices: 17.8 us -> 14.2 us  [swap(): lax.ppermute(across_chips, 'space', pair_x)]
    pallas_call x3, Pallas kernels: 10.3 us -> 13.4 us  [on_device(): call(lambda *refs, n=n: during_kernel(n, *refs), [four, four, four, four,...]
    pallas_call x4 -> x11, Pallas kernels: 6.35 us -> 9.08 us  [the longest x1 2.8 us: on_device(): call(cross_kernel, [eight, eight, four, four], [VMEM] * 2 + source_specs...]
    unnamed x32 -> x40, local copies, waits for them, and re-layouts: 3.72 us -> 5.49 us
    pallas_call x2, Pallas kernels: 4.21 us -> 2.93 us  [on_device(): call(lambda *refs, n=n: middle_kernel(n, *refs), [eight, four, eight, sen...]
  transfers between devices with their start and end apart: 13 -> 12, of which waited for: 5 -> 7; matrix products, arithmetic and copies ran while one was open for 2% -> 0% of each run, Pallas kernels for 15% -> 21%
where the time goes in v3:
time: 100 us
  starting transfers between devices  32.8 us (33%)
  Pallas kernels  30.9 us (31%)
  waiting for transfers between devices  17.5 us (18%)
  blocking collectives  10.9 us (11%)
  local copies, waits for them, and re-layouts  5.49 us (5%)
  between operations  1.74 us (2%)
    ppermute x4, starting transfers between devices, swap(): lax.ppermute(across_chips, 'space', pair_x)  21.8 us
    ppermute x4, waiting for transfers between devices, swap(): lax.ppermute(across_chips, 'space', pair_x)  14.2 us
    pallas_call x3, Pallas kernels, on_device(): call(lambda *refs, n=n: during_kernel(n, *refs), [four, four, four, four,...  13.4 us
    all_to_all x1, blocking collectives, on_device(): back = lax.all_to_all(gath, 'shot', split_axis=0, concat_axis=0, tiled=True)  10.9 us
    unnamed x40, local copies, waits for them, and re-layouts  5.49 us
    ppermute x1, starting transfers between devices, on_device(): v_x = lax.ppermute(own_v_x, 'space', pair_x)  5.32 us
    all_to_all x1, starting transfers between devices, on_device(): lax.all_to_all(out, 'shot', split_axis=0, concat_axis=0, tiled=True)  5.16 us
    pallas_call x1, Pallas kernels, on_device(): call(lambda *refs, n=n: last_kernel(n, *refs), [((1, PL) + plane, f32), (...  3.1 us
  transfers between devices with their start and end apart: 12, of which 7 were waited for; matrix products, arithmetic and copies ran while one was open for 0% of the time, Pallas kernels for 21%

profile of v3, /device:TPU:16, one launch (start us, length us, event | category | flops | bytes accessed | tf_op | source)
XLA Modules:
  0.0 100.0 jit_solution(4680571981654623304)
XLA Ops:
  0.6 2.4 %shard_map.150 = bf16[8,8,64,128]{3,2,1,0:T(8,128)(2,1)} custom-call(s32[64]{0:T(128)} %home.1, s32[8,8]{1,0:T(8,128)} %wanted.1, bf16[8,8,64,64]{3,2,1,0:T(8,128)(2,1)} %store_hbm.1), custom_call_target="tpu_custom_call" | custom-call | tf_op jit(solution)/shard_map/pallas_call | solution.py:513
  3.1 0.0 copy-start.2
  3.1 0.0 copy-start.3
  3.1 5.2 %all-to-all-start = ((bf16[8,8,64,128]{3,2,1,0:T(8,128)(2,1)}), bf16[8,8,64,128]{3,2,1,0:T(8,128)(2,1)S(1)}, u32[]{:S(2)}, u32[]{:S(2)}) async-start(bf16[8,8,64,128]{3,2,1,0:T(8,128)(2,1)} %shard_map.150), calls=%async_computation | async-start | bytes 2097152 | tf_op jit(solution)/shard_map/all_to_all | solution.py:520
  8.2 0.0 copy-start
  8.3 0.0 copy-start.1
  8.3 0.1 collective-permute-start
  8.4 0.0 copy-done.3
  8.4 0.0 copy-start.15
  8.4 0.9 shard_map.151
  9.3 0.0 copy-start.16
  9.3 6.1 %collective-permute-start.2 = (bf16[12,128,256]{2,1,0:T(8,128)(2,1)}, bf16[12,128,256]{2,1,0:T(8,128)(2,1)}, u32[]{:S(2)}, u32[]{:S(2)}) collective-permute-start(bf16[12,128,256]{2,1,0:T(8,128)(2,1)} %get-tuple-element.68), channel_id=1, source_target_pairs={{1,2},{3,4},{5,6},{7,8},{9,10},{11,12},{13,14},{2,1},{4,3},{6,5},{... | collective-permute-start | bytes 2359304 | tf_op jit(solution)/shard_map/ppermute | solution.py:502
  15.4 0.1 collective-permute-start.1
  15.5 0.7 shard_map.153.plan
  16.2 0.8 collective-permute-done.1.pri_in
  17.0 0.0 collective-permute-done.cur_in
  17.1 1.3 %shard_map.152 = (f32[8,128,256]{2,1,0:T(8,128)S(1)}, f32[8,128,256]{2,1,0:T(8,128)S(1)}, f32[4,128,256]{2,1,0:T(8,128)S(1)}, f32[4,128,256]{2,1,0:T(8,128)S(1)}, f32[8,128,256]{2,1,0:T(8,128)S(1)}) custom-call(bf16[512,256]{1,0:T(8,128)(2,1)S(1)} %copy-done, bf16[128,256]{1,0:T(8,128)(2,1)S(1)} %copy-done.1, bf16[1,8,128,256]{3,2,1,0:T(8,128)(2,1)S(1)} %copy-done.2, ...), custom_call_target="tpu_custom_call" | custom-call | tf_op jit(solution)/shard_map/pallas_call | solution.py:535
  18.4 0.0 copy-start.4
  18.4 1.0 copy-done.4
  19.3 1.0 copy-done.6
  20.3 0.8 copy-done.8
  21.1 0.8 copy-done.10
  21.9 2.1 %all-to-all-done.arrived = bf16[8,8,64,128]{3,2,1,0:T(8,128)(2,1)S(1)} async-done(((bf16[8,8,64,128]{3,2,1,0:T(8,128)(2,1)}), bf16[8,8,64,128]{3,2,1,0:T(8,128)(2,1)S(1)}, u32[]{:S(2)}, u32[]{:S(2)}) %all-to-all-start) | async-done | bytes 1048608 | tf_op jit(solution)/shard_map/all_to_all | solution.py:520
  24.0 0.9 shard_map.154
  24.9 0.0 copy-start.12
  24.9 0.0 copy-start.13
  25.0 0.0 copy-start.14
  25.0 5.3 %collective-permute-start.3 = (bf16[4,128,256]{2,1,0:T(8,128)(2,1)S(1)}, bf16[4,128,256]{2,1,0:T(8,128)(2,1)S(1)}, u32[]{:S(2)}, u32[]{:S(2)}) collective-permute-start(bf16[4,128,256]{2,1,0:T(8,128)(2,1)S(1)} %get-tuple-element.72.own_v_x), channel_id=1, source_target_pairs={{1,2},{3,4},{5,6},{7,8},{9,10},{11,12},{13,14},{2,1},{4,3},{6,5},{... | collective-permute-start | bytes 786440 | tf_op jit(solution)/shard_map/ppermute | solution.py:542
  30.3 1.2 %copy-done.7 = f32[8,128,256]{2,1,0:T(8,128)S(1)} copy-done((f32[8,128,256]{2,1,0:T(8,128)S(1)}, f32[8,128,256]{2,1,0:T(8,128)}, u32[]{:S(2)}) %copy-start.7) | copy-done | bytes 1048600
  31.6 1.1 %shard_map.155 = (f32[8,128,256]{2,1,0:T(8,128)S(1)}, f32[4,128,256]{2,1,0:T(8,128)S(1)}, f32[4,128,256]{2,1,0:T(8,128)S(1)}, f32[4,128,256]{2,1,0:T(8,128)S(1)}) custom-call(bf16[512,256]{1,0:T(8,128)(2,1)S(1)} %copy-done, bf16[128,256]{1,0:T(8,128)(2,1)S(1)} %copy-done.1, s32[1,3]{1,0:T(1,128)S(1)} %copy-done.12, s32[1,3]{1,0:T(1,128)S(1)} %copy-done.13, ...), custom_call_target="tpu_custom_call" | custom-call | tf_op jit(solution)/shard_map/pallas_call | solution.py:550
  32.6 0.1 collective-permute-start.4
  32.7 0.5 collective-permute-done.2.got_x
  33.3 2.8 %shard_map.156 = (f32[8,128,256]{2,1,0:T(8,128)S(1)}, f32[8,128,256]{2,1,0:T(8,128)S(1)}, f32[4,128,256]{2,1,0:T(8,128)S(1)}, f32[4,128,256]{2,1,0:T(8,128)S(1)}) custom-call(bf16[512,256]{1,0:T(8,128)(2,1)S(1)} %copy-done, bf16[128,256]{1,0:T(8,128)(2,1)S(1)} %copy-done.1, s32[1,3]{1,0:T(1,128)S(1)} %copy-done.12, s32[1,3]{1,0:T(1,128)S(1)} %copy-done.13, ...), custom_call_target="tpu_custom_call" | custom-call | tf_op jit(solution)/shard_map/pallas_call | solution.py:556
  36.1 0.3 collective-permute-done.3.v_x
  36.4 0.0 collective-permute-done.4.v_in
  36.4 1.0 shard_map.157
  37.4 0.1 shard_map.158
  37.5 0.0 copy-start.18
  37.5 0.0 copy-start.19
  37.5 0.1 collective-permute-start.5
  37.6 5.2 %collective-permute-start.6 = (bf16[9,128,256]{2,1,0:T(8,128)(2,1)S(1)}, bf16[9,128,256]{2,1,0:T(8,128)(2,1)S(1)}, u32[]{:S(2)}, u32[]{:S(2)}) collective-permute-start(bf16[9,128,256]{2,1,0:T(8,128)(2,1)S(1)} %get-tuple-element.92), channel_id=1, source_target_pairs={{1,2},{3,4},{5,6},{7,8},{9,10},{11,12},{13,14},{2,1},{4,3},{6,5},{... | collective-permute-start | bytes 1769480 | tf_op jit(solution)/shard_map/ppermute | solution.py:502
  43.5 0.0 copy-start.17
  43.5 0.6 copy-done.17
  44.1 0.3 shard_map.149
  44.4 0.0 collective-permute-done.5.refs_15_
  44.4 4.4 %shard_map.159 = (f32[4,128,256]{2,1,0:T(8,128)S(1)}, f32[4,128,256]{2,1,0:T(8,128)S(1)}, f32[4,128,256]{2,1,0:T(8,128)S(1)}, f32[4,128,256]{2,1,0:T(8,128)S(1)}, f32[8,2,128]{2,1,0:T(2,128)S(1)}) custom-call(bf16[512,256]{1,0:T(8,128)(2,1)S(1)} %copy-done, bf16[128,256]{1,0:T(8,128)(2,1)S(1)} %copy-done.1, s32[1,3]{1,0:T(1,128)S(1)} %copy-done.12, ...), custom_call_target="tpu_custom_call" | custom-call | tf_op jit(solution)/shard_map/pallas_call | solution.py:567
  48.8 3.6 %collective-permute-done.6.refs_10_ = bf16[9,128,256]{2,1,0:T(8,128)(2,1)S(1)} collective-permute-done((bf16[9,128,256]{2,1,0:T(8,128)(2,1)S(1)}, bf16[9,128,256]{2,1,0:T(8,128)(2,1)S(1)}, u32[]{:S(2)}, u32[]{:S(2)}) %collective-permute-start.6) | collective-permute-done | bytes 589856 | tf_op jit(solution)/shard_map/ppermute | solution.py:502
  52.4 1.5 %shard_map.160 = (f32[8,128,256]{2,1,0:T(8,128)S(1)}, f32[4,128,256]{2,1,0:T(8,128)S(1)}, f32[8,128,256]{2,1,0:T(8,128)S(1)}, bf16[9,128,256]{2,1,0:T(8,128)(2,1)S(1)}) custom-call(bf16[512,256]{1,0:T(8,128)(2,1)S(1)} %copy-done, bf16[128,256]{1,0:T(8,128)(2,1)S(1)} %copy-done.1, s32[1,3]{1,0:T(1,128)S(1)} %copy-done.12, s32[1,3]{1,0:T(1,128)S(1)} %copy-done.13, ...), custom_call_target="tpu_custom_call" | custom-call | tf_op jit(solution)/shard_map/pallas_call | solution.py:575
  53.9 0.1 shard_map.161
  54.0 0.1 collective-permute-start.7
  54.1 5.4 %collective-permute-start.8 = (bf16[9,128,256]{2,1,0:T(8,128)(2,1)S(1)}, bf16[9,128,256]{2,1,0:T(8,128)(2,1)S(1)}, u32[]{:S(2)}, u32[]{:S(2)}) collective-permute-start(bf16[9,128,256]{2,1,0:T(8,128)(2,1)S(1)} %get-tuple-element.101), channel_id=1, source_target_pairs={{1,2},{3,4},{5,6},{7,8},{9,10},{11,12},{13,14},{2,1},{4,3},{6,5},{... | collective-permute-start | bytes 1769480 | tf_op jit(solution)/shard_map/ppermute | solution.py:502
  59.4 0.0 collective-permute-done.7.refs_15_
  59.4 4.3 %shard_map.162 = (f32[4,128,256]{2,1,0:T(8,128)S(1)}, f32[4,128,256]{2,1,0:T(8,128)S(1)}, f32[4,128,256]{2,1,0:T(8,128)S(1)}, f32[4,128,256]{2,1,0:T(8,128)S(1)}, f32[8,2,128]{2,1,0:T(2,128)S(1)}) custom-call(bf16[512,256]{1,0:T(8,128)(2,1)S(1)} %copy-done, bf16[128,256]{1,0:T(8,128)(2,1)S(1)} %copy-done.1, s32[1,3]{1,0:T(1,128)S(1)} %copy-done.12, ...), custom_call_target="tpu_custom_call" | custom-call | tf_op jit(solution)/shard_map/pallas_call | solution.py:567
  63.7 5.2 %collective-permute-done.8.refs_10_ = bf16[9,128,256]{2,1,0:T(8,128)(2,1)S(1)} collective-permute-done((bf16[9,128,256]{2,1,0:T(8,128)(2,1)S(1)}, bf16[9,128,256]{2,1,0:T(8,128)(2,1)S(1)}, u32[]{:S(2)}, u32[]{:S(2)}) %collective-permute-start.8) | collective-permute-done | bytes 589856 | tf_op jit(solution)/shard_map/ppermute | solution.py:502
  68.9 1.5 %shard_map.163 = (f32[8,128,256]{2,1,0:T(8,128)S(1)}, f32[4,128,256]{2,1,0:T(8,128)S(1)}, f32[8,128,256]{2,1,0:T(8,128)S(1)}, bf16[9,128,256]{2,1,0:T(8,128)(2,1)S(1)}) custom-call(bf16[512,256]{1,0:T(8,128)(2,1)S(1)} %copy-done, bf16[128,256]{1,0:T(8,128)(2,1)S(1)} %copy-done.1, s32[1,3]{1,0:T(1,128)S(1)} %copy-done.12, s32[1,3]{1,0:T(1,128)S(1)} %copy-done.13, ...), custom_call_target="tpu_custom_call" | custom-call | tf_op jit(solution)/shard_map/pallas_call | solution.py:575
  70.3 0.1 shard_map.164
  70.4 0.1 collective-permute-start.9
  70.5 5.2 %collective-permute-start.10 = (bf16[9,128,256]{2,1,0:T(8,128)(2,1)S(1)}, bf16[9,128,256]{2,1,0:T(8,128)(2,1)S(1)}, u32[]{:S(2)}, u32[]{:S(2)}) collective-permute-start(bf16[9,128,256]{2,1,0:T(8,128)(2,1)S(1)} %get-tuple-element.110), channel_id=1, source_target_pairs={{1,2},{3,4},{5,6},{7,8},{9,10},{11,12},{13,14},{2,1},{4,3},{6,5},{... | collective-permute-start | bytes 1769480 | tf_op jit(solution)/shard_map/ppermute | solution.py:502
  75.7 0.0 collective-permute-done.9.refs_15_
  75.7 4.8 %shard_map.165 = (f32[4,128,256]{2,1,0:T(8,128)S(1)}, f32[4,128,256]{2,1,0:T(8,128)S(1)}, f32[4,128,256]{2,1,0:T(8,128)}, f32[4,128,256]{2,1,0:T(8,128)S(1)}, f32[8,2,128]{2,1,0:T(2,128)S(1)}) custom-call(bf16[512,256]{1,0:T(8,128)(2,1)S(1)} %copy-done, bf16[128,256]{1,0:T(8,128)(2,1)S(1)} %copy-done.1, s32[1,3]{1,0:T(1,128)S(1)} %copy-done.12, ...), custom_call_target="tpu_custom_call" | custom-call | tf_op jit(solution)/shard_map/pallas_call | solution.py:567
  80.5 4.8 %collective-permute-done.10.refs_18_ = bf16[9,128,256]{2,1,0:T(8,128)(2,1)S(1)} collective-permute-done((bf16[9,128,256]{2,1,0:T(8,128)(2,1)S(1)}, bf16[9,128,256]{2,1,0:T(8,128)(2,1)S(1)}, u32[]{:S(2)}, u32[]{:S(2)}) %collective-permute-start.10) | collective-permute-done | bytes 589856 | tf_op jit(solution)/shard_map/ppermute | solution.py:502
  85.3 3.1 %shard_map.166 = (f32[1,8,128,256]{3,2,1,0:T(8,128)}, f32[8,8,128]{2,1,0:T(8,128)S(1)}) custom-call(s32[1,64]{1,0:T(1,128)S(1)} %get-tuple-element.59.refs_5_.refs_0_, s32[1,1]{1,0:T(1,128)S(6)} %copy.20.count.refs_6_.refs_1_, s32[64,1]{1,0:T(8,128)S(1)} %get-tuple-element.60.refs_7_.refs_2_, f32[64,256]{1,0:T(8,128)S(1)} %get-tuple-element.61.refs_8_.refs_3_, ...), custom_call_target="tpu_custom_call" | custom-call | tf_op jit(solution)/shard_map/pallas_call | solution.py:580
  88.4 10.9 %all_to_all.10 = f32[8,8,128]{2,1,0:T(8,128)S(1)} all-to-all(f32[8,8,128]{2,1,0:T(8,128)S(1)} %get-tuple-element.115), channel_id=1, replica_groups=mesh['shot'=8,'space'=16] {'shot'}, dimensions={0} | all-to-all | bytes 65536 | tf_op jit(solution)/shard_map/all_to_all | solution.py:588
  99.4 0.6 reduce_sum.9
  (21 shorter events, 0.0 us)
Async XLA Ops:
  3.1 5.2 %copy-start.2 = (bf16[1,8,128,256]{3,2,1,0:T(8,128)(2,1)S(1)}, bf16[1,8,128,256]{3,2,1,0:T(8,128)(2,1)}, u32[]{:S(2)}) copy-start(bf16[1,8,128,256]{3,2,1,0:T(8,128)(2,1)} %cur.3) | copy-start | bytes 1572868
  3.1 5.3 %copy-start.3 = (bf16[1,8,128,256]{3,2,1,0:T(8,128)(2,1)S(1)}, bf16[1,8,128,256]{3,2,1,0:T(8,128)(2,1)}, u32[]{:S(2)}) copy-start(bf16[1,8,128,256]{3,2,1,0:T(8,128)(2,1)} %pri.3) | copy-start | bytes 1572868
  3.1 21.0 %all-to-all-start = ((bf16[8,8,64,128]{3,2,1,0:T(8,128)(2,1)}), bf16[8,8,64,128]{3,2,1,0:T(8,128)(2,1)S(1)}, u32[]{:S(2)}, u32[]{:S(2)}) async-start(bf16[8,8,64,128]{3,2,1,0:T(8,128)(2,1)} %shard_map.150), calls=%async_computation | async-start | bytes 2097152 | tf_op jit(solution)/shard_map/all_to_all | solution.py:520
  8.2 8.8 %copy-start = (bf16[512,256]{1,0:T(8,128)(2,1)S(1)}, bf16[512,256]{1,0:T(8,128)(2,1)}, u32[]{:S(2)}) copy-start(bf16[512,256]{1,0:T(8,128)(2,1)} %constant.6.clone.weights.refs_0_.refs_8_) | copy-start | bytes 786436
  8.3 8.8 %copy-start.1 = (bf16[128,256]{1,0:T(8,128)(2,1)S(1)}, bf16[128,256]{1,0:T(8,128)(2,1)}, u32[]{:S(2)}) copy-start(bf16[128,256]{1,0:T(8,128)(2,1)} %constant.7.clone.across.refs_1_.refs_9_) | copy-start | bytes 196612
  8.3 8.8 %collective-permute-start = (bf16[1,8,128,256]{3,2,1,0:T(8,128)(2,1)S(1)}, bf16[1,8,128,256]{3,2,1,0:T(8,128)(2,1)S(1)}, u32[]{:S(2)}, u32[]{:S(2)}) collective-permute-start(bf16[1,8,128,256]{3,2,1,0:T(8,128)(2,1)S(1)} %copy-done.2), channel_id=1, source_target_pairs={{0,1},{1,0},{2,3},{3,2},{4,5},{5,4},{6,7},{7,6},{8,9},{9,8},{10,11... | collective-permute-start | bytes 1572872 | tf_op jit(solution)/shard_map/ppermute | solution.py:526
  8.4 7.2 %copy-start.15 = (s32[8,8]{1,0:T(8,128)S(1)}, s32[8,8]{1,0:T(8,128)}, u32[]{:S(2)}) copy-start(s32[8,8]{1,0:T(8,128)} %wanted.1) | copy-start | bytes 772
  9.3 6.2 %copy-start.16 = (s32[64]{0:T(128)S(1)}, s32[64]{0:T(128)}, u32[]{:S(2)}) copy-start(s32[64]{0:T(128)} %home.1) | copy-start | bytes 772
  9.3 23.9 %collective-permute-start.2 = (bf16[12,128,256]{2,1,0:T(8,128)(2,1)}, bf16[12,128,256]{2,1,0:T(8,128)(2,1)}, u32[]{:S(2)}, u32[]{:S(2)}) collective-permute-start(bf16[12,128,256]{2,1,0:T(8,128)(2,1)} %get-tuple-element.68), channel_id=1, source_target_pairs={{1,2},{3,4},{5,6},{7,8},{9,10},{11,12},{13,14},{2,1},{4,3},{6,5},{... | collective-permute-start | bytes 2359304 | tf_op jit(solution)/shard_map/ppermute | solution.py:502
  15.4 1.6 %collective-permute-start.1 = (bf16[4,128,256]{2,1,0:T(8,128)(2,1)S(1)}, bf16[4,128,256]{2,1,0:T(8,128)(2,1)S(1)}, u32[]{:S(2)}, u32[]{:S(2)}) collective-permute-start(bf16[4,128,256]{2,1,0:T(8,128)(2,1)S(1)} %get-tuple-element.63), channel_id=1, source_target_pairs={{0,1},{1,0},{2,3},{3,2},{4,5},{5,4},{6,7},{7,6},{8,9},{9,8},{10,11... | collective-permute-start | bytes 786440 | tf_op jit(solution)/shard_map/ppermute | solution.py:502
  18.4 1.0 copy-start.4
  19.3 1.0 copy-start.6
  20.3 0.8 copy-start.8
  21.1 0.8 copy-start.10
  24.0 6.3 %copy-start.5 = (f32[8,128,256]{2,1,0:T(8,128)S(1)}, f32[8,128,256]{2,1,0:T(8,128)}, u32[]{:S(2)}) copy-start(f32[8,128,256]{2,1,0:T(8,128)} %copy-done.4) | copy-start | bytes 3145732
  24.9 5.4 %copy-start.12 = (s32[1,3]{1,0:T(1,128)S(1)}, s32[1,3]{1,0:T(1,128)}, u32[]{:S(2)}) copy-start(s32[1,3]{1,0:T(1,128)} %refs_10_.1) | copy-start | bytes 40
  24.9 5.4 %copy-start.13 = (s32[1,3]{1,0:T(1,128)S(1)}, s32[1,3]{1,0:T(1,128)}, u32[]{:S(2)}) copy-start(s32[1,3]{1,0:T(1,128)} %refs_11_.1) | copy-start | bytes 40
  25.0 5.4 %copy-start.14 = (f32[1,8]{1,0:T(1,128)S(1)}, f32[1,8]{1,0:T(1,128)}, u32[]{:S(2)}) copy-start(f32[1,8]{1,0:T(1,128)} %refs_12_.1) | copy-start | bytes 100
  25.0 11.4 %collective-permute-start.3 = (bf16[4,128,256]{2,1,0:T(8,128)(2,1)S(1)}, bf16[4,128,256]{2,1,0:T(8,128)(2,1)S(1)}, u32[]{:S(2)}, u32[]{:S(2)}) collective-permute-start(bf16[4,128,256]{2,1,0:T(8,128)(2,1)S(1)} %get-tuple-element.72.own_v_x), channel_id=1, source_target_pairs={{1,2},{3,4},{5,6},{7,8},{9,10},{11,12},{13,14},{2,1},{4,3},{6,5},{... | collective-permute-start | bytes 786440 | tf_op jit(solution)/shard_map/ppermute | solution.py:542
  30.3 1.2 %copy-start.7 = (f32[8,128,256]{2,1,0:T(8,128)S(1)}, f32[8,128,256]{2,1,0:T(8,128)}, u32[]{:S(2)}) copy-start(f32[8,128,256]{2,1,0:T(8,128)} %copy-done.6) | copy-start | bytes 3145732
  32.6 3.8 %collective-permute-start.4 = (bf16[4,128,256]{2,1,0:T(8,128)(2,1)S(1)}, bf16[4,128,256]{2,1,0:T(8,128)(2,1)S(1)}, u32[]{:S(2)}, u32[]{:S(2)}) collective-permute-start(bf16[4,128,256]{2,1,0:T(8,128)(2,1)S(1)} %get-tuple-element.83.own_v_in), channel_id=1, source_target_pairs={{0,1},{1,0},{2,3},{3,2},{4,5},{5,4},{6,7},{7,6},{8,9},{9,8},{10,11... | collective-permute-start | bytes 786440 | tf_op jit(solution)/shard_map/ppermute | solution.py:555
  33.3 3.1 %copy-start.9 = (f32[4,128,256]{2,1,0:T(8,128)S(1)}, f32[4,128,256]{2,1,0:T(8,128)}, u32[]{:S(2)}) copy-start(f32[4,128,256]{2,1,0:T(8,128)} %copy-done.8) | copy-start | bytes 1572868
  33.3 3.1 %copy-start.11 = (f32[4,128,256]{2,1,0:T(8,128)S(1)}, f32[4,128,256]{2,1,0:T(8,128)}, u32[]{:S(2)}) copy-start(f32[4,128,256]{2,1,0:T(8,128)} %copy-done.10) | copy-start | bytes 1572868
  37.5 6.0 %copy-start.18 = (s32[1,1,64,3]{2,1,3,0:T(1,128)S(1)}, s32[1,1,64,3]{2,1,3,0:T(1,128)}, u32[]{:S(2)}) copy-start(s32[1,1,64,3]{2,1,3,0:T(1,128)} %param.23) | copy-start | bytes 2308
  37.5 6.0 %copy-start.19 = (s32[1,1,64,3]{2,1,3,0:T(1,128)S(1)}, s32[1,1,64,3]{2,1,3,0:T(1,128)}, u32[]{:S(2)}) copy-start(s32[1,1,64,3]{2,1,3,0:T(1,128)} %param.22) | copy-start | bytes 2308
  37.5 6.9 %collective-permute-start.5 = (bf16[9,128,256]{2,1,0:T(8,128)(2,1)S(1)}, bf16[9,128,256]{2,1,0:T(8,128)(2,1)S(1)}, u32[]{:S(2)}, u32[]{:S(2)}) collective-permute-start(bf16[9,128,256]{2,1,0:T(8,128)(2,1)S(1)} %shard_map.158), channel_id=1, source_target_pairs={{0,1},{1,0},{2,3},{3,2},{4,5},{5,4},{6,7},{7,6},{8,9},{9,8},{10,11... | collective-permute-start | bytes 1769480 | tf_op jit(solution)/shard_map/ppermute | solution.py:502
  37.6 14.8 %collective-permute-start.6 = (bf16[9,128,256]{2,1,0:T(8,128)(2,1)S(1)}, bf16[9,128,256]{2,1,0:T(8,128)(2,1)S(1)}, u32[]{:S(2)}, u32[]{:S(2)}) collective-permute-start(bf16[9,128,256]{2,1,0:T(8,128)(2,1)S(1)} %get-tuple-element.92), channel_id=1, source_target_pairs={{1,2},{3,4},{5,6},{7,8},{9,10},{11,12},{13,14},{2,1},{4,3},{6,5},{... | collective-permute-start | bytes 1769480 | tf_op jit(solution)/shard_map/ppermute | solution.py:502
  43.5 0.7 copy-start.17
  54.0 5.5 %collective-permute-start.7 = (bf16[9,128,256]{2,1,0:T(8,128)(2,1)S(1)}, bf16[9,128,256]{2,1,0:T(8,128)(2,1)S(1)}, u32[]{:S(2)}, u32[]{:S(2)}) collective-permute-start(bf16[9,128,256]{2,1,0:T(8,128)(2,1)S(1)} %shard_map.161), channel_id=1, source_target_pairs={{0,1},{1,0},{2,3},{3,2},{4,5},{5,4},{6,7},{7,6},{8,9},{9,8},{10,11... | collective-permute-start | bytes 1769480 | tf_op jit(solution)/shard_map/ppermute | solution.py:502
  54.1 14.8 %collective-permute-start.8 = (bf16[9,128,256]{2,1,0:T(8,128)(2,1)S(1)}, bf16[9,128,256]{2,1,0:T(8,128)(2,1)S(1)}, u32[]{:S(2)}, u32[]{:S(2)}) collective-permute-start(bf16[9,128,256]{2,1,0:T(8,128)(2,1)S(1)} %get-tuple-element.101), channel_id=1, source_target_pairs={{1,2},{3,4},{5,6},{7,8},{9,10},{11,12},{13,14},{2,1},{4,3},{6,5},{... | collective-permute-start | bytes 1769480 | tf_op jit(solution)/shard_map/ppermute | solution.py:502
  70.4 5.3 %collective-permute-start.9 = (bf16[9,128,256]{2,1,0:T(8,128)(2,1)S(1)}, bf16[9,128,256]{2,1,0:T(8,128)(2,1)S(1)}, u32[]{:S(2)}, u32[]{:S(2)}) collective-permute-start(bf16[9,128,256]{2,1,0:T(8,128)(2,1)S(1)} %shard_map.164), channel_id=1, source_target_pairs={{0,1},{1,0},{2,3},{3,2},{4,5},{5,4},{6,7},{7,6},{8,9},{9,8},{10,11... | collective-permute-start | bytes 1769480 | tf_op jit(solution)/shard_map/ppermute | solution.py:502
  70.5 14.8 %collective-permute-start.10 = (bf16[9,128,256]{2,1,0:T(8,128)(2,1)S(1)}, bf16[9,128,256]{2,1,0:T(8,128)(2,1)S(1)}, u32[]{:S(2)}, u32[]{:S(2)}) collective-permute-start(bf16[9,128,256]{2,1,0:T(8,128)(2,1)S(1)} %get-tuple-element.110), channel_id=1, source_target_pairs={{1,2},{3,4},{5,6},{7,8},{9,10},{11,12},{13,14},{2,1},{4,3},{6,5},{... | collective-permute-start | bytes 1769480 | tf_op jit(solution)/shard_map/ppermute | solution.py:502

commit v4 on v3

--- a/solution.py
+++ b/solution.py
@@ -353,18 +353,18 @@
     )
 
 
-def send_kernel(near, u, out):
+def pack_send(u, out):
     for q in range(PL):
         out[q] = u[q].astype(bf16)
-    edge = u[near]
-    out[PL] = (edge - edge.astype(bf16).astype(f32)).astype(bf16)
+    if out.shape[0] > PL:
+        edge = u[0]
+        out[PL] = (edge - edge.astype(bf16).astype(f32)).astype(bf16)
 
 
 def far_kernel(
-    cell_any, frac_any, pulses_any, lead_x, sums_x, v_x, lead_in, sums_in, v_in, base, coef,
-    coef_x, coef_in, outer, inner, last, send_x, cell, frac, pulses, sems,
+    cell, frac, pulses, lead_x, sums_x, v_x, lead_in, sums_in, v_in, base, coef,
+    coef_x, coef_in, outer, inner, last, send_x,
 ):
-    source = fetch(((cell_any, cell), (frac_any, frac), (pulses_any, pulses)), sems)
     even = is_even()
     for j in range(4):
         for r in chunks():
@@ -374,7 +374,6 @@
             c = factor(v_in[3 - j, r])
             coef_in[j, r] = c
             inner[j, r] = lead_in[j, r] + c * sums_in[j, r]
-    wait(source)
     add_source(((outer, -1, True), (inner, PL, False)), even, cell, frac, pulses[0, 0])
     for q in range(PL):
         for r in chunks():
@@ -384,21 +383,17 @@
                 acc = depth(lambda e, r: inner[e - PL, r], q, PL, 12, r, 0.0)
             last[q, r] = base[q, r] + coef[q, r] * acc
     add_source(((last, 0, False),), even, cell, frac, pulses[0, 1])
-    send_kernel(0, last, send_x)
+    pack_send(last, send_x)
 
 
 def during_kernel(
     step, weights, across, cell_any, frac_any, pulses_any, codes, count, owner, spread, place, u, prev, prev_in, coef, coef_in, got_in,
-    part, own_hi, inner, base, gath, halo, rows, cell, frac, pulses, sems,
+    part, own_hi, inner, base, gath, rows, cell, frac, pulses, sems,
 ):
     source = fetch(((cell_any, cell), (frac_any, frac), (pulses_any, pulses)), sems)
     even = is_even()
-    for j in range(PL):
-        x = got_in[PL - 1 - j].astype(f32)
-        halo[j] = x + got_in[PL].astype(f32) if j == 0 else x
-
     def now(e, r):
-        return u[e, r] if e < PL else halo[e - PL, r]
+        return u[e, r] if e < PL else got_in[2 * PL - 1 - e, r]
 
     whole = slice(0, ROWS)
     for e in range(12):
@@ -427,7 +422,7 @@
     even = is_even()
     for j in range(PL):
         x = got_x[j].astype(f32)
-        halo[j] = x + got_x[PL].astype(f32) if j == 0 else x
+        halo[j] = x + got_x[PL].astype(f32) if j == 0 and got_x.shape[0] > PL else x
 
     def now(e, r):
         return halo[-1 - e, r] if e < 0 else u[e, r]
@@ -465,7 +460,7 @@
     source = (copies, cell, frac, pulses)
     after_kernel(step, weights, across, source, *refs[:-9], own, outer, last, halo)
     add_source(((last, 0, False),), is_even(), cell, frac, pulses[0, step + 1])
-    send_kernel(0, last, send_x)
+    pack_send(last, send_x)
 
 
 def last_kernel(
@@ -537,7 +532,7 @@
     )(weights, across, current_field, cur_in, prior_field, pri_in)
     arrived, sums, lead, u = lax.optimization_barrier((arrived, sums, lead, u))
     own_v_x, own_v_in = call(
-        assemble_kernel, [tile_planes, tile_planes], [SMEM, VMEM], limit=8 * MIB
+        assemble_kernel, [tile_planes, tile_planes], [VMEM, VMEM], limit=8 * MIB
     )(plan, arrived)
     v_x = lax.ppermute(own_v_x, "space", pair_x)
     source = (source_cell, source_frac, wavelet)
@@ -558,22 +553,21 @@
         [scratch8] + source_scratch, limit=16 * MIB,
     )(weights, across, *source, u, first_x, coef, part, own_hi, base)
     coef_x, coef_in, prev_x, prev_in, u, send_x = call(
-        far_kernel, [four, four, four, four, eight, send], source_specs + [VMEM] * 8, source_scratch, limit=16 * MIB
+        far_kernel, [four, four, four, four, eight, send], [VMEM] * 11, limit=16 * MIB
     )(*source, lead, total, v_x, lead_in, sums_in, v_in, base, coef)
     gaths = []
     for n in (2, 4, 6):
-        send_in = call(lambda *refs: send_kernel(PL - 1, *refs), [send], [VMEM], limit=4 * MIB)(u)[0]
-        got_x, got_in = swap(send_x, send_in)
+        got_x, got_in = swap(send_x, u)
         part, own_hi, inner, base, gath = call(
             lambda *refs, n=n: during_kernel(n, *refs), [four, four, four, four, ((8, 2, 128), f32)],
-            [VMEM] * 2 + source_specs + receiver_specs + [VMEM] * 6, [scratch8, rows] + source_scratch, limit=16 * MIB,
+            [VMEM] * 2 + source_specs + receiver_specs + [VMEM] * 6, [rows] + source_scratch, limit=16 * MIB,
         )(weights, across, *source, *receivers, u, prev, prev_in, coef, coef_in, got_in)
         gaths.append(gath)
         common = (weights, across, *source, u, prev, prev_x, coef, coef_x, got_x, part, own_hi, base)
         common_specs = [VMEM] * 2 + source_specs + [VMEM] * 9
         if n < 6:
             prev, prev_x, u, send_x = call(
-                lambda *refs, n=n: middle_kernel(n, *refs), [eight, four, eight, send], common_specs, [scratch8] + source_scratch, limit=16 * MIB
+                lambda *refs, n=n: middle_kernel(n, *refs), [eight, four, eight, send if n < 4 else ((PL,) + plane, bf16)], common_specs, [scratch8] + source_scratch, limit=16 * MIB
             )(*common)
             prev_in = inner
         else:

time: 100 us -> 99.3 us (level)
  Pallas kernels: 30.9 us -> 27.9 us
  waiting for transfers between devices: 17.5 us -> 19.4 us
    ppermute x4, waiting for transfers between devices: 14.2 us -> 16.4 us  [swap(): lax.ppermute(across_chips, 'space', pair_x)]
    pallas_call x3, Pallas kernels: 13.4 us -> 11.7 us  [on_device(): call(lambda *refs, n=n: during_kernel(n, *refs), [four, four, four, four,...]
    pallas_call x5 -> x2, Pallas kernels: 2.05 us -> 1.1 us  [the longest x1 0.69 us: on_device(): call(far_kernel, [four, four, four, four, eight, send], [VMEM] * 11, limi...]
  transfers between devices with their start and end apart: 12 -> 12, of which waited for: 7 -> 6; matrix products, arithmetic and copies ran while one was open for 0% -> 0% of each run, Pallas kernels for 21% -> 19%
where the time goes in v4:
time: 99.3 us; the launch traced here: 98.7 us
  starting transfers between devices  32.1 us (32%)
  Pallas kernels  27.9 us (28%)
  waiting for transfers between devices  19.4 us (20%)
  blocking collectives  11.5 us (12%)
  local copies, waits for them, and re-layouts  5.49 us (6%)
  between operations  1.74 us (2%)
    ppermute x4, starting transfers between devices, swap(): lax.ppermute(across_chips, 'space', pair_x)  21.1 us
    ppermute x4, waiting for transfers between devices, swap(): lax.ppermute(across_chips, 'space', pair_x)  16.4 us
    pallas_call x3, Pallas kernels, on_device(): call(lambda *refs, n=n: during_kernel(n, *refs), [four, four, four, four,...  11.7 us
    all_to_all x1, blocking collectives, on_device(): back = lax.all_to_all(gath, 'shot', split_axis=0, concat_axis=0, tiled=True)  11.5 us
    unnamed x40, local copies, waits for them, and re-layouts  5.49 us
    ppermute x1, starting transfers between devices, on_device(): v_x = lax.ppermute(own_v_x, 'space', pair_x)  5.32 us
    all_to_all x1, starting transfers between devices, on_device(): lax.all_to_all(out, 'shot', split_axis=0, concat_axis=0, tiled=True)  5.16 us
    pallas_call x2, Pallas kernels, on_device(): call(lambda *refs, n=n: middle_kernel(n, *refs), [eight, four, eight, sen...  3.11 us
  transfers between devices with their start and end apart: 12, of which 6 were waited for; matrix products, arithmetic and copies ran while one was open for 0% of the time, Pallas kernels for 19%

profile of v4, /device:TPU:16, one launch (start us, length us, event | category | flops | bytes accessed | tf_op | source)
XLA Modules:
  0.0 98.7 jit_solution(13935538351695247663)
XLA Ops:
  0.6 2.4 %shard_map.150 = bf16[8,8,64,128]{3,2,1,0:T(8,128)(2,1)} custom-call(s32[64]{0:T(128)} %home.1, s32[8,8]{1,0:T(8,128)} %wanted.1, bf16[8,8,64,64]{3,2,1,0:T(8,128)(2,1)} %store_hbm.1), custom_call_target="tpu_custom_call" | custom-call | tf_op jit(solution)/shard_map/pallas_call | solution.py:508
  3.1 0.0 copy-start.2
  3.1 0.0 copy-start.3
  3.1 5.2 %all-to-all-start = ((bf16[8,8,64,128]{3,2,1,0:T(8,128)(2,1)}), bf16[8,8,64,128]{3,2,1,0:T(8,128)(2,1)S(1)}, u32[]{:S(2)}, u32[]{:S(2)}) async-start(bf16[8,8,64,128]{3,2,1,0:T(8,128)(2,1)} %shard_map.150), calls=%async_computation | async-start | bytes 2097152 | tf_op jit(solution)/shard_map/all_to_all | solution.py:515
  8.2 0.0 copy-done.2
  8.2 0.0 copy-start
  8.3 0.0 copy-start.1
  8.3 0.1 collective-permute-start
  8.4 0.0 copy-done.3
  8.4 0.0 copy-start.15
  8.4 0.9 shard_map.151
  9.3 0.0 copy-start.16
  9.3 6.1 %collective-permute-start.2 = (bf16[12,128,256]{2,1,0:T(8,128)(2,1)}, bf16[12,128,256]{2,1,0:T(8,128)(2,1)}, u32[]{:S(2)}, u32[]{:S(2)}) collective-permute-start(bf16[12,128,256]{2,1,0:T(8,128)(2,1)} %get-tuple-element.68), channel_id=1, source_target_pairs={{1,2},{3,4},{5,6},{7,8},{9,10},{11,12},{13,14},{2,1},{4,3},{6,5},{... | collective-permute-start | bytes 2359304 | tf_op jit(solution)/shard_map/ppermute | solution.py:497
  15.4 0.1 collective-permute-start.1
  15.5 0.0 copy-done.15
  15.5 0.0 copy-done.16
  15.5 0.7 shard_map.153.plan
  16.2 0.8 collective-permute-done.1.pri_in
  17.0 0.0 collective-permute-done.cur_in
  17.1 1.3 %shard_map.152 = (f32[8,128,256]{2,1,0:T(8,128)S(1)}, f32[8,128,256]{2,1,0:T(8,128)S(1)}, f32[4,128,256]{2,1,0:T(8,128)S(1)}, f32[4,128,256]{2,1,0:T(8,128)S(1)}, f32[8,128,256]{2,1,0:T(8,128)S(1)}) custom-call(bf16[512,256]{1,0:T(8,128)(2,1)S(1)} %copy-done, bf16[128,256]{1,0:T(8,128)(2,1)S(1)} %copy-done.1, bf16[1,8,128,256]{3,2,1,0:T(8,128)(2,1)S(1)} %copy-done.2, ...), custom_call_target="tpu_custom_call" | custom-call | tf_op jit(solution)/shard_map/pallas_call | solution.py:530
  18.4 0.0 copy-start.4
  18.4 1.0 copy-done.4
  19.3 1.0 copy-done.6
  20.3 0.8 copy-done.8
  21.1 0.8 copy-done.10
  21.9 2.1 %all-to-all-done.arrived = bf16[8,8,64,128]{3,2,1,0:T(8,128)(2,1)S(1)} async-done(((bf16[8,8,64,128]{3,2,1,0:T(8,128)(2,1)}), bf16[8,8,64,128]{3,2,1,0:T(8,128)(2,1)S(1)}, u32[]{:S(2)}, u32[]{:S(2)}) %all-to-all-start) | async-done | bytes 1048608 | tf_op jit(solution)/shard_map/all_to_all | solution.py:515
  24.0 0.4 shard_map.154
  24.5 0.0 copy-start.12
  24.5 0.0 copy-start.13
  24.5 0.0 copy-start.14
  24.5 5.3 %collective-permute-start.3 = (bf16[4,128,256]{2,1,0:T(8,128)(2,1)S(1)}, bf16[4,128,256]{2,1,0:T(8,128)(2,1)S(1)}, u32[]{:S(2)}, u32[]{:S(2)}) collective-permute-start(bf16[4,128,256]{2,1,0:T(8,128)(2,1)S(1)} %get-tuple-element.72.own_v_x), channel_id=1, source_target_pairs={{1,2},{3,4},{5,6},{7,8},{9,10},{11,12},{13,14},{2,1},{4,3},{6,5},{... | collective-permute-start | bytes 786440 | tf_op jit(solution)/shard_map/ppermute | solution.py:537
  29.9 1.2 %copy-done.7 = f32[8,128,256]{2,1,0:T(8,128)S(1)} copy-done((f32[8,128,256]{2,1,0:T(8,128)S(1)}, f32[8,128,256]{2,1,0:T(8,128)}, u32[]{:S(2)}) %copy-start.7) | copy-done | bytes 1048600
  31.1 1.1 %shard_map.155 = (f32[8,128,256]{2,1,0:T(8,128)S(1)}, f32[4,128,256]{2,1,0:T(8,128)S(1)}, f32[4,128,256]{2,1,0:T(8,128)S(1)}, f32[4,128,256]{2,1,0:T(8,128)S(1)}) custom-call(bf16[512,256]{1,0:T(8,128)(2,1)S(1)} %copy-done, bf16[128,256]{1,0:T(8,128)(2,1)S(1)} %copy-done.1, s32[1,3]{1,0:T(1,128)S(1)} %copy-done.12, s32[1,3]{1,0:T(1,128)S(1)} %copy-done.13, ...), custom_call_target="tpu_custom_call" | custom-call | tf_op jit(solution)/shard_map/pallas_call | solution.py:545
  32.2 0.1 collective-permute-start.4
  32.2 1.0 %collective-permute-done.2.got_x = bf16[12,128,256]{2,1,0:T(8,128)(2,1)} collective-permute-done((bf16[12,128,256]{2,1,0:T(8,128)(2,1)}, bf16[12,128,256]{2,1,0:T(8,128)(2,1)}, u32[]{:S(2)}, u32[]{:S(2)}) %collective-permute-start.2) | collective-permute-done | bytes 786464 | tf_op jit(solution)/shard_map/ppermute | solution.py:497
  33.3 2.8 %shard_map.156 = (f32[8,128,256]{2,1,0:T(8,128)S(1)}, f32[8,128,256]{2,1,0:T(8,128)S(1)}, f32[4,128,256]{2,1,0:T(8,128)S(1)}, f32[4,128,256]{2,1,0:T(8,128)S(1)}) custom-call(bf16[512,256]{1,0:T(8,128)(2,1)S(1)} %copy-done, bf16[128,256]{1,0:T(8,128)(2,1)S(1)} %copy-done.1, s32[1,3]{1,0:T(1,128)S(1)} %copy-done.12, s32[1,3]{1,0:T(1,128)S(1)} %copy-done.13, ...), custom_call_target="tpu_custom_call" | custom-call | tf_op jit(solution)/shard_map/pallas_call | solution.py:551
  36.1 0.0 collective-permute-done.3.v_x
  36.1 0.0 collective-permute-done.4.v_in
  36.1 0.7 shard_map.157
  36.8 0.0 copy-start.18
  36.8 0.0 copy-start.19
  36.8 0.1 collective-permute-start.5
  36.9 5.0 %collective-permute-start.6 = (bf16[9,128,256]{2,1,0:T(8,128)(2,1)S(1)}, bf16[9,128,256]{2,1,0:T(8,128)(2,1)S(1)}, u32[]{:S(2)}, u32[]{:S(2)}) collective-permute-start(bf16[9,128,256]{2,1,0:T(8,128)(2,1)S(1)} %get-tuple-element.92), channel_id=1, source_target_pairs={{1,2},{3,4},{5,6},{7,8},{9,10},{11,12},{13,14},{2,1},{4,3},{6,5},{... | collective-permute-start | bytes 1769480 | tf_op jit(solution)/shard_map/ppermute | solution.py:497
  42.6 0.0 copy-start.17
  42.6 0.6 copy-done.17
  43.3 0.3 shard_map.149
  43.6 0.0 collective-permute-done.5.refs_15_
  43.6 3.7 %shard_map.158 = (f32[4,128,256]{2,1,0:T(8,128)S(1)}, f32[4,128,256]{2,1,0:T(8,128)S(1)}, f32[4,128,256]{2,1,0:T(8,128)S(1)}, f32[4,128,256]{2,1,0:T(8,128)S(1)}, f32[8,2,128]{2,1,0:T(2,128)S(1)}) custom-call(bf16[512,256]{1,0:T(8,128)(2,1)S(1)} %copy-done, bf16[128,256]{1,0:T(8,128)(2,1)S(1)} %copy-done.1, s32[1,3]{1,0:T(1,128)S(1)} %copy-done.12, ...), custom_call_target="tpu_custom_call" | custom-call | tf_op jit(solution)/shard_map/pallas_call | solution.py:561
  47.3 4.4 %collective-permute-done.6.refs_10_ = bf16[9,128,256]{2,1,0:T(8,128)(2,1)S(1)} collective-permute-done((bf16[9,128,256]{2,1,0:T(8,128)(2,1)S(1)}, bf16[9,128,256]{2,1,0:T(8,128)(2,1)S(1)}, u32[]{:S(2)}, u32[]{:S(2)}) %collective-permute-start.6) | collective-permute-done | bytes 589856 | tf_op jit(solution)/shard_map/ppermute | solution.py:497
  51.7 1.6 %shard_map.159 = (f32[8,128,256]{2,1,0:T(8,128)S(1)}, f32[4,128,256]{2,1,0:T(8,128)S(1)}, f32[8,128,256]{2,1,0:T(8,128)S(1)}, bf16[9,128,256]{2,1,0:T(8,128)(2,1)S(1)}) custom-call(bf16[512,256]{1,0:T(8,128)(2,1)S(1)} %copy-done, bf16[128,256]{1,0:T(8,128)(2,1)S(1)} %copy-done.1, s32[1,3]{1,0:T(1,128)S(1)} %copy-done.12, s32[1,3]{1,0:T(1,128)S(1)} %copy-done.13, ...), custom_call_target="tpu_custom_call" | custom-call | tf_op jit(solution)/shard_map/pallas_call | solution.py:569
  53.4 0.1 collective-permute-start.7
  53.5 5.0 %collective-permute-start.8 = (bf16[9,128,256]{2,1,0:T(8,128)(2,1)S(1)}, bf16[9,128,256]{2,1,0:T(8,128)(2,1)S(1)}, u32[]{:S(2)}, u32[]{:S(2)}) collective-permute-start(bf16[9,128,256]{2,1,0:T(8,128)(2,1)S(1)} %get-tuple-element.101), channel_id=1, source_target_pairs={{1,2},{3,4},{5,6},{7,8},{9,10},{11,12},{13,14},{2,1},{4,3},{6,5},{... | collective-permute-start | bytes 1769480 | tf_op jit(solution)/shard_map/ppermute | solution.py:497
  58.5 0.0 collective-permute-done.7.refs_15_
  58.5 3.9 %shard_map.160 = (f32[4,128,256]{2,1,0:T(8,128)S(1)}, f32[4,128,256]{2,1,0:T(8,128)S(1)}, f32[4,128,256]{2,1,0:T(8,128)S(1)}, f32[4,128,256]{2,1,0:T(8,128)S(1)}, f32[8,2,128]{2,1,0:T(2,128)S(1)}) custom-call(bf16[512,256]{1,0:T(8,128)(2,1)S(1)} %copy-done, bf16[128,256]{1,0:T(8,128)(2,1)S(1)} %copy-done.1, s32[1,3]{1,0:T(1,128)S(1)} %copy-done.12, ...), custom_call_target="tpu_custom_call" | custom-call | tf_op jit(solution)/shard_map/pallas_call | solution.py:561
  62.4 5.9 %collective-permute-done.8.refs_10_ = bf16[9,128,256]{2,1,0:T(8,128)(2,1)S(1)} collective-permute-done((bf16[9,128,256]{2,1,0:T(8,128)(2,1)S(1)}, bf16[9,128,256]{2,1,0:T(8,128)(2,1)S(1)}, u32[]{:S(2)}, u32[]{:S(2)}) %collective-permute-start.8) | collective-permute-done | bytes 589856 | tf_op jit(solution)/shard_map/ppermute | solution.py:497
  68.3 1.5 %shard_map.161 = (f32[8,128,256]{2,1,0:T(8,128)S(1)}, f32[4,128,256]{2,1,0:T(8,128)S(1)}, f32[8,128,256]{2,1,0:T(8,128)S(1)}, bf16[8,128,256]{2,1,0:T(8,128)(2,1)S(1)}) custom-call(bf16[512,256]{1,0:T(8,128)(2,1)S(1)} %copy-done, bf16[128,256]{1,0:T(8,128)(2,1)S(1)} %copy-done.1, s32[1,3]{1,0:T(1,128)S(1)} %copy-done.12, s32[1,3]{1,0:T(1,128)S(1)} %copy-done.13, ...), custom_call_target="tpu_custom_call" | custom-call | tf_op jit(solution)/shard_map/pallas_call | solution.py:569
  69.8 0.1 collective-permute-start.9
  69.9 5.0 %collective-permute-start.10 = (bf16[8,128,256]{2,1,0:T(8,128)(2,1)S(1)}, bf16[8,128,256]{2,1,0:T(8,128)(2,1)S(1)}, u32[]{:S(2)}, u32[]{:S(2)}) collective-permute-start(bf16[8,128,256]{2,1,0:T(8,128)(2,1)S(1)} %get-tuple-element.110), channel_id=1, source_target_pairs={{1,2},{3,4},{5,6},{7,8},{9,10},{11,12},{13,14},{2,1},{4,3},{6,5},{... | collective-permute-start | bytes 1572872 | tf_op jit(solution)/shard_map/ppermute | solution.py:497
  74.9 0.0 collective-permute-done.9.refs_15_
  74.9 4.1 %shard_map.162 = (f32[4,128,256]{2,1,0:T(8,128)S(1)}, f32[4,128,256]{2,1,0:T(8,128)S(1)}, f32[4,128,256]{2,1,0:T(8,128)}, f32[4,128,256]{2,1,0:T(8,128)S(1)}, f32[8,2,128]{2,1,0:T(2,128)S(1)}) custom-call(bf16[512,256]{1,0:T(8,128)(2,1)S(1)} %copy-done, bf16[128,256]{1,0:T(8,128)(2,1)S(1)} %copy-done.1, s32[1,3]{1,0:T(1,128)S(1)} %copy-done.12, ...), custom_call_target="tpu_custom_call" | custom-call | tf_op jit(solution)/shard_map/pallas_call | solution.py:561
  79.0 5.0 %collective-permute-done.10.refs_18_ = bf16[8,128,256]{2,1,0:T(8,128)(2,1)S(1)} collective-permute-done((bf16[8,128,256]{2,1,0:T(8,128)(2,1)S(1)}, bf16[8,128,256]{2,1,0:T(8,128)(2,1)S(1)}, u32[]{:S(2)}, u32[]{:S(2)}) %collective-permute-start.10) | collective-permute-done | bytes 524320 | tf_op jit(solution)/shard_map/ppermute | solution.py:497
  84.0 2.6 %shard_map.163 = (f32[1,8,128,256]{3,2,1,0:T(8,128)}, f32[8,8,128]{2,1,0:T(8,128)S(1)}) custom-call(s32[1,64]{1,0:T(1,128)S(1)} %get-tuple-element.59.refs_5_.refs_0_, s32[1,1]{1,0:T(1,128)S(6)} %copy.20.count.refs_6_.refs_1_, s32[64,1]{1,0:T(8,128)S(1)} %get-tuple-element.60.refs_7_.refs_2_, f32[64,256]{1,0:T(8,128)S(1)} %get-tuple-element.61.refs_8_.refs_3_, ...), custom_call_target="tpu_custom_call" | custom-call | tf_op jit(solution)/shard_map/pallas_call | solution.py:574
  86.6 11.5 %all_to_all.10 = f32[8,8,128]{2,1,0:T(8,128)S(1)} all-to-all(f32[8,8,128]{2,1,0:T(8,128)S(1)} %get-tuple-element.115), channel_id=1, replica_groups=mesh['shot'=8,'space'=16] {'shot'}, dimensions={0} | all-to-all | bytes 65536 | tf_op jit(solution)/shard_map/all_to_all | solution.py:582
  98.1 0.6 reduce_sum.9
  (18 shorter events, 0.0 us)
Async XLA Ops:
  3.1 5.2 %copy-start.2 = (bf16[1,8,128,256]{3,2,1,0:T(8,128)(2,1)S(1)}, bf16[1,8,128,256]{3,2,1,0:T(8,128)(2,1)}, u32[]{:S(2)}) copy-start(bf16[1,8,128,256]{3,2,1,0:T(8,128)(2,1)} %cur.3) | copy-start | bytes 1572868
  3.1 5.3 %copy-start.3 = (bf16[1,8,128,256]{3,2,1,0:T(8,128)(2,1)S(1)}, bf16[1,8,128,256]{3,2,1,0:T(8,128)(2,1)}, u32[]{:S(2)}) copy-start(bf16[1,8,128,256]{3,2,1,0:T(8,128)(2,1)} %pri.3) | copy-start | bytes 1572868
  3.1 21.0 %all-to-all-start = ((bf16[8,8,64,128]{3,2,1,0:T(8,128)(2,1)}), bf16[8,8,64,128]{3,2,1,0:T(8,128)(2,1)S(1)}, u32[]{:S(2)}, u32[]{:S(2)}) async-start(bf16[8,8,64,128]{3,2,1,0:T(8,128)(2,1)} %shard_map.150), calls=%async_computation | async-start | bytes 2097152 | tf_op jit(solution)/shard_map/all_to_all | solution.py:515
  8.2 8.8 %copy-start = (bf16[512,256]{1,0:T(8,128)(2,1)S(1)}, bf16[512,256]{1,0:T(8,128)(2,1)}, u32[]{:S(2)}) copy-start(bf16[512,256]{1,0:T(8,128)(2,1)} %constant.6.clone.weights.refs_0_.refs_8_) | copy-start | bytes 786436
  8.3 8.8 %copy-start.1 = (bf16[128,256]{1,0:T(8,128)(2,1)S(1)}, bf16[128,256]{1,0:T(8,128)(2,1)}, u32[]{:S(2)}) copy-start(bf16[128,256]{1,0:T(8,128)(2,1)} %constant.7.clone.across.refs_1_.refs_9_) | copy-start | bytes 196612
  8.3 8.8 %collective-permute-start = (bf16[1,8,128,256]{3,2,1,0:T(8,128)(2,1)S(1)}, bf16[1,8,128,256]{3,2,1,0:T(8,128)(2,1)S(1)}, u32[]{:S(2)}, u32[]{:S(2)}) collective-permute-start(bf16[1,8,128,256]{3,2,1,0:T(8,128)(2,1)S(1)} %copy-done.2), channel_id=1, source_target_pairs={{0,1},{1,0},{2,3},{3,2},{4,5},{5,4},{6,7},{7,6},{8,9},{9,8},{10,11... | collective-permute-start | bytes 1572872 | tf_op jit(solution)/shard_map/ppermute | solution.py:521
  8.4 7.2 %copy-start.15 = (s32[8,8]{1,0:T(8,128)S(1)}, s32[8,8]{1,0:T(8,128)}, u32[]{:S(2)}) copy-start(s32[8,8]{1,0:T(8,128)} %wanted.1) | copy-start | bytes 772
  9.3 6.2 %copy-start.16 = (s32[64]{0:T(128)S(1)}, s32[64]{0:T(128)}, u32[]{:S(2)}) copy-start(s32[64]{0:T(128)} %home.1) | copy-start | bytes 772
  9.3 23.9 %collective-permute-start.2 = (bf16[12,128,256]{2,1,0:T(8,128)(2,1)}, bf16[12,128,256]{2,1,0:T(8,128)(2,1)}, u32[]{:S(2)}, u32[]{:S(2)}) collective-permute-start(bf16[12,128,256]{2,1,0:T(8,128)(2,1)} %get-tuple-element.68), channel_id=1, source_target_pairs={{1,2},{3,4},{5,6},{7,8},{9,10},{11,12},{13,14},{2,1},{4,3},{6,5},{... | collective-permute-start | bytes 2359304 | tf_op jit(solution)/shard_map/ppermute | solution.py:497
  15.4 1.6 %collective-permute-start.1 = (bf16[4,128,256]{2,1,0:T(8,128)(2,1)S(1)}, bf16[4,128,256]{2,1,0:T(8,128)(2,1)S(1)}, u32[]{:S(2)}, u32[]{:S(2)}) collective-permute-start(bf16[4,128,256]{2,1,0:T(8,128)(2,1)S(1)} %get-tuple-element.63), channel_id=1, source_target_pairs={{0,1},{1,0},{2,3},{3,2},{4,5},{5,4},{6,7},{7,6},{8,9},{9,8},{10,11... | collective-permute-start | bytes 786440 | tf_op jit(solution)/shard_map/ppermute | solution.py:497
  18.4 1.0 copy-start.4
  19.3 1.0 copy-start.6
  20.3 0.8 copy-start.8
  21.1 0.8 copy-start.10
  24.0 5.8 %copy-start.5 = (f32[8,128,256]{2,1,0:T(8,128)S(1)}, f32[8,128,256]{2,1,0:T(8,128)}, u32[]{:S(2)}) copy-start(f32[8,128,256]{2,1,0:T(8,128)} %copy-done.4) | copy-start | bytes 3145732
  24.5 5.4 %copy-start.12 = (s32[1,3]{1,0:T(1,128)S(1)}, s32[1,3]{1,0:T(1,128)}, u32[]{:S(2)}) copy-start(s32[1,3]{1,0:T(1,128)} %refs_10_.1) | copy-start | bytes 40
  24.5 5.4 %copy-start.13 = (s32[1,3]{1,0:T(1,128)S(1)}, s32[1,3]{1,0:T(1,128)}, u32[]{:S(2)}) copy-start(s32[1,3]{1,0:T(1,128)} %refs_11_.1) | copy-start | bytes 40
  24.5 5.4 %copy-start.14 = (f32[1,8]{1,0:T(1,128)S(1)}, f32[1,8]{1,0:T(1,128)}, u32[]{:S(2)}) copy-start(f32[1,8]{1,0:T(1,128)} %refs_12_.1) | copy-start | bytes 100
  24.5 11.6 %collective-permute-start.3 = (bf16[4,128,256]{2,1,0:T(8,128)(2,1)S(1)}, bf16[4,128,256]{2,1,0:T(8,128)(2,1)S(1)}, u32[]{:S(2)}, u32[]{:S(2)}) collective-permute-start(bf16[4,128,256]{2,1,0:T(8,128)(2,1)S(1)} %get-tuple-element.72.own_v_x), channel_id=1, source_target_pairs={{1,2},{3,4},{5,6},{7,8},{9,10},{11,12},{13,14},{2,1},{4,3},{6,5},{... | collective-permute-start | bytes 786440 | tf_op jit(solution)/shard_map/ppermute | solution.py:537
  29.9 1.2 %copy-start.7 = (f32[8,128,256]{2,1,0:T(8,128)S(1)}, f32[8,128,256]{2,1,0:T(8,128)}, u32[]{:S(2)}) copy-start(f32[8,128,256]{2,1,0:T(8,128)} %copy-done.6) | copy-start | bytes 3145732
  32.2 3.9 %collective-permute-start.4 = (bf16[4,128,256]{2,1,0:T(8,128)(2,1)S(1)}, bf16[4,128,256]{2,1,0:T(8,128)(2,1)S(1)}, u32[]{:S(2)}, u32[]{:S(2)}) collective-permute-start(bf16[4,128,256]{2,1,0:T(8,128)(2,1)S(1)} %get-tuple-element.83.own_v_in), channel_id=1, source_target_pairs={{0,1},{1,0},{2,3},{3,2},{4,5},{5,4},{6,7},{7,6},{8,9},{9,8},{10,11... | collective-permute-start | bytes 786440 | tf_op jit(solution)/shard_map/ppermute | solution.py:550
  33.3 2.8 %copy-start.9 = (f32[4,128,256]{2,1,0:T(8,128)S(1)}, f32[4,128,256]{2,1,0:T(8,128)}, u32[]{:S(2)}) copy-start(f32[4,128,256]{2,1,0:T(8,128)} %copy-done.8) | copy-start | bytes 1572868
  33.3 2.8 %copy-start.11 = (f32[4,128,256]{2,1,0:T(8,128)S(1)}, f32[4,128,256]{2,1,0:T(8,128)}, u32[]{:S(2)}) copy-start(f32[4,128,256]{2,1,0:T(8,128)} %copy-done.10) | copy-start | bytes 1572868
  36.8 5.8 %copy-start.18 = (s32[1,1,64,3]{2,1,3,0:T(1,128)S(1)}, s32[1,1,64,3]{2,1,3,0:T(1,128)}, u32[]{:S(2)}) copy-start(s32[1,1,64,3]{2,1,3,0:T(1,128)} %param.23) | copy-start | bytes 2308
  36.8 5.8 %copy-start.19 = (s32[1,1,64,3]{2,1,3,0:T(1,128)S(1)}, s32[1,1,64,3]{2,1,3,0:T(1,128)}, u32[]{:S(2)}) copy-start(s32[1,1,64,3]{2,1,3,0:T(1,128)} %param.22) | copy-start | bytes 2308
  36.8 6.8 %collective-permute-start.5 = (f32[8,128,256]{2,1,0:T(8,128)S(1)}, f32[8,128,256]{2,1,0:T(8,128)S(1)}, u32[]{:S(2)}, u32[]{:S(2)}) collective-permute-start(f32[8,128,256]{2,1,0:T(8,128)S(1)} %get-tuple-element.85.refs_10_.refs_5_), channel_id=1, source_target_pairs={{0,1},{1,0},{2,3},{3,2},{4,5},{5,4},{6,7},{7,6},{8,9},{9,8},{10,11... | collective-permute-start | bytes 3145736 | tf_op jit(solution)/shard_map/ppermute | solution.py:497
  36.9 14.8 %collective-permute-start.6 = (bf16[9,128,256]{2,1,0:T(8,128)(2,1)S(1)}, bf16[9,128,256]{2,1,0:T(8,128)(2,1)S(1)}, u32[]{:S(2)}, u32[]{:S(2)}) collective-permute-start(bf16[9,128,256]{2,1,0:T(8,128)(2,1)S(1)} %get-tuple-element.92), channel_id=1, source_target_pairs={{1,2},{3,4},{5,6},{7,8},{9,10},{11,12},{13,14},{2,1},{4,3},{6,5},{... | collective-permute-start | bytes 1769480 | tf_op jit(solution)/shard_map/ppermute | solution.py:497
  42.6 0.7 copy-start.17
  53.4 5.1 %collective-permute-start.7 = (f32[8,128,256]{2,1,0:T(8,128)S(1)}, f32[8,128,256]{2,1,0:T(8,128)S(1)}, u32[]{:S(2)}, u32[]{:S(2)}) collective-permute-start(f32[8,128,256]{2,1,0:T(8,128)S(1)} %get-tuple-element.96.refs_10_.refs_5_), channel_id=1, source_target_pairs={{0,1},{1,0},{2,3},{3,2},{4,5},{5,4},{6,7},{7,6},{8,9},{9,8},{10,11... | collective-permute-start | bytes 3145736 | tf_op jit(solution)/shard_map/ppermute | solution.py:497
  53.5 14.8 %collective-permute-start.8 = (bf16[9,128,256]{2,1,0:T(8,128)(2,1)S(1)}, bf16[9,128,256]{2,1,0:T(8,128)(2,1)S(1)}, u32[]{:S(2)}, u32[]{:S(2)}) collective-permute-start(bf16[9,128,256]{2,1,0:T(8,128)(2,1)S(1)} %get-tuple-element.101), channel_id=1, source_target_pairs={{1,2},{3,4},{5,6},{7,8},{9,10},{11,12},{13,14},{2,1},{4,3},{6,5},{... | collective-permute-start | bytes 1769480 | tf_op jit(solution)/shard_map/ppermute | solution.py:497
  69.8 5.1 %collective-permute-start.9 = (f32[8,128,256]{2,1,0:T(8,128)S(1)}, f32[8,128,256]{2,1,0:T(8,128)S(1)}, u32[]{:S(2)}, u32[]{:S(2)}) collective-permute-start(f32[8,128,256]{2,1,0:T(8,128)S(1)} %get-tuple-element.105.refs_10_.refs_13_), channel_id=1, source_target_pairs={{0,1},{1,0},{2,3},{3,2},{4,5},{5,4},{6,7},{7,6},{8,9},{9,8},{10,11... | collective-permute-start | bytes 3145736 | tf_op jit(solution)/shard_map/ppermute | solution.py:497
  69.9 14.1 %collective-permute-start.10 = (bf16[8,128,256]{2,1,0:T(8,128)(2,1)S(1)}, bf16[8,128,256]{2,1,0:T(8,128)(2,1)S(1)}, u32[]{:S(2)}, u32[]{:S(2)}) collective-permute-start(bf16[8,128,256]{2,1,0:T(8,128)(2,1)S(1)} %get-tuple-element.110), channel_id=1, source_target_pairs={{1,2},{3,4},{5,6},{7,8},{9,10},{11,12},{13,14},{2,1},{4,3},{6,5},{... | collective-permute-start | bytes 1572872 | tf_op jit(solution)/shard_map/ppermute | solution.py:497

commit v5 on v4

--- a/solution.py
+++ b/solution.py
@@ -128,20 +128,19 @@
     return jnp.concatenate([x[:, EDGE:], x[:, :EDGE]], 1)
 
 
-def assemble_kernel(plan, arrived, v_x, v_in):
+def assemble_kernel(first, plan, arrived, out):
     left = lax.broadcasted_iota(jnp.int32, (EDGE, 2 * EDGE), 1) < EDGE
     owners = [plan[0, j] for j in range(8)]
     ranks = [plan[0, 8 + j] for j in range(8)]
     for j in range(0, 8, 2):
         rows = slice(j // 4 * EDGE, (j // 4 + 1) * EDGE)
         lanes = slice(j % 4 * EDGE, (j % 4 + 2) * EDGE)
-        for q in range(PL):
-            x = arrived[owners[j], q]
-            y = arrived[owners[j + 1], q]
+        for q in range(4):
+            x = arrived[owners[j], first + q]
+            y = arrived[owners[j + 1], first + q]
             x = jnp.where(ranks[j] == 0, x, swapped(x))
             y = jnp.where(ranks[j + 1] == 0, swapped(y), y)
-            out = v_x if q < 4 else v_in
-            out[q % 4, rows, lanes] = jnp.where(left, x, y)
+            out[q, rows, lanes] = jnp.where(left, x, y)
 
 
 CHUNK = 16
@@ -275,10 +274,11 @@
 
 
 def near_kernel(
-    weights, across, cell_any, frac_any, pulses_any, u, sums, lead, own_v_x, own_v_in,
-    coef, part, own_hi, base, cell, frac, pulses, sems,
+    weights, across, cell_any, frac_any, pulses_any, u, sums, lead, own_v_x, plan, arrived,
+    own_v_in, coef, part, own_hi, base, cell, frac, pulses, sems,
 ):
     source = fetch(((cell_any, cell), (frac_any, frac), (pulses_any, pulses)), sems)
+    assemble_kernel(4, plan, arrived, own_v_in)
     for e in range(PL):
         for r in chunks():
             c = factor((own_v_x if e < 4 else own_v_in)[e % 4, r])
@@ -461,6 +461,13 @@
     after_kernel(step, weights, across, source, *refs[:-9], own, outer, last, halo)
     add_source(((last, 0, False),), is_even(), cell, frac, pulses[0, step + 1])
     pack_send(last, send_x)
+
+
+def gather_kernel(back, out):
+    total = back[0]
+    for s in range(1, 8):
+        total = total + back[s]
+    out[0, 0] = total
 
 
 def last_kernel(
@@ -531,9 +538,7 @@
         open_kernel, [eight, eight, four, four, eight], [VMEM] * 6, [scratch8], limit=16 * MIB
     )(weights, across, current_field, cur_in, prior_field, pri_in)
     arrived, sums, lead, u = lax.optimization_barrier((arrived, sums, lead, u))
-    own_v_x, own_v_in = call(
-        assemble_kernel, [tile_planes, tile_planes], [VMEM, VMEM], limit=8 * MIB
-    )(plan, arrived)
+    own_v_x = call(lambda *refs: assemble_kernel(0, *refs), [tile_planes], [VMEM, VMEM], limit=8 * MIB)(plan, arrived)[0]
     v_x = lax.ppermute(own_v_x, "space", pair_x)
     source = (source_cell, source_frac, wavelet)
     source_specs = [ANY] * 3
@@ -542,11 +547,10 @@
     ]
     receivers = (codes, receiver_count, owners, spread, place)
     receiver_specs = [SMEM, SMEM, VMEM, VMEM, VMEM]
-    coef, part, own_hi, base = call(
-        near_kernel, [eight, four, four, four], [VMEM] * 2 + source_specs + [VMEM] * 5,
+    own_v_in, coef, part, own_hi, base = call(
+        near_kernel, [tile_planes, eight, four, four, four], [VMEM] * 2 + source_specs + [VMEM] * 6,
         source_scratch, limit=16 * MIB,
-    )(weights, across, *source, u, sums, lead, own_v_x, own_v_in)
-    own_v_in, part = lax.optimization_barrier((own_v_in, part))
+    )(weights, across, *source, u, sums, lead, own_v_x, plan, arrived)
     v_in = lax.ppermute(own_v_in, "space", pair_in)
     prev, base, lead, total = call(
         cross_kernel, [eight, eight, four, four], [VMEM] * 2 + source_specs + [VMEM] * 6,
@@ -580,7 +584,8 @@
                 limit=20 * MIB, places=[ANY, VMEM],
             )(*receivers, *gaths, *common)
     back = lax.all_to_all(gath, "shot", split_axis=0, concat_axis=0, tiled=True)
-    return final, jnp.sum(back, axis=0)[None, None]
+    gathers = call(gather_kernel, [((1, 1, STEPS, 128), f32)], [VMEM], limit=4 * MIB)(back)[0]
+    return final, gathers
 
 
 def solution(mesh):

time: 99.3 us -> 101 us (1.017)
  starting transfers between devices: 32.1 us -> 36.2 us
  waiting for transfers between devices: 19.4 us -> 17 us
  Pallas kernels: 27.9 us -> 29.2 us
    ppermute x4, waiting for transfers between devices: 16.4 us -> 11.6 us  [swap(): lax.ppermute(across_chips, 'space', pair_x)]
    ppermute x4, starting transfers between devices: 21.1 us -> 24.4 us  [swap(): lax.ppermute(across_chips, 'space', pair_x)]
    ppermute x1, waiting for transfers between devices: 0.01 us -> 2.3 us  [on_device(): v_x = lax.ppermute(own_v_x, 'space', pair_x)]
    pallas_call x2 -> x3, Pallas kernels: 1.47 us -> 2.22 us  [the longest x1 1.33 us: on_device(): call(near_kernel, [tile_planes, eight, four, four, four], [VMEM] * 2 + so...]
where the time goes in v5:
time: 101 us
  starting transfers between devices  36.2 us (36%)
  Pallas kernels  29.2 us (29%)
  waiting for transfers between devices  17 us (17%)
  blocking collectives  10.9 us (11%)
  local copies, waits for them, and re-layouts  6.39 us (6%)
  between operations  1.69 us (2%)
    ppermute x4, starting transfers between devices, swap(): lax.ppermute(across_chips, 'space', pair_x)  24.4 us
    pallas_call x3, Pallas kernels, on_device(): call(lambda *refs, n=n: during_kernel(n, *refs), [four, four, four, four,...  12.1 us
    ppermute x4, waiting for transfers between devices, swap(): lax.ppermute(across_chips, 'space', pair_x)  11.6 us
    all_to_all x1, blocking collectives, on_device(): back = lax.all_to_all(gath, 'shot', split_axis=0, concat_axis=0, tiled=True)  10.9 us
    unnamed x40, local copies, waits for them, and re-layouts  6.39 us
    ppermute x1, starting transfers between devices, on_device(): v_x = lax.ppermute(own_v_x, 'space', pair_x)  6.11 us
    all_to_all x1, starting transfers between devices, on_device(): lax.all_to_all(out, 'shot', split_axis=0, concat_axis=0, tiled=True)  5.16 us
    pallas_call x2, Pallas kernels, on_device(): call(lambda *refs, n=n: middle_kernel(n, *refs), [eight, four, eight, sen...  3.17 us
  transfers between devices with their start and end apart: 12, of which 6 were waited for; matrix products, arithmetic and copies ran while one was open for 0% of the time, Pallas kernels for 19%

profile of v5, /device:TPU:16, one launch (start us, length us, event | category | flops | bytes accessed | tf_op | source)
XLA Modules:
  0.0 101.4 jit_solution(7899348780766177359)
XLA Ops:
  0.6 2.4 %shard_map.150 = bf16[8,8,64,128]{3,2,1,0:T(8,128)(2,1)} custom-call(s32[64]{0:T(128)} %home.1, s32[8,8]{1,0:T(8,128)} %wanted.1, bf16[8,8,64,64]{3,2,1,0:T(8,128)(2,1)} %store_hbm.1), custom_call_target="tpu_custom_call" | custom-call | tf_op jit(solution)/shard_map/pallas_call | solution.py:515
  3.1 0.0 copy-start.2
  3.1 0.0 copy-start.3
  3.1 5.2 %all-to-all-start = ((bf16[8,8,64,128]{3,2,1,0:T(8,128)(2,1)}), bf16[8,8,64,128]{3,2,1,0:T(8,128)(2,1)S(1)}, u32[]{:S(2)}, u32[]{:S(2)}) async-start(bf16[8,8,64,128]{3,2,1,0:T(8,128)(2,1)} %shard_map.150), calls=%async_computation | async-start | bytes 2097152 | tf_op jit(solution)/shard_map/all_to_all | solution.py:522
  8.3 0.0 copy-done.2
  8.3 0.0 copy-start
  8.3 0.0 copy-start.1
  8.3 0.1 collective-permute-start
  8.4 0.0 copy-done.3
  8.4 0.0 copy-start.15
  8.4 0.9 shard_map.151
  9.3 0.0 copy-start.16
  9.3 6.1 %collective-permute-start.2 = (bf16[12,128,256]{2,1,0:T(8,128)(2,1)}, bf16[12,128,256]{2,1,0:T(8,128)(2,1)}, u32[]{:S(2)}, u32[]{:S(2)}) collective-permute-start(bf16[12,128,256]{2,1,0:T(8,128)(2,1)} %get-tuple-element.65), channel_id=1, source_target_pairs={{1,2},{3,4},{5,6},{7,8},{9,10},{11,12},{13,14},{2,1},{4,3},{6,5},{... | collective-permute-start | bytes 2359304 | tf_op jit(solution)/shard_map/ppermute | solution.py:504
  15.4 0.1 collective-permute-start.1
  15.5 0.7 shard_map.153.refs_0_.plan
  16.2 0.8 collective-permute-done.1.pri_in
  17.0 0.0 collective-permute-done.cur_in
  17.1 1.2 %shard_map.152 = (f32[8,128,256]{2,1,0:T(8,128)S(1)}, f32[8,128,256]{2,1,0:T(8,128)S(1)}, f32[4,128,256]{2,1,0:T(8,128)S(1)}, f32[4,128,256]{2,1,0:T(8,128)S(1)}, f32[8,128,256]{2,1,0:T(8,128)S(1)}) custom-call(bf16[512,256]{1,0:T(8,128)(2,1)S(1)} %copy-done, bf16[128,256]{1,0:T(8,128)(2,1)S(1)} %copy-done.1, bf16[1,8,128,256]{3,2,1,0:T(8,128)(2,1)S(1)} %copy-done.2, ...), custom_call_target="tpu_custom_call" | custom-call | tf_op jit(solution)/shard_map/pallas_call | solution.py:537
  18.2 0.0 copy-start.4
  18.3 1.0 copy-done.4
  19.2 1.0 copy-done.6
  20.2 0.8 copy-done.8
  21.0 0.8 copy-done.10
  21.8 2.3 %all-to-all-done.refs_1_.arrived = bf16[8,8,64,128]{3,2,1,0:T(8,128)(2,1)S(1)} async-done(((bf16[8,8,64,128]{3,2,1,0:T(8,128)(2,1)}), bf16[8,8,64,128]{3,2,1,0:T(8,128)(2,1)S(1)}, u32[]{:S(2)}, u32[]{:S(2)}) %all-to-all-start) | async-done | bytes 1048608 | tf_op jit(solution)/shard_map/all_to_all | solution.py:522
  24.1 0.3 shard_map.154.own_v_x
  24.4 0.9 copy-done.5
  25.3 0.0 copy-done.12
  25.3 0.0 copy-done.14
  25.3 1.2 %copy-done.7 = f32[8,128,256]{2,1,0:T(8,128)S(1)} copy-done((f32[8,128,256]{2,1,0:T(8,128)S(1)}, f32[8,128,256]{2,1,0:T(8,128)}, u32[]{:S(2)}) %copy-start.7) | copy-done | bytes 1048600
  26.5 1.3 %shard_map.155 = (bf16[4,128,256]{2,1,0:T(8,128)(2,1)S(1)}, f32[8,128,256]{2,1,0:T(8,128)S(1)}, f32[4,128,256]{2,1,0:T(8,128)S(1)}, f32[4,128,256]{2,1,0:T(8,128)S(1)}, f32[4,128,256]{2,1,0:T(8,128)S(1)}) custom-call(bf16[512,256]{1,0:T(8,128)(2,1)S(1)} %copy-done, bf16[128,256]{1,0:T(8,128)(2,1)S(1)} %copy-done.1, s32[1,3]{1,0:T(1,128)S(1)} %copy-done.12, ...), custom_call_target="tpu_custom_call" | custom-call | tf_op jit(solution)/shard_map/pallas_call | solution.py:550
  27.8 0.1 collective-permute-start.4
  27.9 6.1 %collective-permute-start.3 = (bf16[4,128,256]{2,1,0:T(8,128)(2,1)S(1)}, bf16[4,128,256]{2,1,0:T(8,128)(2,1)S(1)}, u32[]{:S(2)}, u32[]{:S(2)}) collective-permute-start(bf16[4,128,256]{2,1,0:T(8,128)(2,1)S(1)} %shard_map.154.own_v_x), channel_id=1, source_target_pairs={{1,2},{3,4},{5,6},{7,8},{9,10},{11,12},{13,14},{2,1},{4,3},{6,5},{... | collective-permute-start | bytes 786440 | tf_op jit(solution)/shard_map/ppermute | solution.py:542
  34.1 0.0 collective-permute-done.2.got_x
  34.1 0.0 copy-start.9
  34.1 0.0 copy-start.11
  34.1 2.8 %shard_map.156 = (f32[8,128,256]{2,1,0:T(8,128)S(1)}, f32[8,128,256]{2,1,0:T(8,128)S(1)}, f32[4,128,256]{2,1,0:T(8,128)S(1)}, f32[4,128,256]{2,1,0:T(8,128)S(1)}) custom-call(bf16[512,256]{1,0:T(8,128)(2,1)S(1)} %copy-done, bf16[128,256]{1,0:T(8,128)(2,1)S(1)} %copy-done.1, s32[1,3]{1,0:T(1,128)S(1)} %copy-done.12, s32[1,3]{1,0:T(1,128)S(1)} %copy-done.13, ...), custom_call_target="tpu_custom_call" | custom-call | tf_op jit(solution)/shard_map/pallas_call | solution.py:555
  36.9 0.0 collective-permute-done.4.v_in
  36.9 2.3 %collective-permute-done.3.v_x = bf16[4,128,256]{2,1,0:T(8,128)(2,1)S(1)} collective-permute-done((bf16[4,128,256]{2,1,0:T(8,128)(2,1)S(1)}, bf16[4,128,256]{2,1,0:T(8,128)(2,1)S(1)}, u32[]{:S(2)}, u32[]{:S(2)}) %collective-permute-start.3) | collective-permute-done | bytes 262176 | tf_op jit(solution)/shard_map/ppermute | solution.py:542
  39.3 0.7 shard_map.157
  39.9 0.0 copy-start.18
  39.9 0.0 copy-start.19
  40.0 0.1 collective-permute-start.5
  40.1 6.1 %collective-permute-start.6 = (bf16[9,128,256]{2,1,0:T(8,128)(2,1)S(1)}, bf16[9,128,256]{2,1,0:T(8,128)(2,1)S(1)}, u32[]{:S(2)}, u32[]{:S(2)}) collective-permute-start(bf16[9,128,256]{2,1,0:T(8,128)(2,1)S(1)} %get-tuple-element.86), channel_id=1, source_target_pairs={{1,2},{3,4},{5,6},{7,8},{9,10},{11,12},{13,14},{2,1},{4,3},{6,5},{... | collective-permute-start | bytes 1769480 | tf_op jit(solution)/shard_map/ppermute | solution.py:504
  46.8 0.0 copy-start.17
  46.9 0.6 copy-done.17
  47.5 0.3 shard_map.149
  47.8 0.0 collective-permute-done.5.refs_15_
  47.8 3.8 %shard_map.158 = (f32[4,128,256]{2,1,0:T(8,128)S(1)}, f32[4,128,256]{2,1,0:T(8,128)S(1)}, f32[4,128,256]{2,1,0:T(8,128)S(1)}, f32[4,128,256]{2,1,0:T(8,128)S(1)}, f32[8,2,128]{2,1,0:T(2,128)S(1)}) custom-call(bf16[512,256]{1,0:T(8,128)(2,1)S(1)} %copy-done, bf16[128,256]{1,0:T(8,128)(2,1)S(1)} %copy-done.1, s32[1,3]{1,0:T(1,128)S(1)} %copy-done.12, ...), custom_call_target="tpu_custom_call" | custom-call | tf_op jit(solution)/shard_map/pallas_call | solution.py:565
  51.6 3.3 %collective-permute-done.6.refs_10_ = bf16[9,128,256]{2,1,0:T(8,128)(2,1)S(1)} collective-permute-done((bf16[9,128,256]{2,1,0:T(8,128)(2,1)S(1)}, bf16[9,128,256]{2,1,0:T(8,128)(2,1)S(1)}, u32[]{:S(2)}, u32[]{:S(2)}) %collective-permute-start.6) | collective-permute-done | bytes 589856 | tf_op jit(solution)/shard_map/ppermute | solution.py:504
  54.9 1.6 %shard_map.159 = (f32[8,128,256]{2,1,0:T(8,128)S(1)}, f32[4,128,256]{2,1,0:T(8,128)S(1)}, f32[8,128,256]{2,1,0:T(8,128)S(1)}, bf16[9,128,256]{2,1,0:T(8,128)(2,1)S(1)}) custom-call(bf16[512,256]{1,0:T(8,128)(2,1)S(1)} %copy-done, bf16[128,256]{1,0:T(8,128)(2,1)S(1)} %copy-done.1, s32[1,3]{1,0:T(1,128)S(1)} %copy-done.12, s32[1,3]{1,0:T(1,128)S(1)} %copy-done.13, ...), custom_call_target="tpu_custom_call" | custom-call | tf_op jit(solution)/shard_map/pallas_call | solution.py:573
  56.5 0.1 collective-permute-start.7
  56.5 6.1 %collective-permute-start.8 = (bf16[9,128,256]{2,1,0:T(8,128)(2,1)S(1)}, bf16[9,128,256]{2,1,0:T(8,128)(2,1)S(1)}, u32[]{:S(2)}, u32[]{:S(2)}) collective-permute-start(bf16[9,128,256]{2,1,0:T(8,128)(2,1)S(1)} %get-tuple-element.95), channel_id=1, source_target_pairs={{1,2},{3,4},{5,6},{7,8},{9,10},{11,12},{13,14},{2,1},{4,3},{6,5},{... | collective-permute-start | bytes 1769480 | tf_op jit(solution)/shard_map/ppermute | solution.py:504
  62.7 0.0 collective-permute-done.7.refs_15_
  62.7 4.0 %shard_map.160 = (f32[4,128,256]{2,1,0:T(8,128)S(1)}, f32[4,128,256]{2,1,0:T(8,128)S(1)}, f32[4,128,256]{2,1,0:T(8,128)S(1)}, f32[4,128,256]{2,1,0:T(8,128)S(1)}, f32[8,2,128]{2,1,0:T(2,128)S(1)}) custom-call(bf16[512,256]{1,0:T(8,128)(2,1)S(1)} %copy-done, bf16[128,256]{1,0:T(8,128)(2,1)S(1)} %copy-done.1, s32[1,3]{1,0:T(1,128)S(1)} %copy-done.12, ...), custom_call_target="tpu_custom_call" | custom-call | tf_op jit(solution)/shard_map/pallas_call | solution.py:565
  66.7 4.7 %collective-permute-done.8.refs_10_ = bf16[9,128,256]{2,1,0:T(8,128)(2,1)S(1)} collective-permute-done((bf16[9,128,256]{2,1,0:T(8,128)(2,1)S(1)}, bf16[9,128,256]{2,1,0:T(8,128)(2,1)S(1)}, u32[]{:S(2)}, u32[]{:S(2)}) %collective-permute-start.8) | collective-permute-done | bytes 589856 | tf_op jit(solution)/shard_map/ppermute | solution.py:504
  71.4 1.6 %shard_map.161 = (f32[8,128,256]{2,1,0:T(8,128)S(1)}, f32[4,128,256]{2,1,0:T(8,128)S(1)}, f32[8,128,256]{2,1,0:T(8,128)S(1)}, bf16[8,128,256]{2,1,0:T(8,128)(2,1)S(1)}) custom-call(bf16[512,256]{1,0:T(8,128)(2,1)S(1)} %copy-done, bf16[128,256]{1,0:T(8,128)(2,1)S(1)} %copy-done.1, s32[1,3]{1,0:T(1,128)S(1)} %copy-done.12, s32[1,3]{1,0:T(1,128)S(1)} %copy-done.13, ...), custom_call_target="tpu_custom_call" | custom-call | tf_op jit(solution)/shard_map/pallas_call | solution.py:573
  73.0 0.1 collective-permute-start.9
  73.1 6.1 %collective-permute-start.10 = (bf16[8,128,256]{2,1,0:T(8,128)(2,1)S(1)}, bf16[8,128,256]{2,1,0:T(8,128)(2,1)S(1)}, u32[]{:S(2)}, u32[]{:S(2)}) collective-permute-start(bf16[8,128,256]{2,1,0:T(8,128)(2,1)S(1)} %get-tuple-element.104), channel_id=1, source_target_pairs={{1,2},{3,4},{5,6},{7,8},{9,10},{11,12},{13,14},{2,1},{4,3},{6,5},{... | collective-permute-start | bytes 1572872 | tf_op jit(solution)/shard_map/ppermute | solution.py:504
  79.2 0.0 collective-permute-done.9.refs_15_
  79.2 4.3 %shard_map.162 = (f32[4,128,256]{2,1,0:T(8,128)S(1)}, f32[4,128,256]{2,1,0:T(8,128)S(1)}, f32[4,128,256]{2,1,0:T(8,128)}, f32[4,128,256]{2,1,0:T(8,128)S(1)}, f32[8,2,128]{2,1,0:T(2,128)S(1)}) custom-call(bf16[512,256]{1,0:T(8,128)(2,1)S(1)} %copy-done, bf16[128,256]{1,0:T(8,128)(2,1)S(1)} %copy-done.1, s32[1,3]{1,0:T(1,128)S(1)} %copy-done.12, ...), custom_call_target="tpu_custom_call" | custom-call | tf_op jit(solution)/shard_map/pallas_call | solution.py:565
  83.5 3.7 %collective-permute-done.10.refs_18_ = bf16[8,128,256]{2,1,0:T(8,128)(2,1)S(1)} collective-permute-done((bf16[8,128,256]{2,1,0:T(8,128)(2,1)S(1)}, bf16[8,128,256]{2,1,0:T(8,128)(2,1)S(1)}, u32[]{:S(2)}, u32[]{:S(2)}) %collective-permute-start.10) | collective-permute-done | bytes 524320 | tf_op jit(solution)/shard_map/ppermute | solution.py:504
  87.2 2.7 %shard_map.163 = (f32[1,8,128,256]{3,2,1,0:T(8,128)}, f32[8,8,128]{2,1,0:T(8,128)S(1)}) custom-call(s32[1,64]{1,0:T(1,128)S(1)} %get-tuple-element.56.refs_5_.refs_0_, s32[1,1]{1,0:T(1,128)S(6)} %copy.20.count.refs_6_.refs_1_, s32[64,1]{1,0:T(8,128)S(1)} %get-tuple-element.57.refs_7_.refs_2_, f32[64,256]{1,0:T(8,128)S(1)} %get-tuple-element.58.refs_8_.refs_3_, ...), custom_call_target="tpu_custom_call" | custom-call | tf_op jit(solution)/shard_map/pallas_call | solution.py:578
  89.9 10.9 %all_to_all.10.back = f32[8,8,128]{2,1,0:T(8,128)S(1)} all-to-all(f32[8,8,128]{2,1,0:T(8,128)S(1)} %get-tuple-element.109), channel_id=1, replica_groups=mesh['shot'=8,'space'=16] {'shot'}, dimensions={0} | all-to-all | bytes 65536 | tf_op jit(solution)/shard_map/all_to_all | solution.py:586
  100.8 0.6 shard_map.164
  (18 shorter events, 0.0 us)
Async XLA Ops:
  3.1 5.2 %copy-start.2 = (bf16[1,8,128,256]{3,2,1,0:T(8,128)(2,1)S(1)}, bf16[1,8,128,256]{3,2,1,0:T(8,128)(2,1)}, u32[]{:S(2)}) copy-start(bf16[1,8,128,256]{3,2,1,0:T(8,128)(2,1)} %cur.3) | copy-start | bytes 1572868
  3.1 5.3 %copy-start.3 = (bf16[1,8,128,256]{3,2,1,0:T(8,128)(2,1)S(1)}, bf16[1,8,128,256]{3,2,1,0:T(8,128)(2,1)}, u32[]{:S(2)}) copy-start(bf16[1,8,128,256]{3,2,1,0:T(8,128)(2,1)} %pri.3) | copy-start | bytes 1572868
  3.1 21.0 %all-to-all-start = ((bf16[8,8,64,128]{3,2,1,0:T(8,128)(2,1)}), bf16[8,8,64,128]{3,2,1,0:T(8,128)(2,1)S(1)}, u32[]{:S(2)}, u32[]{:S(2)}) async-start(bf16[8,8,64,128]{3,2,1,0:T(8,128)(2,1)} %shard_map.150), calls=%async_computation | async-start | bytes 2097152 | tf_op jit(solution)/shard_map/all_to_all | solution.py:522
  8.3 8.8 %copy-start = (bf16[512,256]{1,0:T(8,128)(2,1)S(1)}, bf16[512,256]{1,0:T(8,128)(2,1)}, u32[]{:S(2)}) copy-start(bf16[512,256]{1,0:T(8,128)(2,1)} %constant.4.clone.weights.refs_0_.refs_8_) | copy-start | bytes 786436
  8.3 8.8 %copy-start.1 = (bf16[128,256]{1,0:T(8,128)(2,1)S(1)}, bf16[128,256]{1,0:T(8,128)(2,1)}, u32[]{:S(2)}) copy-start(bf16[128,256]{1,0:T(8,128)(2,1)} %constant.5.clone.across.refs_1_.refs_9_) | copy-start | bytes 196612
  8.3 8.8 %collective-permute-start = (bf16[1,8,128,256]{3,2,1,0:T(8,128)(2,1)S(1)}, bf16[1,8,128,256]{3,2,1,0:T(8,128)(2,1)S(1)}, u32[]{:S(2)}, u32[]{:S(2)}) collective-permute-start(bf16[1,8,128,256]{3,2,1,0:T(8,128)(2,1)S(1)} %copy-done.2), channel_id=1, source_target_pairs={{0,1},{1,0},{2,3},{3,2},{4,5},{5,4},{6,7},{7,6},{8,9},{9,8},{10,11... | collective-permute-start | bytes 1572872 | tf_op jit(solution)/shard_map/ppermute | solution.py:528
  8.4 7.1 %copy-start.15 = (s32[8,8]{1,0:T(8,128)S(1)}, s32[8,8]{1,0:T(8,128)}, u32[]{:S(2)}) copy-start(s32[8,8]{1,0:T(8,128)} %wanted.1) | copy-start | bytes 772
  9.3 6.2 %copy-start.16 = (s32[64]{0:T(128)S(1)}, s32[64]{0:T(128)}, u32[]{:S(2)}) copy-start(s32[64]{0:T(128)} %home.1) | copy-start | bytes 772
  9.3 24.7 %collective-permute-start.2 = (bf16[12,128,256]{2,1,0:T(8,128)(2,1)}, bf16[12,128,256]{2,1,0:T(8,128)(2,1)}, u32[]{:S(2)}, u32[]{:S(2)}) collective-permute-start(bf16[12,128,256]{2,1,0:T(8,128)(2,1)} %get-tuple-element.65), channel_id=1, source_target_pairs={{1,2},{3,4},{5,6},{7,8},{9,10},{11,12},{13,14},{2,1},{4,3},{6,5},{... | collective-permute-start | bytes 2359304 | tf_op jit(solution)/shard_map/ppermute | solution.py:504
  15.4 1.6 %collective-permute-start.1 = (bf16[4,128,256]{2,1,0:T(8,128)(2,1)S(1)}, bf16[4,128,256]{2,1,0:T(8,128)(2,1)S(1)}, u32[]{:S(2)}, u32[]{:S(2)}) collective-permute-start(bf16[4,128,256]{2,1,0:T(8,128)(2,1)S(1)} %get-tuple-element.60), channel_id=1, source_target_pairs={{0,1},{1,0},{2,3},{3,2},{4,5},{5,4},{6,7},{7,6},{8,9},{9,8},{10,11... | collective-permute-start | bytes 786440 | tf_op jit(solution)/shard_map/ppermute | solution.py:504
  18.2 1.0 copy-start.4
  19.2 1.0 copy-start.6
  20.2 0.8 copy-start.8
  21.0 0.8 copy-start.10
  24.1 1.2 %copy-start.5 = (f32[8,128,256]{2,1,0:T(8,128)S(1)}, f32[8,128,256]{2,1,0:T(8,128)}, u32[]{:S(2)}) copy-start(f32[8,128,256]{2,1,0:T(8,128)} %copy-done.4) | copy-start | bytes 3145732
  24.1 1.2 %copy-start.12 = (s32[1,3]{1,0:T(1,128)S(1)}, s32[1,3]{1,0:T(1,128)}, u32[]{:S(2)}) copy-start(s32[1,3]{1,0:T(1,128)} %refs_10_.1) | copy-start | bytes 40
  24.1 1.2 %copy-start.13 = (s32[1,3]{1,0:T(1,128)S(1)}, s32[1,3]{1,0:T(1,128)}, u32[]{:S(2)}) copy-start(s32[1,3]{1,0:T(1,128)} %refs_11_.1) | copy-start | bytes 40
  24.1 1.2 %copy-start.14 = (f32[1,8]{1,0:T(1,128)S(1)}, f32[1,8]{1,0:T(1,128)}, u32[]{:S(2)}) copy-start(f32[1,8]{1,0:T(1,128)} %refs_12_.1) | copy-start | bytes 100
  25.3 1.2 %copy-start.7 = (f32[8,128,256]{2,1,0:T(8,128)S(1)}, f32[8,128,256]{2,1,0:T(8,128)}, u32[]{:S(2)}) copy-start(f32[8,128,256]{2,1,0:T(8,128)} %copy-done.6) | copy-start | bytes 3145732
  27.8 9.1 %collective-permute-start.4 = (bf16[4,128,256]{2,1,0:T(8,128)(2,1)S(1)}, bf16[4,128,256]{2,1,0:T(8,128)(2,1)S(1)}, u32[]{:S(2)}, u32[]{:S(2)}) collective-permute-start(bf16[4,128,256]{2,1,0:T(8,128)(2,1)S(1)} %get-tuple-element.77), channel_id=1, source_target_pairs={{0,1},{1,0},{2,3},{3,2},{4,5},{5,4},{6,7},{7,6},{8,9},{9,8},{10,11... | collective-permute-start | bytes 786440 | tf_op jit(solution)/shard_map/ppermute | solution.py:554
  27.9 11.3 %collective-permute-start.3 = (bf16[4,128,256]{2,1,0:T(8,128)(2,1)S(1)}, bf16[4,128,256]{2,1,0:T(8,128)(2,1)S(1)}, u32[]{:S(2)}, u32[]{:S(2)}) collective-permute-start(bf16[4,128,256]{2,1,0:T(8,128)(2,1)S(1)} %shard_map.154.own_v_x), channel_id=1, source_target_pairs={{1,2},{3,4},{5,6},{7,8},{9,10},{11,12},{13,14},{2,1},{4,3},{6,5},{... | collective-permute-start | bytes 786440 | tf_op jit(solution)/shard_map/ppermute | solution.py:542
  34.1 5.2 %copy-start.9 = (f32[4,128,256]{2,1,0:T(8,128)S(1)}, f32[4,128,256]{2,1,0:T(8,128)}, u32[]{:S(2)}) copy-start(f32[4,128,256]{2,1,0:T(8,128)} %copy-done.8) | copy-start | bytes 1572868
  34.1 5.2 %copy-start.11 = (f32[4,128,256]{2,1,0:T(8,128)S(1)}, f32[4,128,256]{2,1,0:T(8,128)}, u32[]{:S(2)}) copy-start(f32[4,128,256]{2,1,0:T(8,128)} %copy-done.10) | copy-start | bytes 1572868
  39.9 6.9 %copy-start.18 = (s32[1,1,64,3]{2,1,3,0:T(1,128)S(1)}, s32[1,1,64,3]{2,1,3,0:T(1,128)}, u32[]{:S(2)}) copy-start(s32[1,1,64,3]{2,1,3,0:T(1,128)} %param.23) | copy-start | bytes 2308
  39.9 6.9 %copy-start.19 = (s32[1,1,64,3]{2,1,3,0:T(1,128)S(1)}, s32[1,1,64,3]{2,1,3,0:T(1,128)}, u32[]{:S(2)}) copy-start(s32[1,1,64,3]{2,1,3,0:T(1,128)} %param.22) | copy-start | bytes 2308
  40.0 7.9 %collective-permute-start.5 = (f32[8,128,256]{2,1,0:T(8,128)S(1)}, f32[8,128,256]{2,1,0:T(8,128)S(1)}, u32[]{:S(2)}, u32[]{:S(2)}) collective-permute-start(f32[8,128,256]{2,1,0:T(8,128)S(1)} %get-tuple-element.79.refs_10_.refs_5_), channel_id=1, source_target_pairs={{0,1},{1,0},{2,3},{3,2},{4,5},{5,4},{6,7},{7,6},{8,9},{9,8},{10,11... | collective-permute-start | bytes 3145736 | tf_op jit(solution)/shard_map/ppermute | solution.py:504
  40.1 14.8 %collective-permute-start.6 = (bf16[9,128,256]{2,1,0:T(8,128)(2,1)S(1)}, bf16[9,128,256]{2,1,0:T(8,128)(2,1)S(1)}, u32[]{:S(2)}, u32[]{:S(2)}) collective-permute-start(bf16[9,128,256]{2,1,0:T(8,128)(2,1)S(1)} %get-tuple-element.86), channel_id=1, source_target_pairs={{1,2},{3,4},{5,6},{7,8},{9,10},{11,12},{13,14},{2,1},{4,3},{6,5},{... | collective-permute-start | bytes 1769480 | tf_op jit(solution)/shard_map/ppermute | solution.py:504
  46.8 0.7 copy-start.17
  56.5 6.2 %collective-permute-start.7 = (f32[8,128,256]{2,1,0:T(8,128)S(1)}, f32[8,128,256]{2,1,0:T(8,128)S(1)}, u32[]{:S(2)}, u32[]{:S(2)}) collective-permute-start(f32[8,128,256]{2,1,0:T(8,128)S(1)} %get-tuple-element.90.refs_10_.refs_5_), channel_id=1, source_target_pairs={{0,1},{1,0},{2,3},{3,2},{4,5},{5,4},{6,7},{7,6},{8,9},{9,8},{10,11... | collective-permute-start | bytes 3145736 | tf_op jit(solution)/shard_map/ppermute | solution.py:504
  56.5 14.8 %collective-permute-start.8 = (bf16[9,128,256]{2,1,0:T(8,128)(2,1)S(1)}, bf16[9,128,256]{2,1,0:T(8,128)(2,1)S(1)}, u32[]{:S(2)}, u32[]{:S(2)}) collective-permute-start(bf16[9,128,256]{2,1,0:T(8,128)(2,1)S(1)} %get-tuple-element.95), channel_id=1, source_target_pairs={{1,2},{3,4},{5,6},{7,8},{9,10},{11,12},{13,14},{2,1},{4,3},{6,5},{... | collective-permute-start | bytes 1769480 | tf_op jit(solution)/shard_map/ppermute | solution.py:504
  73.0 6.2 %collective-permute-start.9 = (f32[8,128,256]{2,1,0:T(8,128)S(1)}, f32[8,128,256]{2,1,0:T(8,128)S(1)}, u32[]{:S(2)}, u32[]{:S(2)}) collective-permute-start(f32[8,128,256]{2,1,0:T(8,128)S(1)} %get-tuple-element.99.refs_10_.refs_13_), channel_id=1, source_target_pairs={{0,1},{1,0},{2,3},{3,2},{4,5},{5,4},{6,7},{7,6},{8,9},{9,8},{10,11... | collective-permute-start | bytes 3145736 | tf_op jit(solution)/shard_map/ppermute | solution.py:504
  73.1 14.1 %collective-permute-start.10 = (bf16[8,128,256]{2,1,0:T(8,128)(2,1)S(1)}, bf16[8,128,256]{2,1,0:T(8,128)(2,1)S(1)}, u32[]{:S(2)}, u32[]{:S(2)}) collective-permute-start(bf16[8,128,256]{2,1,0:T(8,128)(2,1)S(1)} %get-tuple-element.104), channel_id=1, source_target_pairs={{1,2},{3,4},{5,6},{7,8},{9,10},{11,12},{13,14},{2,1},{4,3},{6,5},{... | collective-permute-start | bytes 1572872 | tf_op jit(solution)/shard_map/ppermute | solution.py:504
